TPU v7x, 32 devices: a whole 2x2x4 slice. The times are simulated.
32 devices in a mesh: dense: 16 (over z, x, core), attn: 2 (over y).
Axes of the slice: x: 2, y: 2, z: 4, core: 2. Of those that a mesh axis runs over, the one named last changes fastest.
Arguments:
- queries: bfloat16 [4096, 4096], P('dense', 'attn'), may hold values from -30 to 30
- keys: bfloat16 [4096, 1024], P('dense', 'attn'), may hold values from -13 to 13
- values: bfloat16 [4096, 1024], P('dense', 'attn'), may hold values from -24 to 24
- segments: int32 [4096], replicated, may hold values from 0 to 5, never falling along the last dimension, each value on 1 to 2048 neighbouring positions
- out_weight: bfloat16 [4096, 4096], P('attn', 'dense'), may hold values from -0.09375 to 0.09375
Outputs:
- projected: bfloat16 [4096, 4096], P('dense', 'attn')
All inputs are finite; a program needn't handle non-finite values.
Results may differ from a plain program's by a relative error of at most 0.012.
Values may be sent and summed in bfloat16 or wider, within the bound.
No kernel may reach another device: no remote copies, remote signals or barrier semaphores. Data moves between devices by JAX's collectives and lax.ppermute only.
A program may use at most 128 MiB of HBM per device.

v0:
```python
import math

import jax
import jax.numpy as jnp
from jax import lax
from jax.sharding import PartitionSpec as P

HEAD_WIDTH = 128


NEGATIVE = -1e30


def attend(query_rows, positions, query_docs, keys, values, segments):
    token_count = query_rows.shape[0]
    kv_local = keys.shape[1] // HEAD_WIDTH
    head_group = query_rows.shape[1] // HEAD_WIDTH // kv_local
    blocks_count = max(token_count // 128, 1)
    block_rows = token_count // blocks_count
    inv_root = 1.0 / math.sqrt(HEAD_WIDTH)
    query_heads = query_rows.reshape(token_count, kv_local, head_group, HEAD_WIDTH)
    initial = tuple(
        (
            (
                jnp.full((kv_local, head_group, block_rows), NEGATIVE, jnp.float32),
                jnp.zeros((kv_local, head_group, block_rows), jnp.float32),
                jnp.zeros((kv_local, head_group, block_rows, HEAD_WIDTH), jnp.float32),
            )
            for which_block in range(blocks_count)
        )
    )
    key_piece = lax.all_gather(keys, "dense", axis=0, tiled=True)
    value_piece = lax.all_gather(values, "dense", axis=0, tiled=True)
    key_count = key_piece.shape[0]
    key_positions = jnp.arange(key_count, dtype=jnp.int32)
    key_heads = key_piece.reshape(key_count, kv_local, HEAD_WIDTH)
    value_heads = value_piece.reshape(key_count, kv_local, HEAD_WIDTH)
    updated = []
    for which_block in range(blocks_count):
        lower = which_block * block_rows
        upper = lower + block_rows
        visible = (query_docs[lower:upper, None] == segments[None, :]) & (
            key_positions[None, :] <= positions[lower:upper, None]
        )
        sliced = query_heads[lower:upper]

        def compute(state):
            row_max, totals, summed = state
            scores = (
                jnp.einsum("qgjd,kgd->gjqk", sliced, key_heads, preferred_element_type=jnp.float32)
                * inv_root
            )
            scores = jnp.where(visible, scores, NEGATIVE)
            new_max = jnp.maximum(row_max, jnp.max(scores, axis=-1))
            weights = jnp.where(visible, jnp.exp(scores - new_max[..., None]), 0.0)
            totals = jnp.sum(weights, axis=-1)
            summed = jnp.einsum(
                "gjqk,kgd->gjqd",
                weights.astype(jnp.bfloat16),
                value_heads,
                preferred_element_type=jnp.float32,
            )
            return (new_max, totals, summed)

        updated.append(
            lax.cond(jnp.any(visible), compute, lambda state: state, initial[which_block])
        )
    final = tuple(updated)
    outputs = []
    for state in final:
        outputs.append(state[2] / state[1][..., None])
    attended = jnp.concatenate(outputs, axis=2).astype(jnp.bfloat16)
    return attended.transpose(2, 0, 1, 3).reshape(token_count, kv_local * head_group * HEAD_WIDTH)


def project(attended, out_weight):
    partial_sums = jnp.dot(
        attended,
        lax.all_gather(out_weight, "dense", axis=1, tiled=True),
        preferred_element_type=jnp.float32,
    )
    return lax.psum_scatter(
        partial_sums.astype(jnp.bfloat16), "attn", scatter_dimension=1, tiled=True
    )


def shards(queries, keys, values, segments, out_weight):
    device_index = lax.axis_index("dense")
    token_count = queries.shape[0]
    positions = device_index * token_count + jnp.arange(token_count, dtype=jnp.int32)
    query_docs = lax.dynamic_slice_in_dim(segments, device_index * token_count, token_count)
    attended = attend(queries, positions, query_docs, keys, values, segments)
    projected = project(attended, out_weight)
    return projected


def solution(mesh):
    return jax.shard_map(
        shards,
        mesh=mesh,
        in_specs=(
            P("dense", "attn"),
            P("dense", "attn"),
            P("dense", "attn"),
            P(),
            P("attn", "dense"),
        ),
        out_specs=P("dense", "attn"),
        check_vma=False,
    )
```

profile of v0, /device:TPU:25, one launch (start us, length us, event | category | flops | bytes accessed | tf_op | source)
XLA Modules:
  0.0 296.3 jit_solution(2333828071562027797)
XLA Ops:
  6.5 0.0 all-gather.4.cloned.1.call-start
  6.5 1.8 copy.12
  8.3 0.0 all-gather.4.cloned.1.call-update
  8.4 0.0 all-gather.6.cloned.1.call-start
  8.4 1.8 copy.13
  10.2 0.0 all-gather.6.cloned.1.call-update
  10.2 0.0 all-gather.8.cloned.1.call-start
  10.3 0.7 all-gather.8.cloned.1.call-update
  10.9 0.0 reduce-scatter.2.cloned.1.call-start
  11.0 0.8 dynamic_slice.3
  11.8 3.0 %fusion.27 = (pred[]{:T(512)}, pred[]{:T(512)}, pred[128,4096]{0,1:T(8,128)(4,1)S(1)}, pred[128,4096]{0,1:T(8,128)(4,1)S(1)}) fusion(s32[128]{0:T(128)S(1)} %get-tuple-element.63, s32[4096]{0:T(1024)} %param.12, s32[128]{0:T(128)S(1)} %get-tuple-element.60, s32[128]{0:T(128)S(1)} %get-tuple-element.64, s32[128]{0:T(128)S(1)} %get-tuple-element.59), kind=kLoop, calls=%fused_computation.38 | loop fusion | flops 4194302 | bytes 1067010 | tf_op jit(solution)/shard_map/reduce_or | solution.py:66
  16.1 46.2 %all-gather.4.cloned.1.call-done = bf16[4096,512]{0,1:T(8,128)(2,1)} async-done(((bf16[256,512]{0,1:T(8,128)(2,1)}), bf16[4096,512]{0,1:T(8,128)(2,1)}) %all-gather.4.cloned.1.call-update) | async-done | bytes 4194320 | tf_op jit(solution)/shard_map/all_gather | solution.py:32
  62.3 53.6 %all-gather.6.cloned.1.call-done = bf16[4096,512]{0,1:T(8,128)(2,1)} async-done(((bf16[256,512]{0,1:T(8,128)(2,1)}), bf16[4096,512]{0,1:T(8,128)(2,1)}) %all-gather.6.cloned.1.call-update) | async-done | bytes 4194320 | tf_op jit(solution)/shard_map/all_gather | solution.py:33
  115.8 49.1 %conditional.2 = (f32[4,4,128]{2,1,0:T(4,128)S(1)}, f32[4,4,128,128]{2,3,1,0:T(8,128)S(1)}) conditional(s32[]{:T(128)} %convert_element_type.16, () %tuple.21, (pred[128,4096]{0,1:T(8,128)(4,1)S(1)}, bf16[256,2048]{1,0:T(8,128)(2,1)}, bf16[4096,4,128]{0,2,1:T(8,128)(2,1)}, bf16[4096,4,128]{0,2,1:T(8,128)(2,1)}) %tuple.54), branch_computations={%region_1.0_spmd, %region_2.5_spmd} | conditional | flops 4404017152 | bytes 115392528 | solution.py:66
  115.8 1.5 copy.14
  117.4 16.9 %fusion = (f32[4,4,128]{2,1,0:T(4,128)S(1)}, f32[4,4096,128,4]{2,1,3,0:T(8,128)}) fusion(pred[128,4096]{0,1:T(8,128)(4,1)S(1)} %get-tuple-element.25, bf16[128,4,4,128]{0,3,2,1:T(8,128)(2,1)S(1)} %bitcast.60, bf16[4096,4,128]{0,2,1:T(8,128)(2,1)} %get-tuple-element.43), kind=kOutput, calls=%fused_computation.2 | convolution fusion | flops 2172647424 | bytes 38805504 | tf_op jit(solution)/shard_map/cond/branch_1_fun/qgjd,kgd->gjqk/dot_general | solution.py:50
  134.3 15.9 %fusion.3 = f32[4,4,128,128]{2,3,1,0:T(8,128)S(1)} fusion(f32[4,4096,128,4]{2,1,3,0:T(8,128)} %get-tuple-element.54, f32[4,4,128]{2,1,0:T(4,128)S(1)} %broadcast_maximum_fusion, pred[128,4096]{0,1:T(8,128)(4,1)S(1)} %get-tuple-element.25, bf16[4096,4,128]{0,2,1:T(8,128)(2,1)} %get-tuple-element.44), kind=kOutput, calls=%fused_computation.5 | convolution fusion | flops 2189426688 | bytes 39329792 | tf_op jit(solution)/shard_map/cond | solution.py:66
  150.2 14.7 %fusion.2 = f32[4,4,128]{2,1,0:T(4,128)S(1)} fusion(f32[4,4096,128,4]{2,1,3,0:T(8,128)} %get-tuple-element.54, f32[4,4,128]{2,1,0:T(4,128)S(1)} %broadcast_maximum_fusion, pred[128,4096]{0,1:T(8,128)(4,1)S(1)} %get-tuple-element.25), kind=kLoop, calls=%fused_computation.4 | loop fusion | flops 41940992 | bytes 34095104 | tf_op jit(solution)/shard_map/cond/branch_1_fun/reduce_sum | solution.py:56
  165.0 49.3 %conditional.3 = (f32[4,4,128]{2,1,0:T(4,128)S(1)}, f32[4,4,128,128]{2,3,1,0:T(8,128)S(1)}) conditional(s32[]{:T(128)} %convert_element_type.17, () %tuple.23, (pred[128,4096]{0,1:T(8,128)(4,1)S(1)}, bf16[256,2048]{1,0:T(8,128)(2,1)}, bf16[4096,4,128]{0,2,1:T(8,128)(2,1)}, bf16[4096,4,128]{0,2,1:T(8,128)(2,1)}) %tuple.55), branch_computations={%region_6.7_spmd, %region_7.10_spmd} | conditional | flops 4404017152 | bytes 115392528 | solution.py:66
  165.2 1.5 copy.18
  166.7 16.8 %fusion.12 = (f32[4,4,128]{2,1,0:T(4,128)S(1)}, f32[4,4096,128,4]{2,1,3,0:T(8,128)}) fusion(pred[128,4096]{0,1:T(8,128)(4,1)S(1)} %get-tuple-element.29, bf16[128,4,4,128]{0,3,2,1:T(8,128)(2,1)S(1)} %bitcast.61, bf16[4096,4,128]{0,2,1:T(8,128)(2,1)} %get-tuple-element.47), kind=kOutput, calls=%fused_computation.16 | convolution fusion | flops 2172647424 | bytes 38805504 | tf_op jit(solution)/shard_map/cond/branch_1_fun/qgjd,kgd->gjqk/dot_general | solution.py:50
  183.5 16.1 %fusion.15 = f32[4,4,128,128]{2,3,1,0:T(8,128)S(1)} fusion(f32[4,4096,128,4]{2,1,3,0:T(8,128)} %get-tuple-element.56, f32[4,4,128]{2,1,0:T(4,128)S(1)} %broadcast_maximum_fusion.1, pred[128,4096]{0,1:T(8,128)(4,1)S(1)} %get-tuple-element.29, bf16[4096,4,128]{0,2,1:T(8,128)(2,1)} %get-tuple-element.48), kind=kOutput, calls=%fused_computation.19 | convolution fusion | flops 2189426688 | bytes 39329792 | tf_op jit(solution)/shard_map/cond | solution.py:66
  199.6 14.7 %fusion.14 = f32[4,4,128]{2,1,0:T(4,128)S(1)} fusion(f32[4,4096,128,4]{2,1,3,0:T(8,128)} %get-tuple-element.56, f32[4,4,128]{2,1,0:T(4,128)S(1)} %broadcast_maximum_fusion.1, pred[128,4096]{0,1:T(8,128)(4,1)S(1)} %get-tuple-element.29), kind=kLoop, calls=%fused_computation.18 | loop fusion | flops 41940992 | bytes 34095104 | tf_op jit(solution)/shard_map/cond/branch_1_fun/reduce_sum | solution.py:56
  214.3 0.1 divide_convert_fusion.1
  214.4 0.1 divide_convert_fusion
  214.6 0.1 pad_maximum_fusion
  214.7 31.9 %all-gather.8.cloned.1.call-done = bf16[2048,4096]{1,0:T(8,128)(2,1)} async-done(((bf16[2048,256]{1,0:T(8,128)(2,1)}), bf16[2048,4096]{1,0:T(8,128)(2,1)}) %all-gather.8.cloned.1.call-update) | async-done | bytes 16777232 | tf_op jit(solution)/shard_map/all_gather | solution.py:79
  246.6 11.6 %convolution_convert_fusion = bf16[256,4096]{1,0:T(8,128)(2,1)} fusion(bf16[256,2048]{0,1:T(8,128)(2,1)S(1)} %bitcast.59, bf16[2048,4096]{1,0:T(8,128)(2,1)} %all-gather.8.cloned.1.call-done), kind=kOutput, calls=%fused_computation.28 | convolution fusion | flops 4296015872 | bytes 19922944 | tf_op jit(solution)/shard_map/dot_general | solution.py:77
  258.1 0.0 reduce-scatter.2.cloned.1.call-update
  258.1 31.6 %reduce-scatter.2.cloned.1.call-done = bf16[256,2048]{1,0:T(8,128)(2,1)} async-done(((bf16[256,4096]{1,0:T(8,128)(2,1)}), bf16[256,2048]{1,0:T(8,128)(2,1)}) %reduce-scatter.2.cloned.1.call-update) | async-done | bytes 1048592 | tf_op jit(solution)/shard_map/reduce_scatter | solution.py:82
  (6 shorter events, 0.1 us)
Async XLA Ops:
  6.5 55.7 %all-gather.4.cloned.1.call-start = ((), (), s32[]{:S(2)}) async-start(), calls=%async_computation.1 | async-start | bytes 4456448 | tf_op jit(solution)/shard_map/all_gather | solution.py:32
  8.4 107.5 %all-gather.6.cloned.1.call-start = ((), (), s32[]{:S(2)}) async-start(), calls=%async_computation.2 | async-start | bytes 4456448 | tf_op jit(solution)/shard_map/all_gather | solution.py:33
  10.2 236.4 %all-gather.8.cloned.1.call-start = ((), (), s32[]{:S(2)}) async-start(), calls=%async_computation.3 | async-start | bytes 17825792 | tf_op jit(solution)/shard_map/all_gather | solution.py:79
  10.9 278.8 %reduce-scatter.2.cloned.1.call-start = ((), (), s32[]{:S(2)}) async-start(), calls=%async_computation.4 | async-start | bytes 3145728 | tf_op jit(solution)/shard_map/reduce_scatter | solution.py:82
Sparse Core Ops, SparseCore 0:
  9.5 52.7 all-gather.3
  64.4 51.3 all-gather.5
  118.0 128.5 all-gather.7
  258.3 31.4 reduce-scatter.1
where the time goes:
time: 299 us; the launch traced here: 296 us
  waiting for transfers between devices  164 us (55%)
  matrix products  77.3 us (26%)
  other arithmetic  32.8 us (11%)
  between operations  14.5 us (5%)
  local copies, waits for them, and re-layouts  7.37 us (2%)
    all_gather x1, waiting for transfers between devices, attend(): value_piece = lax.all_gather(values, 'dense', axis=0, tiled=True)  53.6 us
    all_gather x1, waiting for transfers between devices, attend(): key_piece = lax.all_gather(keys, 'dense', axis=0, tiled=True)  46.2 us
    dot_general x2, matrix products, compute(): jnp.einsum('qgjd,kgd->gjqk', sliced, key_heads, preferred_element_type=jn...  33.7 us
    cond x2, matrix products, attend(): lax.cond(jnp.any(visible), compute, lambda state: state, initial[which_bl...  32 us
    all_gather x1, waiting for transfers between devices, project(): lax.all_gather(out_weight, 'dense', axis=1, tiled=True)  31.9 us
    reduce_scatter x1, waiting for transfers between devices, project(): lax.psum_scatter(partial_sums.astype(jnp.bfloat16), 'attn', scatter_dimen...  31.6 us
    reduce_sum x2, other arithmetic, compute(): totals = jnp.sum(weights, axis=-1)  29.4 us
    dot_general x1, matrix products, project(): jnp.dot(attended, lax.all_gather(out_weight, 'dense', axis=1, tiled=True)...  11.6 us
  transfers between devices with their start and end apart: 4, of which 4 were waited for; matrix products, arithmetic and copies ran while one was open for 35% of the time, Pallas kernels for 0%

commit v1 on v0

v1 whole, which is shorter than its diff:
```python
import functools
import math

import jax
import jax.numpy as jnp
import numpy as np
from jax import lax
from jax.experimental import pallas as pl
from jax.experimental.pallas import tpu as pltpu
from jax.sharding import PartitionSpec as P

HEAD = 128
NEGATIVE = -1e30
AXES = ("dense", "attn")
ANY = pl.BlockSpec(memory_space=pl.ANY)
SMEM = pl.BlockSpec(memory_space=pltpu.SMEM)
VMEM = pl.BlockSpec(memory_space=pltpu.VMEM)


def xor(a, b):
    return lax.bitwise_xor(a, jnp.int32(b))


def params(mib):
    return pltpu.CompilerParams(vmem_limit_bytes=mib * 2**20)


def split_kv_kernel(group, meta_ref, k_ref, v_ref, *outs):
    g = lax.rem(meta_ref[0], group)
    for k in range(group):
        at = pl.ds(pl.multiple_of(xor(g, k) * HEAD, HEAD), HEAD)
        outs[k][:, :HEAD] = k_ref[:, at]
        outs[k][:, HEAD:] = v_ref[:, at]


def split_q_kernel(group, meta_ref, q_ref, *outs):
    g = lax.rem(meta_ref[0], group)
    width = outs[0].shape[1]
    for k in range(group):
        outs[k][...] = q_ref[:, pl.ds(pl.multiple_of(xor(g, k) * width, width), width)]


def attention_kernel(group, hops, heads, meta_ref, seg_ref, segrow_ref, *refs):
    n_kv = (hops + 1) * group
    q_refs, kv_refs = refs[:group], refs[group : group + n_kv]
    out_refs = refs[group + n_kv : group + n_kv + 2]
    q_s, k_s, v_s, s_s, m_s, l_s, acc_s, seg_s, sem = refs[group + n_kv + 2 :]
    n = q_s.shape[2]
    copies = []
    for k in range(group):
        for h in range(heads):
            copies.append((q_refs[k].at[:, pl.ds(h * HEAD, HEAD)], q_s.at[k, h]))
    for i in range(n_kv):
        copies.append((kv_refs[i].at[:, pl.ds(0, HEAD)], k_s.at[i]))
        copies.append((kv_refs[i].at[:, pl.ds(HEAD, HEAD)], v_s.at[i]))
    copies = [pltpu.make_async_copy(a, b, sem.at[i]) for i, (a, b) in enumerate(copies)]
    for c in copies:
        c.start()
    for c in copies:
        c.wait()

    device = meta_ref[0]
    plane, g = device // group, lax.rem(device, group)
    scale = math.log2(math.e) / math.sqrt(HEAD)
    lanes = n // HEAD

    def piece(i):
        return (plane - i // group) * group + lax.bitwise_xor(g, lax.rem(i, group))

    def one_query_piece(k, carry):
        qp = plane * group + lax.bitwise_xor(g, k)
        q_first, q_last = seg_ref[qp * n], seg_ref[qp * n + n - 1]
        row = segrow_ref[pl.ds(qp, 1), :].astype(jnp.float32)
        seg_s[...] = jnp.broadcast_to(row, (HEAD, n)).T
        m_s[...] = jnp.full(m_s.shape, NEGATIVE, jnp.float32)
        l_s[...] = jnp.zeros(l_s.shape, jnp.float32)
        acc_s[...] = jnp.zeros(acc_s.shape, jnp.float32)

        def state(i):
            kp = piece(i)
            safe = jnp.maximum(kp, 0)
            active = (kp >= 0) & (kp <= qp) & (seg_ref[safe * n + n - 1] >= q_first)
            whole = (kp < qp) & (seg_ref[safe * n] == q_last)
            return kp, safe, active, whole

        def score(i, carry):
            kp, safe, active, whole = state(i)

            def scores(h):
                return lax.dot_general(
                    q_s[k, h], k_s[i], (((1,), (1,)), ((), ())), preferred_element_type=jnp.float32
                )

            def keep(h, parts):
                best = m_s[h]
                for t, part in enumerate(parts):
                    s_s[i, h, :, t * HEAD : (t + 1) * HEAD] = part
                    best = jnp.maximum(best, part)
                m_s[h] = best

            @pl.when(active & whole)
            def _():
                for h in range(heads):
                    s = scores(h)
                    keep(h, [s[:, t * HEAD : (t + 1) * HEAD] for t in range(lanes)])

            @pl.when(active & jnp.logical_not(whole))
            def _():
                seg_k = segrow_ref[pl.ds(safe, 1), :].astype(jnp.float32)
                ahead = lax.broadcasted_iota(jnp.int32, (n, HEAD), 1) - lax.broadcasted_iota(
                    jnp.int32, (n, HEAD), 0
                )
                seen = [
                    (ahead + t * HEAD <= (qp - kp) * n)
                    & (seg_s[...] == seg_k[:, t * HEAD : (t + 1) * HEAD])
                    for t in range(lanes)
                ]
                for h in range(heads):
                    s = scores(h)
                    keep(
                        h,
                        [
                            jnp.where(seen[t], s[:, t * HEAD : (t + 1) * HEAD], NEGATIVE)
                            for t in range(lanes)
                        ],
                    )

            return carry

        lax.fori_loop(0, n_kv, score, 0)
        for h in range(heads):
            m_s[h] = jnp.broadcast_to(jnp.max(m_s[h], axis=1, keepdims=True), (n, HEAD))

        def mix(i, carry):
            active = state(i)[2]

            @pl.when(active)
            def _():
                for h in range(heads):
                    top = m_s[h]
                    parts = [
                        jnp.exp2((s_s[i, h, :, t * HEAD : (t + 1) * HEAD] - top) * scale)
                        for t in range(lanes)
                    ]
                    l_s[h] += functools.reduce(jnp.add, parts)
                    weights = jnp.concatenate([p.astype(jnp.bfloat16) for p in parts], axis=1)
                    acc_s[h] += jnp.dot(weights, v_s[i], preferred_element_type=jnp.float32)

            return carry

        lax.fori_loop(0, n_kv, mix, 0)
        half = heads // 2
        for h in range(heads):
            total = jnp.sum(l_s[h], axis=1, keepdims=True)
            out_refs[h // half][k, :, (h % half) * HEAD : (h % half + 1) * HEAD] = (
                acc_s[h] / total
            ).astype(jnp.bfloat16)
        return carry

    lax.fori_loop(0, group, one_query_piece, 0)


def project_kernel(group, attn, cands, sel_at, meta_ref, *refs):
    n_w = len(cands) * attn
    w_refs = [refs[c * attn : (c + 1) * attn] for c in range(len(cands))]
    a_refs = refs[n_w : n_w + 2 * group * attn]
    out_refs = refs[n_w + 2 * group * attn : n_w + 2 * group * attn + group * attn]
    a_s, w_s, a_sem, w_sem = refs[n_w + 3 * group * attn :]
    g = lax.rem(meta_ref[0], group)
    n, width = a_refs[0].shape[1], a_refs[0].shape[2] * 2
    half = width // 2

    def w_copy(c, to, m, j):
        rows = pl.ds(pl.multiple_of(xor(g, j) * width, width), width)
        return pltpu.make_async_copy(
            w_refs[c][m].at[rows, :], w_s.at[to, pl.ds((m * group + j) * width, width), :], w_sem.at[to]
        )

    def each_w(act):
        for to in range(attn):
            for c, code in enumerate(cands):

                @pl.when(meta_ref[sel_at + to] == code)
                def _(c=c, to=to):
                    for m in range(attn):
                        for j in range(group):
                            act(w_copy(c, to, m, j))

    def a_copies(k):
        found = []
        for m in range(attn):
            for j in range(group):
                for part in range(2):
                    at = (m * group + j) * width + part * half
                    found.append(
                        pltpu.make_async_copy(
                            a_refs[(m * group + j) * 2 + part].at[j ^ k],
                            a_s.at[k, :, pl.ds(at, half)],
                            a_sem.at[k],
                        )
                    )
        return found

    each_w(lambda copy: copy.start())
    for k in range(group):
        for copy in a_copies(k):
            copy.start()
    each_w(lambda copy: copy.wait())
    cols = w_s.shape[2]
    for k in range(group):
        for copy in a_copies(k):
            copy.wait()
        if cols % HEAD == 0:
            weights = jnp.concatenate([w_s[to] for to in range(attn)], axis=1)
            found = jnp.dot(a_s[k], weights, preferred_element_type=jnp.float32)
            for to in range(attn):
                out_refs[to * group + k][...] = found[:, to * cols : (to + 1) * cols].astype(jnp.bfloat16)
        else:
            for to in range(attn):
                out_refs[to * group + k][...] = jnp.dot(
                    a_s[k], w_s[to], preferred_element_type=jnp.float32
                ).astype(jnp.bfloat16)


def place_kernel(group, attn, rounds, zz_at, meta_ref, y_ref, *refs):
    out_ref = refs[-1]
    g, y = lax.rem(meta_ref[0], group), y_ref[0]
    cols = refs[0].shape[1]
    for r in range(rounds):
        for m in range(attn):
            for k in range(group):
                at = ((meta_ref[zz_at + r] * group + xor(g, k)) * attn + xor(y, m)) * cols
                out_ref[:, pl.ds(pl.multiple_of(at, cols), cols)] = refs[(r * attn + m) * group + k][...]


def schedule(planes, attn):
    rounds = planes // attn
    table = np.zeros((planes, rounds, attn), np.int64)
    for z in range(planes):
        for y in range(attn):
            blocks = range(y * rounds, (y + 1) * rounds)
            table[z, :, y] = sorted(blocks, key=lambda b: (abs(b - z), b))
    return table


def code_of(z, block, planes):
    return z - block if block <= z else planes - 1 + block - z


def shards(dense, attn, queries, keys, values, segments, out_weight):
    n = queries.shape[0]
    tokens = segments.shape[0]
    group = keys.shape[1] // HEAD
    heads = queries.shape[1] // HEAD // group
    width = heads * HEAD
    planes = dense // group
    rounds = planes // attn
    hops = min(-(-(tokens // 2 - 1) // (n * group)), planes - 1)
    cols = out_weight.shape[1] // attn

    def number(z, g, y):
        return (z * group + g) * attn + y

    def pairs(move):
        found = []
        for z in range(planes):
            for g in range(group):
                for y in range(attn):
                    to = move(z, g, y)
                    if 0 <= to[0] < planes:
                        found.append((number(z, g, y), number(*to)))
        return found

    def across(array, j, m):
        return lax.ppermute(array, AXES, pairs(lambda z, g, y: (z, g ^ j, y ^ m)))

    def up(array):
        return lax.ppermute(array, AXES, pairs(lambda z, g, y: (z + 1, g, y)))

    def down(array):
        return lax.ppermute(array, AXES, pairs(lambda z, g, y: (z - 1, g, y)))

    order = schedule(planes, attn)
    length = rounds * attn + rounds
    table = np.zeros((planes, attn, length), np.int32)
    cands = [set() for _ in range(rounds)]
    for z in range(planes):
        for y in range(attn):
            for r in range(rounds):
                for m in range(attn):
                    code = code_of(z, int(order[z, r, y ^ m]), planes)
                    table[z, y, r * attn + m] = code
                    cands[r].add(code)
                table[z, y, rounds * attn + r] = order[z, r, y] - y * rounds
    device = lax.axis_index("dense").astype(jnp.int32)
    y_here = lax.axis_index("attn").astype(jnp.int32)
    row = lax.dynamic_index_in_dim(
        jnp.asarray(table.reshape(planes * attn, length)), device // group * attn + y_here, 0, keepdims=False
    )
    meta = jnp.concatenate([device[None], row])
    y_meta = y_here[None]

    kv = pl.pallas_call(
        functools.partial(split_kv_kernel, group),
        out_shape=[jax.ShapeDtypeStruct((n, 2 * HEAD), jnp.bfloat16)] * group,
        in_specs=[SMEM, VMEM, VMEM],
        out_specs=[VMEM] * group,
        name="split_kv",
    )(meta, keys, values)
    kv = [kv[0]] + [across(kv[j], j, 0) for j in range(1, group)]
    all_kv = list(kv)
    for _ in range(hops):
        kv = [up(piece) for piece in kv]
        all_kv += kv

    q = pl.pallas_call(
        functools.partial(split_q_kernel, group),
        out_shape=[jax.ShapeDtypeStruct((n, width), jnp.bfloat16)] * group,
        in_specs=[SMEM, VMEM],
        out_specs=[VMEM] * group,
        name="split_q",
    )(meta, queries)
    q = [q[0]] + [across(q[j], j, 0) for j in range(1, group)]

    own = []
    for m in range(attn):
        part = lax.dynamic_slice_in_dim(out_weight, lax.bitwise_xor(y_here, jnp.int32(m)) * cols, cols, 1)
        own.append(part if m == 0 else across(part, 0, m))
    blocks = {0: own}
    here = own
    for s in range(1, planes):
        here = [down(part) for part in here]
        blocks[planes - 1 + s] = here
    tied = lax.optimization_barrier(tuple(own) + tuple(all_kv[-group:]))
    here = list(tied[:attn])
    all_kv[-group:] = tied[attn:]
    for s in range(1, planes):
        here = [up(part) for part in here]
        blocks[s] = here

    n_kv = (hops + 1) * group
    n_copies = group * heads + 2 * n_kv
    attended = pl.pallas_call(
        functools.partial(attention_kernel, group, hops, heads),
        out_shape=[jax.ShapeDtypeStruct((group, n, width // 2), jnp.bfloat16)] * 2,
        in_specs=[SMEM, SMEM, VMEM] + [ANY] * (group + n_kv),
        out_specs=[VMEM] * 2,
        scratch_shapes=[
            pltpu.VMEM((group, heads, n, HEAD), jnp.bfloat16),
            pltpu.VMEM((n_kv, n, HEAD), jnp.bfloat16),
            pltpu.VMEM((n_kv, n, HEAD), jnp.bfloat16),
            pltpu.VMEM((n_kv, heads, n, n), jnp.float32),
            pltpu.VMEM((heads, n, HEAD), jnp.float32),
            pltpu.VMEM((heads, n, HEAD), jnp.float32),
            pltpu.VMEM((heads, n, HEAD), jnp.float32),
            pltpu.VMEM((n, HEAD), jnp.float32),
            pltpu.SemaphoreType.DMA((n_copies,)),
        ],
        compiler_params=params(56),
        cost_estimate=pl.CostEstimate(
            flops=10 * 10**9, bytes_accessed=4 * 2**20, transcendentals=10**7
        ),
        name="attention",
    )(meta, segments, segments.reshape(dense, n), *q, *all_kv)

    gathered = {}
    for m in range(attn):
        for j in range(group):
            gathered[j, m] = [half if j == m == 0 else across(half, j, m) for half in attended]
    everything = [half for m in range(attn) for j in range(group) for half in gathered[j, m]]

    placed = []
    for r in range(rounds):
        codes = sorted(cands[r])
        found = pl.pallas_call(
            functools.partial(project_kernel, group, attn, codes, 1 + r * attn),
            out_shape=[jax.ShapeDtypeStruct((n, cols), jnp.bfloat16)] * (attn * group),
            in_specs=[SMEM] + [ANY] * (len(codes) * attn + 2 * group * attn),
            out_specs=[VMEM] * (attn * group),
            scratch_shapes=[
                pltpu.VMEM((group, n, attn * group * width), jnp.bfloat16),
                pltpu.VMEM((attn, attn * group * width, cols), jnp.bfloat16),
                pltpu.SemaphoreType.DMA((group,)),
                pltpu.SemaphoreType.DMA((attn,)),
            ],
            compiler_params=params(40),
            cost_estimate=pl.CostEstimate(
                flops=4 * 10**9, bytes_accessed=10 * 2**20, transcendentals=0
            ),
            name="project",
        )(meta, *[part for code in codes for part in blocks[code]], *everything)
        for m in range(attn):
            for k in range(group):
                piece = found[m * group + k]
                placed.append(piece if m == k == 0 else across(piece, k, m))

    if cols % HEAD == 0:
        return pl.pallas_call(
            functools.partial(place_kernel, group, attn, rounds, 1 + rounds * attn),
            out_shape=jax.ShapeDtypeStruct((n, rounds * group * attn * cols), jnp.bfloat16),
            in_specs=[SMEM, SMEM] + [VMEM] * len(placed),
            out_specs=VMEM,
            name="place",
        )(meta, y_meta, *placed)
    out = jnp.zeros((n, rounds * group * attn * cols), jnp.bfloat16)
    g = lax.rem(device, jnp.int32(group))
    for r in range(rounds):
        for m in range(attn):
            for k in range(group):
                at = ((meta[1 + rounds * attn + r] * group + xor(g, k)) * attn + xor(y_here, m)) * cols
                out = lax.dynamic_update_slice_in_dim(out, placed[(r * attn + m) * group + k], at, 1)
    return out


def solution(mesh):
    return jax.shard_map(
        functools.partial(shards, mesh.shape["dense"], mesh.shape["attn"]),
        mesh=mesh,
        in_specs=(
            P("dense", "attn"),
            P("dense", "attn"),
            P("dense", "attn"),
            P(),
            P("attn", "dense"),
        ),
        out_specs=P("dense", "attn"),
        check_vma=False,
    )
```

time: 299 us -> 237 us (0.79)
  starting transfers between devices: 0.12 us -> 96 us
  waiting for transfers between devices: 164 us -> 77.9 us
  matrix products: 77.3 us -> 0 us
  Pallas kernels: 0 us -> 50 us
  other arithmetic: 32.8 us -> 0.58 us
  between operations: 14.5 us -> 0.68 us
    all_gather x3 -> x0, waiting for transfers between devices: 132 us -> none  [the longest x1 53.6 us: attend(): value_piece = lax.all_gather(values, 'dense', axis=0, tiled=True)]
    ppermute x0 -> x55, starting transfers between devices: none -> 96 us  [the longest x35 55.2 us: across(): return lax.ppermute(array, AXES, pairs(lambda z, g, y: (z, g ^ j, y ^ m)))]
    ppermute x0 -> x55, waiting for transfers between devices: none -> 77.9 us  [the longest x35 75.1 us: across(): return lax.ppermute(array, AXES, pairs(lambda z, g, y: (z, g ^ j, y ^ m)))]
    pallas_call x0 -> x6, Pallas kernels: none -> 50 us  [the longest x1 24.1 us: shards(): pl.pallas_call(functools.partial(attention_kernel, group, hops, heads), o...]
    dot_general x3 -> x0, matrix products: 45.3 us -> none  [the longest x2 33.7 us: compute(): jnp.einsum('qgjd,kgd->gjqk', sliced, key_heads, preferred_element_type=jn...]
    cond x2 -> x0, matrix products: 32 us -> none  [attend(): lax.cond(jnp.any(visible), compute, lambda state: state, initial[which_bl...]
    reduce_scatter x1 -> x0, waiting for transfers between devices: 31.6 us -> none  [project(): lax.psum_scatter(partial_sums.astype(jnp.bfloat16), 'attn', scatter_dimen...]
    reduce_sum x2 -> x0, other arithmetic: 29.4 us -> none  [compute(): totals = jnp.sum(weights, axis=-1)]
  transfers between devices with their start and end apart: 4 -> 55, of which waited for: 4 -> 10; matrix products, arithmetic and copies ran while one was open for 35% -> 1% of each run, Pallas kernels for 0% -> 19%
where the time goes in v1:
time: 237 us; the launch traced here: 234 us
  starting transfers between devices  96 us (41%)
  waiting for transfers between devices  77.9 us (33%)
  Pallas kernels  50 us (21%)
  local copies, waits for them, and re-layouts  9.19 us (4%)
    ppermute x35, waiting for transfers between devices, across(): return lax.ppermute(array, AXES, pairs(lambda z, g, y: (z, g ^ j, y ^ m)))  75.1 us
    ppermute x35, starting transfers between devices, across(): return lax.ppermute(array, AXES, pairs(lambda z, g, y: (z, g ^ j, y ^ m)))  55.2 us
    pallas_call x1, Pallas kernels, shards(): pl.pallas_call(functools.partial(attention_kernel, group, hops, heads), o...  24.1 us
    ppermute x6, starting transfers between devices, down(): return lax.ppermute(array, AXES, pairs(lambda z, g, y: (z - 1, g, y)))  22.7 us
    pallas_call x2, Pallas kernels, shards(): pl.pallas_call(functools.partial(project_kernel, group, attn, codes, 1 +...  19.1 us
    ppermute x14, starting transfers between devices, up(): return lax.ppermute(array, AXES, pairs(lambda z, g, y: (z + 1, g, y)))  18 us
    unnamed x72, local copies, waits for them, and re-layouts  6.63 us
  transfers between devices with their start and end apart: 55, of which 10 were waited for; matrix products, arithmetic and copies ran while one was open for 1% of the time, Pallas kernels for 19%

profile of v1, /device:TPU:25, one launch (start us, length us, event | category | flops | bytes accessed | tf_op | source)
XLA Modules:
  0.0 234.3 jit_solution(2393422776453694928)
XLA Ops:
  0.0 0.7 fusion
  1.3 1.9 split_kv.1
  3.2 1.3 collective-permute-start.1
  4.5 0.7 collective-permute-start.3
  5.2 1.2 collective-permute-start.6
  6.9 2.7 %collective-permute-done.1.refs_8_ = bf16[256,256]{1,0:T(8,128)(2,1)S(1)} collective-permute-done((bf16[256,256]{1,0:T(8,128)(2,1)}, bf16[256,256]{1,0:T(8,128)(2,1)S(1)}, u32[]{:S(2)}, u32[]{:S(2)}) %collective-permute-start.1) | collective-permute-done | bytes 131104 | tf_op jit(solution)/shard_map/ppermute | solution.py:278
  9.7 1.3 collective-permute-start.2
  10.9 1.3 constant_dynamic-slice_fusion
  12.2 1.3 collective-permute-start
  13.5 1.3 collective-permute-start.4
  14.8 1.3 collective-permute-start.7
  16.2 1.3 collective-permute-start.10
  18.1 5.9 %collective-permute-start.16 = (bf16[2048,128]{1,0:T(8,128)(2,1)S(1)}, bf16[2048,128]{1,0:T(8,128)(2,1)S(1)}, u32[]{:S(2)}, u32[]{:S(2)}) collective-permute-start(bf16[2048,128]{1,0:T(8,128)(2,1)S(1)} %get-tuple-element.41.refs_0_), channel_id=1, source_target_pairs={{8,0},{9,1},{10,2},{11,3},{12,4},{13,5},{14,6},{15,7},{16,8},{17,9... | collective-permute-start | bytes 1572872 | tf_op jit(solution)/shard_map/ppermute | solution.py:281
  24.1 1.3 collective-permute-start.5
  25.4 1.3 collective-permute-start.8
  26.7 1.3 collective-permute-start.11
  28.0 2.3 split_q.1
  30.4 4.3 %collective-permute-start.20 = (bf16[256,512]{1,0:T(8,128)(2,1)}, bf16[256,512]{1,0:T(8,128)(2,1)S(1)}, u32[]{:S(2)}, u32[]{:S(2)}) collective-permute-start(bf16[256,512]{1,0:T(8,128)(2,1)} %get-tuple-element.44), channel_id=1, source_target_pairs={{0,2},{1,3},{2,0},{3,1},{4,6},{5,7},{6,4},{7,5},{8,10},{9,11},{10,... | collective-permute-start | bytes 786440 | tf_op jit(solution)/shard_map/ppermute | solution.py:275
  35.3 1.2 collective-permute-start.21
  37.2 2.6 %collective-permute-start.22 = (bf16[256,512]{1,0:T(8,128)(2,1)}, bf16[256,512]{1,0:T(8,128)(2,1)S(1)}, u32[]{:S(2)}, u32[]{:S(2)}) collective-permute-start(bf16[256,512]{1,0:T(8,128)(2,1)} %get-tuple-element.46), channel_id=1, source_target_pairs={{0,6},{1,7},{2,4},{3,5},{4,2},{5,3},{6,0},{7,1},{8,14},{9,15},{10,... | collective-permute-start | bytes 786440 | tf_op jit(solution)/shard_map/ppermute | solution.py:275
  40.4 1.3 collective-permute-start.12
  41.7 1.3 collective-permute-start.13
  43.0 4.6 %collective-permute-start.17 = (bf16[2048,128]{1,0:T(8,128)(2,1)S(1)}, bf16[2048,128]{1,0:T(8,128)(2,1)S(1)}, u32[]{:S(2)}, u32[]{:S(2)}) collective-permute-start(bf16[2048,128]{1,0:T(8,128)(2,1)S(1)} %collective-permute-done.refs_1_), channel_id=1, source_target_pairs={{8,0},{9,1},{10,2},{11,3},{12,4},{13,5},{14,6},{15,7},{16,8},{17,9... | collective-permute-start | bytes 1572872 | tf_op jit(solution)/shard_map/ppermute | solution.py:281
  47.7 3.4 %collective-permute-start.18 = (bf16[2048,128]{1,0:T(8,128)(2,1)S(1)}, bf16[2048,128]{1,0:T(8,128)(2,1)S(1)}, u32[]{:S(2)}, u32[]{:S(2)}) collective-permute-start(bf16[2048,128]{1,0:T(8,128)(2,1)S(1)} %collective-permute-done.16.refs_6_), channel_id=1, source_target_pairs={{8,0},{9,1},{10,2},{11,3},{12,4},{13,5},{14,6},{15,7},{16,8},{17,9... | collective-permute-start | bytes 1572872 | tf_op jit(solution)/shard_map/ppermute | solution.py:281
  51.8 24.1 %attention.1 = (bf16[4,256,256]{2,1,0:T(8,128)(2,1)}, bf16[4,256,256]{2,1,0:T(8,128)(2,1)}) custom-call(s32[7]{0:T(128)} %pad_add_fusion.meta_ref, s32[4096]{0:T(1024)} %seg_ref.1, s32[16,256]{1,0:T(8,128)} %reshape.3.segrow_ref, bf16[256,512]{1,0:T(8,128)(2,1)} %get-tuple-element.43.refs_0_, bf16[256,512]{1,0:T(8,128)(2,1)} %copy-done.22, ...), custom_call_target="tpu_custom_call" | custom-call | flops 10000000000 | bytes 4194304 | tf_op jit(solution)/shard_map/attention/pallas_call | solution.py:343
  76.0 3.0 %collective-permute-start.23 = (bf16[4,256,256]{2,1,0:T(8,128)(2,1)}, bf16[4,256,256]{2,1,0:T(8,128)(2,1)S(1)}, u32[]{:S(2)}, u32[]{:S(2)}) collective-permute-start(bf16[4,256,256]{2,1,0:T(8,128)(2,1)} %get-tuple-element.51.refs_10_.refs_12_), channel_id=1, source_target_pairs={{0,2},{1,3},{2,0},{3,1},{4,6},{5,7},{6,4},{7,5},{8,10},{9,11},{10,... | collective-permute-start | bytes 1572872 | tf_op jit(solution)/shard_map/ppermute | solution.py:275
  79.1 1.2 collective-permute-start.25
  80.6 2.1 collective-permute-start.27
  83.0 9.4 %collective-permute-done.25.refs_14_.refs_16_ = bf16[4,256,256]{2,1,0:T(8,128)(2,1)S(1)} collective-permute-done((bf16[4,256,256]{2,1,0:T(8,128)(2,1)}, bf16[4,256,256]{2,1,0:T(8,128)(2,1)S(1)}, u32[]{:S(2)}, u32[]{:S(2)}) %collective-permute-start.25) | collective-permute-done | bytes 524320 | tf_op jit(solution)/shard_map/ppermute | solution.py:275
  92.6 11.0 %collective-permute-done.26.refs_15_.refs_17_ = bf16[4,256,256]{2,1,0:T(8,128)(2,1)S(1)} collective-permute-done((bf16[4,256,256]{2,1,0:T(8,128)(2,1)}, bf16[4,256,256]{2,1,0:T(8,128)(2,1)S(1)}, u32[]{:S(2)}, u32[]{:S(2)}) %collective-permute-start.26) | collective-permute-done | bytes 524320 | tf_op jit(solution)/shard_map/ppermute | solution.py:275
  103.6 2.3 collective-permute-start.31
  105.9 10.7 %collective-permute-done.27.refs_16_.refs_18_ = bf16[4,256,256]{2,1,0:T(8,128)(2,1)S(1)} collective-permute-done((bf16[4,256,256]{2,1,0:T(8,128)(2,1)}, bf16[4,256,256]{2,1,0:T(8,128)(2,1)S(1)}, u32[]{:S(2)}, u32[]{:S(2)}) %collective-permute-start.27) | collective-permute-done | bytes 524320 | tf_op jit(solution)/shard_map/ppermute | solution.py:275
  116.6 10.4 %collective-permute-done.28.refs_17_.refs_19_ = bf16[4,256,256]{2,1,0:T(8,128)(2,1)S(1)} collective-permute-done((bf16[4,256,256]{2,1,0:T(8,128)(2,1)}, bf16[4,256,256]{2,1,0:T(8,128)(2,1)S(1)}, u32[]{:S(2)}, u32[]{:S(2)}) %collective-permute-start.28) | collective-permute-done | bytes 524320 | tf_op jit(solution)/shard_map/ppermute | solution.py:275
  127.0 1.2 collective-permute-start.33
  128.1 1.2 collective-permute-start.34
  129.3 1.1 collective-permute-start.35
  130.5 1.3 collective-permute-start.14
  131.8 1.3 collective-permute-start.15
  133.1 8.9 %collective-permute-done.33.refs_22_.refs_24_ = bf16[4,256,256]{2,1,0:T(8,128)(2,1)S(1)} collective-permute-done((bf16[4,256,256]{2,1,0:T(8,128)(2,1)}, bf16[4,256,256]{2,1,0:T(8,128)(2,1)S(1)}, u32[]{:S(2)}, u32[]{:S(2)}) %collective-permute-start.33) | collective-permute-done | bytes 524320 | tf_op jit(solution)/shard_map/ppermute | solution.py:275
  142.0 1.3 collective-permute-start.19
  143.3 9.9 %collective-permute-done.34.refs_23_.refs_25_ = bf16[4,256,256]{2,1,0:T(8,128)(2,1)S(1)} collective-permute-done((bf16[4,256,256]{2,1,0:T(8,128)(2,1)}, bf16[4,256,256]{2,1,0:T(8,128)(2,1)S(1)}, u32[]{:S(2)}, u32[]{:S(2)}) %collective-permute-start.34) | collective-permute-done | bytes 524320 | tf_op jit(solution)/shard_map/ppermute | solution.py:275
  153.2 1.5 collective-permute-start.36
  154.8 9.7 %collective-permute-done.35.refs_24_.refs_26_ = bf16[4,256,256]{2,1,0:T(8,128)(2,1)S(1)} collective-permute-done((bf16[4,256,256]{2,1,0:T(8,128)(2,1)}, bf16[4,256,256]{2,1,0:T(8,128)(2,1)S(1)}, u32[]{:S(2)}, u32[]{:S(2)}) %collective-permute-start.35) | collective-permute-done | bytes 524320 | tf_op jit(solution)/shard_map/ppermute | solution.py:275
  164.5 1.3 collective-permute-start.46
  165.8 1.3 collective-permute-start.44
  167.1 1.3 collective-permute-start.45
  168.4 6.2 %collective-permute-start.47 = (bf16[2048,128]{1,0:T(8,128)(2,1)S(1)}, bf16[2048,128]{1,0:T(8,128)(2,1)S(1)}, u32[]{:S(2)}, u32[]{:S(2)}) collective-permute-start(bf16[2048,128]{1,0:T(8,128)(2,1)S(1)} %collective-permute-done.19.refs_9_), channel_id=1, source_target_pairs={{8,0},{9,1},{10,2},{11,3},{12,4},{13,5},{14,6},{15,7},{16,8},{17,9... | collective-permute-start | bytes 1572872 | tf_op jit(solution)/shard_map/ppermute | solution.py:281
  174.6 1.0 copy-done.3
  175.7 1.0 copy-done.4
  176.7 9.4 %project.2 = (bf16[256,128]{1,0:T(8,128)(2,1)S(1)}, bf16[256,128]{1,0:T(8,128)(2,1)S(1)}, bf16[256,128]{1,0:T(8,128)(2,1)S(1)}, bf16[256,128]{1,0:T(8,128)(2,1)S...) custom-call(s32[7]{0:T(128)S(1)} %copy-done.2, ...), custom_call_target="tpu_custom_call" | custom-call | flops 4000000000 | bytes 10485760 | tf_op jit(solution)/shard_map/project/pallas_call | solution.py:375
  186.8 12.6 %collective-permute-start.37 = (bf16[256,128]{1,0:T(8,128)(2,1)S(1)}, bf16[256,128]{1,0:T(8,128)(2,1)S(1)}, u32[]{:S(2)}, u32[]{:S(2)}) collective-permute-start(bf16[256,128]{1,0:T(8,128)(2,1)S(1)} %get-tuple-element.54), channel_id=1, source_target_pairs={{0,2},{1,3},{2,0},{3,1},{4,6},{5,7},{6,4},{7,5},{8,10},{9,11},{10,... | collective-permute-start | bytes 196616 | tf_op jit(solution)/shard_map/ppermute | solution.py:275
  199.6 1.4 collective-permute-start.39
  201.0 4.9 %collective-permute-start.40 = (bf16[256,128]{1,0:T(8,128)(2,1)S(1)}, bf16[256,128]{1,0:T(8,128)(2,1)S(1)}, u32[]{:S(2)}, u32[]{:S(2)}) collective-permute-start(bf16[256,128]{1,0:T(8,128)(2,1)S(1)} %get-tuple-element.57), channel_id=1, source_target_pairs={{0,1},{1,0},{2,3},{3,2},{4,5},{5,4},{6,7},{7,6},{8,9},{9,8},{10,11... | collective-permute-start | bytes 196616 | tf_op jit(solution)/shard_map/ppermute | solution.py:275
  205.9 9.7 %project.3 = (bf16[256,128]{1,0:T(8,128)(2,1)S(1)}, bf16[256,128]{1,0:T(8,128)(2,1)S(1)}, bf16[256,128]{1,0:T(8,128)(2,1)S(1)}, bf16[256,128]{1,0:T(8,128)(2,1)S...) custom-call(s32[7]{0:T(128)S(1)} %copy-done.2, ...), custom_call_target="tpu_custom_call" | custom-call | flops 4000000000 | bytes 10485760 | tf_op jit(solution)/shard_map/project/pallas_call | solution.py:375
  216.3 2.3 collective-permute-start.42
  218.6 0.7 collective-permute-start.43
  219.5 1.1 collective-permute-start.49
  220.6 0.8 collective-permute-start.50
  221.4 1.4 collective-permute-start.51
  222.8 1.2 collective-permute-done.43.refs_7_
  224.6 1.8 collective-permute-start.53
  226.4 0.8 collective-permute-start.54
  227.3 3.8 %collective-permute-done.52.refs_13_ = bf16[256,128]{1,0:T(8,128)(2,1)S(1)} collective-permute-done((bf16[256,128]{1,0:T(8,128)(2,1)S(1)}, bf16[256,128]{1,0:T(8,128)(2,1)S(1)}, u32[]{:S(2)}, u32[]{:S(2)}) %collective-permute-start.52) | collective-permute-done | bytes 65568 | tf_op jit(solution)/shard_map/ppermute | solution.py:275
  231.8 2.5 %place.1 = bf16[256,2048]{1,0:T(8,128)(2,1)} custom-call(s32[7]{0:T(128)} %pad_add_fusion.meta_ref, s32[1]{0:T(128)} %bitcast.2.y_ref, bf16[256,128]{1,0:T(8,128)(2,1)} %copy-done, bf16[256,128]{1,0:T(8,128)(2,1)} %copy-done.7, bf16[256,128]{1,0:T(8,128)(2,1)} %copy-done.8, bf16[256,128]{1,0:T(8,128)(2,1)} %copy-done.9, bf16[256,128]{1,0:T(8,128)(2,1)} %copy-done.10, ...), custom_call_target="tpu_custom_call" | custom-call | tf_op jit(solution)/shard_map/place/pallas_call | solution.py:398
  (128 shorter events, 8.1 us)
Async XLA Ops:
  3.2 6.5 %collective-permute-start.1 = (bf16[256,256]{1,0:T(8,128)(2,1)}, bf16[256,256]{1,0:T(8,128)(2,1)S(1)}, u32[]{:S(2)}, u32[]{:S(2)}) collective-permute-start(bf16[256,256]{1,0:T(8,128)(2,1)} %get-tuple-element.37.refs_4_), channel_id=1, source_target_pairs={{0,8},{1,9},{2,10},{3,11},{4,12},{5,13},{6,14},{7,15},{8,16},{9,17... | collective-permute-start | bytes 393224 | tf_op jit(solution)/shard_map/ppermute | solution.py:278
  4.5 9.1 %collective-permute-start.3 = (bf16[256,256]{1,0:T(8,128)(2,1)}, bf16[256,256]{1,0:T(8,128)(2,1)S(1)}, u32[]{:S(2)}, u32[]{:S(2)}) collective-permute-start(bf16[256,256]{1,0:T(8,128)(2,1)} %get-tuple-element.38), channel_id=1, source_target_pairs={{0,2},{1,3},{2,0},{3,1},{4,6},{5,7},{6,4},{7,5},{8,10},{9,11},{10,... | collective-permute-start | bytes 393224 | tf_op jit(solution)/shard_map/ppermute | solution.py:275
  5.2 9.6 %collective-permute-start.6 = (bf16[256,256]{1,0:T(8,128)(2,1)}, bf16[256,256]{1,0:T(8,128)(2,1)S(1)}, u32[]{:S(2)}, u32[]{:S(2)}) collective-permute-start(bf16[256,256]{1,0:T(8,128)(2,1)} %get-tuple-element.39), channel_id=1, source_target_pairs={{0,4},{1,5},{2,6},{3,7},{4,0},{5,1},{6,2},{7,3},{8,12},{9,13},{10,... | collective-permute-start | bytes 393224 | tf_op jit(solution)/shard_map/ppermute | solution.py:275
  6.4 9.7 %collective-permute-start.9 = (bf16[256,256]{1,0:T(8,128)(2,1)}, bf16[256,256]{1,0:T(8,128)(2,1)S(1)}, u32[]{:S(2)}, u32[]{:S(2)}) collective-permute-start(bf16[256,256]{1,0:T(8,128)(2,1)} %get-tuple-element.40), channel_id=1, source_target_pairs={{0,6},{1,7},{2,4},{3,5},{4,2},{5,3},{6,0},{7,1},{8,14},{9,15},{10,... | collective-permute-start | bytes 393224 | tf_op jit(solution)/shard_map/ppermute | solution.py:275
  9.7 7.8 %collective-permute-start.2 = (bf16[256,256]{1,0:T(8,128)(2,1)S(1)}, bf16[256,256]{1,0:T(8,128)(2,1)S(1)}, u32[]{:S(2)}, u32[]{:S(2)}) collective-permute-start(bf16[256,256]{1,0:T(8,128)(2,1)S(1)} %collective-permute-done.1.refs_8_), channel_id=1, source_target_pairs={{0,8},{1,9},{2,10},{3,11},{4,12},{5,13},{6,14},{7,15},{8,16},{9,17... | collective-permute-start | bytes 393224 | tf_op jit(solution)/shard_map/ppermute | solution.py:278
  12.2 28.2 %collective-permute-start = (bf16[2048,128]{1,0:T(8,128)(2,1)S(1)}, bf16[2048,128]{1,0:T(8,128)(2,1)S(1)}, u32[]{:S(2)}, u32[]{:S(2)}) collective-permute-start(bf16[2048,128]{1,0:T(8,128)(2,1)S(1)} %get-tuple-element.69), channel_id=1, source_target_pairs={{0,1},{1,0},{2,3},{3,2},{4,5},{5,4},{6,7},{7,6},{8,9},{9,8},{10,11... | collective-permute-start | bytes 1572872 | tf_op jit(solution)/shard_map/ppermute | solution.py:275
  13.5 16.8 %copy-start.26 = (bf16[256,256]{1,0:T(8,128)(2,1)}, bf16[256,256]{1,0:T(8,128)(2,1)S(1)}, u32[]{:S(2)}) copy-start(bf16[256,256]{1,0:T(8,128)(2,1)S(1)} %collective-permute-done.3.refs_5_) | copy-start | bytes 393220
  13.5 10.5 %collective-permute-start.4 = (bf16[256,256]{1,0:T(8,128)(2,1)S(1)}, bf16[256,256]{1,0:T(8,128)(2,1)S(1)}, u32[]{:S(2)}, u32[]{:S(2)}) collective-permute-start(bf16[256,256]{1,0:T(8,128)(2,1)S(1)} %collective-permute-done.3.refs_5_), channel_id=1, source_target_pairs={{0,8},{1,9},{2,10},{3,11},{4,12},{5,13},{6,14},{7,15},{8,16},{9,17... | collective-permute-start | bytes 393224 | tf_op jit(solution)/shard_map/ppermute | solution.py:278
  14.8 15.5 %copy-start.27 = (bf16[256,256]{1,0:T(8,128)(2,1)}, bf16[256,256]{1,0:T(8,128)(2,1)S(1)}, u32[]{:S(2)}) copy-start(bf16[256,256]{1,0:T(8,128)(2,1)S(1)} %collective-permute-done.6.refs_6_) | copy-start | bytes 393220
  14.8 10.5 %collective-permute-start.7 = (bf16[256,256]{1,0:T(8,128)(2,1)S(1)}, bf16[256,256]{1,0:T(8,128)(2,1)S(1)}, u32[]{:S(2)}, u32[]{:S(2)}) collective-permute-start(bf16[256,256]{1,0:T(8,128)(2,1)S(1)} %collective-permute-done.6.refs_6_), channel_id=1, source_target_pairs={{0,8},{1,9},{2,10},{3,11},{4,12},{5,13},{6,14},{7,15},{8,16},{9,17... | collective-permute-start | bytes 393224 | tf_op jit(solution)/shard_map/ppermute | solution.py:278
  16.2 14.1 %copy-start.28 = (bf16[256,256]{1,0:T(8,128)(2,1)}, bf16[256,256]{1,0:T(8,128)(2,1)S(1)}, u32[]{:S(2)}) copy-start(bf16[256,256]{1,0:T(8,128)(2,1)S(1)} %collective-permute-done.9.refs_7_) | copy-start | bytes 393220
  16.2 10.5 %collective-permute-start.10 = (bf16[256,256]{1,0:T(8,128)(2,1)S(1)}, bf16[256,256]{1,0:T(8,128)(2,1)S(1)}, u32[]{:S(2)}, u32[]{:S(2)}) collective-permute-start(bf16[256,256]{1,0:T(8,128)(2,1)S(1)} %collective-permute-done.9.refs_7_), channel_id=1, source_target_pairs={{0,8},{1,9},{2,10},{3,11},{4,12},{5,13},{6,14},{7,15},{8,16},{9,17... | collective-permute-start | bytes 393224 | tf_op jit(solution)/shard_map/ppermute | solution.py:278
  18.1 29.5 %collective-permute-start.16 = (bf16[2048,128]{1,0:T(8,128)(2,1)S(1)}, bf16[2048,128]{1,0:T(8,128)(2,1)S(1)}, u32[]{:S(2)}, u32[]{:S(2)}) collective-permute-start(bf16[2048,128]{1,0:T(8,128)(2,1)S(1)} %get-tuple-element.41.refs_0_), channel_id=1, source_target_pairs={{8,0},{9,1},{10,2},{11,3},{12,4},{13,5},{14,6},{15,7},{16,8},{17,9... | collective-permute-start | bytes 1572872 | tf_op jit(solution)/shard_map/ppermute | solution.py:281
  24.1 6.3 %collective-permute-start.5 = (bf16[256,256]{1,0:T(8,128)(2,1)S(1)}, bf16[256,256]{1,0:T(8,128)(2,1)S(1)}, u32[]{:S(2)}, u32[]{:S(2)}) collective-permute-start(bf16[256,256]{1,0:T(8,128)(2,1)S(1)} %collective-permute-done.4.refs_9_), channel_id=1, source_target_pairs={{0,8},{1,9},{2,10},{3,11},{4,12},{5,13},{6,14},{7,15},{8,16},{9,17... | collective-permute-start | bytes 393224 | tf_op jit(solution)/shard_map/ppermute | solution.py:278
  25.4 9.3 %collective-permute-start.8 = (bf16[256,256]{1,0:T(8,128)(2,1)S(1)}, bf16[256,256]{1,0:T(8,128)(2,1)S(1)}, u32[]{:S(2)}, u32[]{:S(2)}) collective-permute-start(bf16[256,256]{1,0:T(8,128)(2,1)S(1)} %collective-permute-done.7.refs_10_), channel_id=1, source_target_pairs={{0,8},{1,9},{2,10},{3,11},{4,12},{5,13},{6,14},{7,15},{8,16},{9,17... | collective-permute-start | bytes 393224 | tf_op jit(solution)/shard_map/ppermute | solution.py:278
  26.7 9.8 %collective-permute-start.11 = (bf16[256,256]{1,0:T(8,128)(2,1)S(1)}, bf16[256,256]{1,0:T(8,128)(2,1)S(1)}, u32[]{:S(2)}, u32[]{:S(2)}) collective-permute-start(bf16[256,256]{1,0:T(8,128)(2,1)S(1)} %collective-permute-done.10.refs_11_), channel_id=1, source_target_pairs={{0,8},{1,9},{2,10},{3,11},{4,12},{5,13},{6,14},{7,15},{8,16},{9,17... | collective-permute-start | bytes 393224 | tf_op jit(solution)/shard_map/ppermute | solution.py:278
  30.3 20.8 %copy-start.33 = (bf16[256,256]{1,0:T(8,128)(2,1)}, bf16[256,256]{1,0:T(8,128)(2,1)S(1)}, u32[]{:S(2)}) copy-start(bf16[256,256]{1,0:T(8,128)(2,1)S(1)} %collective-permute-done.5.refs_13_) | copy-start | bytes 393220
  30.4 11.3 %collective-permute-start.20 = (bf16[256,512]{1,0:T(8,128)(2,1)}, bf16[256,512]{1,0:T(8,128)(2,1)S(1)}, u32[]{:S(2)}, u32[]{:S(2)}) collective-permute-start(bf16[256,512]{1,0:T(8,128)(2,1)} %get-tuple-element.44), channel_id=1, source_target_pairs={{0,2},{1,3},{2,0},{3,1},{4,6},{5,7},{6,4},{7,5},{8,10},{9,11},{10,... | collective-permute-start | bytes 786440 | tf_op jit(solution)/shard_map/ppermute | solution.py:275
  35.3 7.7 %collective-permute-start.21 = (bf16[256,512]{1,0:T(8,128)(2,1)}, bf16[256,512]{1,0:T(8,128)(2,1)S(1)}, u32[]{:S(2)}, u32[]{:S(2)}) collective-permute-start(bf16[256,512]{1,0:T(8,128)(2,1)} %get-tuple-element.45), channel_id=1, source_target_pairs={{0,4},{1,5},{2,6},{3,7},{4,0},{5,1},{6,2},{7,3},{8,12},{9,13},{10,... | collective-permute-start | bytes 786440 | tf_op jit(solution)/shard_map/ppermute | solution.py:275
  37.2 13.9 %collective-permute-start.22 = (bf16[256,512]{1,0:T(8,128)(2,1)}, bf16[256,512]{1,0:T(8,128)(2,1)S(1)}, u32[]{:S(2)}, u32[]{:S(2)}) collective-permute-start(bf16[256,512]{1,0:T(8,128)(2,1)} %get-tuple-element.46), channel_id=1, source_target_pairs={{0,6},{1,7},{2,4},{3,5},{4,2},{5,3},{6,0},{7,1},{8,14},{9,15},{10,... | collective-permute-start | bytes 786440 | tf_op jit(solution)/shard_map/ppermute | solution.py:275
  40.4 38.6 %collective-permute-start.12 = (bf16[2048,128]{1,0:T(8,128)(2,1)S(1)}, bf16[2048,128]{1,0:T(8,128)(2,1)S(1)}, u32[]{:S(2)}, u32[]{:S(2)}) collective-permute-start(bf16[2048,128]{1,0:T(8,128)(2,1)S(1)} %get-tuple-element.41.refs_0_), channel_id=1, source_target_pairs={{0,8},{1,9},{2,10},{3,11},{4,12},{5,13},{6,14},{7,15},{8,16},{9,17... | collective-permute-start | bytes 1572872 | tf_op jit(solution)/shard_map/ppermute | solution.py:278
  41.7 37.4 %collective-permute-start.13 = (bf16[2048,128]{1,0:T(8,128)(2,1)S(1)}, bf16[2048,128]{1,0:T(8,128)(2,1)S(1)}, u32[]{:S(2)}, u32[]{:S(2)}) collective-permute-start(bf16[2048,128]{1,0:T(8,128)(2,1)S(1)} %collective-permute-done.refs_1_), channel_id=1, source_target_pairs={{0,8},{1,9},{2,10},{3,11},{4,12},{5,13},{6,14},{7,15},{8,16},{9,17... | collective-permute-start | bytes 1572872 | tf_op jit(solution)/shard_map/ppermute | solution.py:278
  43.0 37.3 %collective-permute-start.17 = (bf16[2048,128]{1,0:T(8,128)(2,1)S(1)}, bf16[2048,128]{1,0:T(8,128)(2,1)S(1)}, u32[]{:S(2)}, u32[]{:S(2)}) collective-permute-start(bf16[2048,128]{1,0:T(8,128)(2,1)S(1)} %collective-permute-done.refs_1_), channel_id=1, source_target_pairs={{8,0},{9,1},{10,2},{11,3},{12,4},{13,5},{14,6},{15,7},{16,8},{17,9... | collective-permute-start | bytes 1572872 | tf_op jit(solution)/shard_map/ppermute | solution.py:281
  47.7 32.9 %collective-permute-start.18 = (bf16[2048,128]{1,0:T(8,128)(2,1)S(1)}, bf16[2048,128]{1,0:T(8,128)(2,1)S(1)}, u32[]{:S(2)}, u32[]{:S(2)}) collective-permute-start(bf16[2048,128]{1,0:T(8,128)(2,1)S(1)} %collective-permute-done.16.refs_6_), channel_id=1, source_target_pairs={{8,0},{9,1},{10,2},{11,3},{12,4},{13,5},{14,6},{15,7},{16,8},{17,9... | collective-permute-start | bytes 1572872 | tf_op jit(solution)/shard_map/ppermute | solution.py:281
  76.0 98.6 %copy-start.2 = (s32[7]{0:T(128)S(1)}, s32[7]{0:T(128)}, u32[]{:S(2)}) copy-start(s32[7]{0:T(128)} %pad_add_fusion.meta_ref) | copy-start | bytes 88
  76.0 6.7 %collective-permute-start.23 = (bf16[4,256,256]{2,1,0:T(8,128)(2,1)}, bf16[4,256,256]{2,1,0:T(8,128)(2,1)S(1)}, u32[]{:S(2)}, u32[]{:S(2)}) collective-permute-start(bf16[4,256,256]{2,1,0:T(8,128)(2,1)} %get-tuple-element.51.refs_10_.refs_12_), channel_id=1, source_target_pairs={{0,2},{1,3},{2,0},{3,1},{4,6},{5,7},{6,4},{7,5},{8,10},{9,11},{10,... | collective-permute-start | bytes 1572872 | tf_op jit(solution)/shard_map/ppermute | solution.py:275
  79.0 3.7 %collective-permute-start.24 = (bf16[4,256,256]{2,1,0:T(8,128)(2,1)}, bf16[4,256,256]{2,1,0:T(8,128)(2,1)S(1)}, u32[]{:S(2)}, u32[]{:S(2)}) collective-permute-start(bf16[4,256,256]{2,1,0:T(8,128)(2,1)} %get-tuple-element.52.refs_11_.refs_13_), channel_id=1, source_target_pairs={{0,2},{1,3},{2,0},{3,1},{4,6},{5,7},{6,4},{7,5},{8,10},{9,11},{10,... | collective-permute-start | bytes 1572872 | tf_op jit(solution)/shard_map/ppermute | solution.py:275
  79.1 13.3 %collective-permute-start.25 = (bf16[4,256,256]{2,1,0:T(8,128)(2,1)}, bf16[4,256,256]{2,1,0:T(8,128)(2,1)S(1)}, u32[]{:S(2)}, u32[]{:S(2)}) collective-permute-start(bf16[4,256,256]{2,1,0:T(8,128)(2,1)} %get-tuple-element.51.refs_10_.refs_12_), channel_id=1, source_target_pairs={{0,4},{1,5},{2,6},{3,7},{4,0},{5,1},{6,2},{7,3},{8,12},{9,13},{10,... | collective-permute-start | bytes 1572872 | tf_op jit(solution)/shard_map/ppermute | solution.py:275
  80.3 23.3 %collective-permute-start.26 = (bf16[4,256,256]{2,1,0:T(8,128)(2,1)}, bf16[4,256,256]{2,1,0:T(8,128)(2,1)S(1)}, u32[]{:S(2)}, u32[]{:S(2)}) collective-permute-start(bf16[4,256,256]{2,1,0:T(8,128)(2,1)} %get-tuple-element.52.refs_11_.refs_13_), channel_id=1, source_target_pairs={{0,4},{1,5},{2,6},{3,7},{4,0},{5,1},{6,2},{7,3},{8,12},{9,13},{10,... | collective-permute-start | bytes 1572872 | tf_op jit(solution)/shard_map/ppermute | solution.py:275
  80.6 36.0 %collective-permute-start.27 = (bf16[4,256,256]{2,1,0:T(8,128)(2,1)}, bf16[4,256,256]{2,1,0:T(8,128)(2,1)S(1)}, u32[]{:S(2)}, u32[]{:S(2)}) collective-permute-start(bf16[4,256,256]{2,1,0:T(8,128)(2,1)} %get-tuple-element.51.refs_10_.refs_12_), channel_id=1, source_target_pairs={{0,6},{1,7},{2,4},{3,5},{4,2},{5,3},{6,0},{7,1},{8,14},{9,15},{10,... | collective-permute-start | bytes 1572872 | tf_op jit(solution)/shard_map/ppermute | solution.py:275
  82.7 44.3 %collective-permute-start.28 = (bf16[4,256,256]{2,1,0:T(8,128)(2,1)}, bf16[4,256,256]{2,1,0:T(8,128)(2,1)S(1)}, u32[]{:S(2)}, u32[]{:S(2)}) collective-permute-start(bf16[4,256,256]{2,1,0:T(8,128)(2,1)} %get-tuple-element.52.refs_11_.refs_13_), channel_id=1, source_target_pairs={{0,6},{1,7},{2,4},{3,5},{4,2},{5,3},{6,0},{7,1},{8,14},{9,15},{10,... | collective-permute-start | bytes 1572872 | tf_op jit(solution)/shard_map/ppermute | solution.py:275
  82.8 45.4 %collective-permute-start.29 = (bf16[4,256,256]{2,1,0:T(8,128)(2,1)}, bf16[4,256,256]{2,1,0:T(8,128)(2,1)S(1)}, u32[]{:S(2)}, u32[]{:S(2)}) collective-permute-start(bf16[4,256,256]{2,1,0:T(8,128)(2,1)} %get-tuple-element.51.refs_10_.refs_12_), channel_id=1, source_target_pairs={{0,1},{1,0},{2,3},{3,2},{4,5},{5,4},{6,7},{7,6},{8,9},{9,8},{10,11... | collective-permute-start | bytes 1572872 | tf_op jit(solution)/shard_map/ppermute | solution.py:275
  92.4 37.0 %collective-permute-start.30 = (bf16[4,256,256]{2,1,0:T(8,128)(2,1)}, bf16[4,256,256]{2,1,0:T(8,128)(2,1)S(1)}, u32[]{:S(2)}, u32[]{:S(2)}) collective-permute-start(bf16[4,256,256]{2,1,0:T(8,128)(2,1)} %get-tuple-element.52.refs_11_.refs_13_), channel_id=1, source_target_pairs={{0,1},{1,0},{2,3},{3,2},{4,5},{5,4},{6,7},{7,6},{8,9},{9,8},{10,11... | collective-permute-start | bytes 1572872 | tf_op jit(solution)/shard_map/ppermute | solution.py:275
  103.6 26.9 %collective-permute-start.31 = (bf16[4,256,256]{2,1,0:T(8,128)(2,1)}, bf16[4,256,256]{2,1,0:T(8,128)(2,1)S(1)}, u32[]{:S(2)}, u32[]{:S(2)}) collective-permute-start(bf16[4,256,256]{2,1,0:T(8,128)(2,1)} %get-tuple-element.51.refs_10_.refs_12_), channel_id=1, source_target_pairs={{0,3},{1,2},{2,1},{3,0},{4,7},{5,6},{6,5},{7,4},{8,11},{9,10},{10,... | collective-permute-start | bytes 1572872 | tf_op jit(solution)/shard_map/ppermute | solution.py:275
  116.6 15.2 %collective-permute-start.32 = (bf16[4,256,256]{2,1,0:T(8,128)(2,1)}, bf16[4,256,256]{2,1,0:T(8,128)(2,1)S(1)}, u32[]{:S(2)}, u32[]{:S(2)}) collective-permute-start(bf16[4,256,256]{2,1,0:T(8,128)(2,1)} %get-tuple-element.52.refs_11_.refs_13_), channel_id=1, source_target_pairs={{0,3},{1,2},{2,1},{3,0},{4,7},{5,6},{6,5},{7,4},{8,11},{9,10},{10,... | collective-permute-start | bytes 1572872 | tf_op jit(solution)/shard_map/ppermute | solution.py:275
  127.0 15.0 %collective-permute-start.33 = (bf16[4,256,256]{2,1,0:T(8,128)(2,1)}, bf16[4,256,256]{2,1,0:T(8,128)(2,1)S(1)}, u32[]{:S(2)}, u32[]{:S(2)}) collective-permute-start(bf16[4,256,256]{2,1,0:T(8,128)(2,1)} %get-tuple-element.51.refs_10_.refs_12_), channel_id=1, source_target_pairs={{0,5},{1,4},{2,7},{3,6},{4,1},{5,0},{6,3},{7,2},{8,13},{9,12},{10,... | collective-permute-start | bytes 1572872 | tf_op jit(solution)/shard_map/ppermute | solution.py:275
  128.1 25.1 %collective-permute-start.34 = (bf16[4,256,256]{2,1,0:T(8,128)(2,1)}, bf16[4,256,256]{2,1,0:T(8,128)(2,1)S(1)}, u32[]{:S(2)}, u32[]{:S(2)}) collective-permute-start(bf16[4,256,256]{2,1,0:T(8,128)(2,1)} %get-tuple-element.52.refs_11_.refs_13_), channel_id=1, source_target_pairs={{0,5},{1,4},{2,7},{3,6},{4,1},{5,0},{6,3},{7,2},{8,13},{9,12},{10,... | collective-permute-start | bytes 1572872 | tf_op jit(solution)/shard_map/ppermute | solution.py:275
  129.3 35.1 %collective-permute-start.35 = (bf16[4,256,256]{2,1,0:T(8,128)(2,1)}, bf16[4,256,256]{2,1,0:T(8,128)(2,1)S(1)}, u32[]{:S(2)}, u32[]{:S(2)}) collective-permute-start(bf16[4,256,256]{2,1,0:T(8,128)(2,1)} %get-tuple-element.51.refs_10_.refs_12_), channel_id=1, source_target_pairs={{0,7},{1,6},{2,5},{3,4},{4,3},{5,2},{6,1},{7,0},{8,15},{9,14},{10,... | collective-permute-start | bytes 1572872 | tf_op jit(solution)/shard_map/ppermute | solution.py:275
  130.5 35.3 %collective-permute-start.14 = (bf16[2048,128]{1,0:T(8,128)(2,1)S(1)}, bf16[2048,128]{1,0:T(8,128)(2,1)S(1)}, u32[]{:S(2)}, u32[]{:S(2)}) collective-permute-start(bf16[2048,128]{1,0:T(8,128)(2,1)S(1)} %collective-permute-done.12.refs_2_.refs_0_), channel_id=1, source_target_pairs={{0,8},{1,9},{2,10},{3,11},{4,12},{5,13},{6,14},{7,15},{8,16},{9,17... | collective-permute-start | bytes 1572872 | tf_op jit(solution)/shard_map/ppermute | solution.py:278
  131.8 35.3 %collective-permute-start.15 = (bf16[2048,128]{1,0:T(8,128)(2,1)S(1)}, bf16[2048,128]{1,0:T(8,128)(2,1)S(1)}, u32[]{:S(2)}, u32[]{:S(2)}) collective-permute-start(bf16[2048,128]{1,0:T(8,128)(2,1)S(1)} %collective-permute-done.13.refs_3_.refs_1_), channel_id=1, source_target_pairs={{0,8},{1,9},{2,10},{3,11},{4,12},{5,13},{6,14},{7,15},{8,16},{9,17... | collective-permute-start | bytes 1572872 | tf_op jit(solution)/shard_map/ppermute | solution.py:278
  142.0 26.4 %collective-permute-start.19 = (bf16[2048,128]{1,0:T(8,128)(2,1)S(1)}, bf16[2048,128]{1,0:T(8,128)(2,1)S(1)}, u32[]{:S(2)}, u32[]{:S(2)}) collective-permute-start(bf16[2048,128]{1,0:T(8,128)(2,1)S(1)} %collective-permute-done.17.refs_7_), channel_id=1, source_target_pairs={{8,0},{9,1},{10,2},{11,3},{12,4},{13,5},{14,6},{15,7},{16,8},{17,9... | collective-permute-start | bytes 1572872 | tf_op jit(solution)/shard_map/ppermute | solution.py:281
  153.2 21.4 %collective-permute-start.36 = (bf16[4,256,256]{2,1,0:T(8,128)(2,1)}, bf16[4,256,256]{2,1,0:T(8,128)(2,1)S(1)}, u32[]{:S(2)}, u32[]{:S(2)}) collective-permute-start(bf16[4,256,256]{2,1,0:T(8,128)(2,1)} %get-tuple-element.52.refs_11_.refs_13_), channel_id=1, source_target_pairs={{0,7},{1,6},{2,5},{3,4},{4,3},{5,2},{6,1},{7,0},{8,15},{9,14},{10,... | collective-permute-start | bytes 1572872 | tf_op jit(solution)/shard_map/ppermute | solution.py:275
  164.5 21.7 %copy-start.5 = (bf16[4,256,256]{2,1,0:T(8,128)(2,1)}, bf16[4,256,256]{2,1,0:T(8,128)(2,1)S(1)}, u32[]{:S(2)}) copy-start(bf16[4,256,256]{2,1,0:T(8,128)(2,1)S(1)} %collective-permute-done.35.refs_24_.refs_26_) | copy-start | bytes 1572868
  164.5 34.9 %collective-permute-start.46 = (bf16[2048,128]{1,0:T(8,128)(2,1)S(1)}, bf16[2048,128]{1,0:T(8,128)(2,1)S(1)}, u32[]{:S(2)}, u32[]{:S(2)}) collective-permute-start(bf16[2048,128]{1,0:T(8,128)(2,1)S(1)} %collective-permute-done.18.refs_8_), channel_id=1, source_target_pairs={{8,0},{9,1},{10,2},{11,3},{12,4},{13,5},{14,6},{15,7},{16,8},{17,9... | collective-permute-start | bytes 1572872 | tf_op jit(solution)/shard_map/ppermute | solution.py:281
  165.8 33.8 %collective-permute-start.44 = (bf16[2048,128]{1,0:T(8,128)(2,1)S(1)}, bf16[2048,128]{1,0:T(8,128)(2,1)S(1)}, u32[]{:S(2)}, u32[]{:S(2)}) collective-permute-start(bf16[2048,128]{1,0:T(8,128)(2,1)S(1)} %collective-permute-done.14.refs_4_.refs_2_), channel_id=1, source_target_pairs={{0,8},{1,9},{2,10},{3,11},{4,12},{5,13},{6,14},{7,15},{8,16},{9,17... | collective-permute-start | bytes 1572872 | tf_op jit(solution)/shard_map/ppermute | solution.py:278
  167.1 33.9 %collective-permute-start.45 = (bf16[2048,128]{1,0:T(8,128)(2,1)S(1)}, bf16[2048,128]{1,0:T(8,128)(2,1)S(1)}, u32[]{:S(2)}, u32[]{:S(2)}) collective-permute-start(bf16[2048,128]{1,0:T(8,128)(2,1)S(1)} %collective-permute-done.15.refs_5_.refs_3_), channel_id=1, source_target_pairs={{0,8},{1,9},{2,10},{3,11},{4,12},{5,13},{6,14},{7,15},{8,16},{9,17... | collective-permute-start | bytes 1572872 | tf_op jit(solution)/shard_map/ppermute | solution.py:278
  168.4 37.5 %collective-permute-start.47 = (bf16[2048,128]{1,0:T(8,128)(2,1)S(1)}, bf16[2048,128]{1,0:T(8,128)(2,1)S(1)}, u32[]{:S(2)}, u32[]{:S(2)}) collective-permute-start(bf16[2048,128]{1,0:T(8,128)(2,1)S(1)} %collective-permute-done.19.refs_9_), channel_id=1, source_target_pairs={{8,0},{9,1},{10,2},{11,3},{12,4},{13,5},{14,6},{15,7},{16,8},{17,9... | collective-permute-start | bytes 1572872 | tf_op jit(solution)/shard_map/ppermute | solution.py:281
  186.8 29.5 %collective-permute-start.37 = (bf16[256,128]{1,0:T(8,128)(2,1)S(1)}, bf16[256,128]{1,0:T(8,128)(2,1)S(1)}, u32[]{:S(2)}, u32[]{:S(2)}) collective-permute-start(bf16[256,128]{1,0:T(8,128)(2,1)S(1)} %get-tuple-element.54), channel_id=1, source_target_pairs={{0,2},{1,3},{2,0},{3,1},{4,6},{5,7},{6,4},{7,5},{8,10},{9,11},{10,... | collective-permute-start | bytes 196616 | tf_op jit(solution)/shard_map/ppermute | solution.py:275
  199.3 19.2 %collective-permute-start.38 = (bf16[256,128]{1,0:T(8,128)(2,1)S(1)}, bf16[256,128]{1,0:T(8,128)(2,1)S(1)}, u32[]{:S(2)}, u32[]{:S(2)}) collective-permute-start(bf16[256,128]{1,0:T(8,128)(2,1)S(1)} %get-tuple-element.55), channel_id=1, source_target_pairs={{0,4},{1,5},{2,6},{3,7},{4,0},{5,1},{6,2},{7,3},{8,12},{9,13},{10,... | collective-permute-start | bytes 196616 | tf_op jit(solution)/shard_map/ppermute | solution.py:275
  199.6 19.7 %collective-permute-start.39 = (bf16[256,128]{1,0:T(8,128)(2,1)S(1)}, bf16[256,128]{1,0:T(8,128)(2,1)S(1)}, u32[]{:S(2)}, u32[]{:S(2)}) collective-permute-start(bf16[256,128]{1,0:T(8,128)(2,1)S(1)} %get-tuple-element.56), channel_id=1, source_target_pairs={{0,6},{1,7},{2,4},{3,5},{4,2},{5,3},{6,0},{7,1},{8,14},{9,15},{10,... | collective-permute-start | bytes 196616 | tf_op jit(solution)/shard_map/ppermute | solution.py:275
  201.0 18.5 %collective-permute-start.40 = (bf16[256,128]{1,0:T(8,128)(2,1)S(1)}, bf16[256,128]{1,0:T(8,128)(2,1)S(1)}, u32[]{:S(2)}, u32[]{:S(2)}) collective-permute-start(bf16[256,128]{1,0:T(8,128)(2,1)S(1)} %get-tuple-element.57), channel_id=1, source_target_pairs={{0,1},{1,0},{2,3},{3,2},{4,5},{5,4},{6,7},{7,6},{8,9},{9,8},{10,11... | collective-permute-start | bytes 196616 | tf_op jit(solution)/shard_map/ppermute | solution.py:275
  205.9 14.7 %collective-permute-start.41 = (bf16[256,128]{1,0:T(8,128)(2,1)S(1)}, bf16[256,128]{1,0:T(8,128)(2,1)S(1)}, u32[]{:S(2)}, u32[]{:S(2)}) collective-permute-start(bf16[256,128]{1,0:T(8,128)(2,1)S(1)} %get-tuple-element.58), channel_id=1, source_target_pairs={{0,3},{1,2},{2,1},{3,0},{4,7},{5,6},{6,5},{7,4},{8,11},{9,10},{10,... | collective-permute-start | bytes 196616 | tf_op jit(solution)/shard_map/ppermute | solution.py:275
  216.3 14.9 %copy-start.7 = (bf16[256,128]{1,0:T(8,128)(2,1)}, bf16[256,128]{1,0:T(8,128)(2,1)S(1)}, u32[]{:S(2)}) copy-start(bf16[256,128]{1,0:T(8,128)(2,1)S(1)} %collective-permute-done.37.refs_1_) | copy-start | bytes 196612
  216.3 5.2 %collective-permute-start.42 = (bf16[256,128]{1,0:T(8,128)(2,1)S(1)}, bf16[256,128]{1,0:T(8,128)(2,1)S(1)}, u32[]{:S(2)}, u32[]{:S(2)}) collective-permute-start(bf16[256,128]{1,0:T(8,128)(2,1)S(1)} %get-tuple-element.59), channel_id=1, source_target_pairs={{0,5},{1,4},{2,7},{3,6},{4,1},{5,0},{6,3},{7,2},{8,13},{9,12},{10,... | collective-permute-start | bytes 196616 | tf_op jit(solution)/shard_map/ppermute | solution.py:275
  218.6 12.6 %copy-start.8 = (bf16[256,128]{1,0:T(8,128)(2,1)}, bf16[256,128]{1,0:T(8,128)(2,1)S(1)}, u32[]{:S(2)}) copy-start(bf16[256,128]{1,0:T(8,128)(2,1)S(1)} %collective-permute-done.38.refs_2_) | copy-start | bytes 196612
  218.6 5.5 %collective-permute-start.43 = (bf16[256,128]{1,0:T(8,128)(2,1)S(1)}, bf16[256,128]{1,0:T(8,128)(2,1)S(1)}, u32[]{:S(2)}, u32[]{:S(2)}) collective-permute-start(bf16[256,128]{1,0:T(8,128)(2,1)S(1)} %get-tuple-element.60), channel_id=1, source_target_pairs={{0,7},{1,6},{2,5},{3,4},{4,3},{5,2},{6,1},{7,0},{8,15},{9,14},{10,... | collective-permute-start | bytes 196616 | tf_op jit(solution)/shard_map/ppermute | solution.py:275
  219.3 11.9 %copy-start.9 = (bf16[256,128]{1,0:T(8,128)(2,1)}, bf16[256,128]{1,0:T(8,128)(2,1)S(1)}, u32[]{:S(2)}) copy-start(bf16[256,128]{1,0:T(8,128)(2,1)S(1)} %collective-permute-done.39.refs_3_) | copy-start | bytes 196612
  219.3 5.3 %collective-permute-start.48 = (bf16[256,128]{1,0:T(8,128)(2,1)S(1)}, bf16[256,128]{1,0:T(8,128)(2,1)S(1)}, u32[]{:S(2)}, u32[]{:S(2)}) collective-permute-start(bf16[256,128]{1,0:T(8,128)(2,1)S(1)} %get-tuple-element.62), channel_id=1, source_target_pairs={{0,2},{1,3},{2,0},{3,1},{4,6},{5,7},{6,4},{7,5},{8,10},{9,11},{10,... | collective-permute-start | bytes 196616 | tf_op jit(solution)/shard_map/ppermute | solution.py:275
  219.5 7.0 %collective-permute-start.49 = (bf16[256,128]{1,0:T(8,128)(2,1)S(1)}, bf16[256,128]{1,0:T(8,128)(2,1)S(1)}, u32[]{:S(2)}, u32[]{:S(2)}) collective-permute-start(bf16[256,128]{1,0:T(8,128)(2,1)S(1)} %get-tuple-element.63), channel_id=1, source_target_pairs={{0,4},{1,5},{2,6},{3,7},{4,0},{5,1},{6,2},{7,3},{8,12},{9,13},{10,... | collective-permute-start | bytes 196616 | tf_op jit(solution)/shard_map/ppermute | solution.py:275
  220.6 6.7 %collective-permute-start.50 = (bf16[256,128]{1,0:T(8,128)(2,1)S(1)}, bf16[256,128]{1,0:T(8,128)(2,1)S(1)}, u32[]{:S(2)}, u32[]{:S(2)}) collective-permute-start(bf16[256,128]{1,0:T(8,128)(2,1)S(1)} %get-tuple-element.64), channel_id=1, source_target_pairs={{0,6},{1,7},{2,4},{3,5},{4,2},{5,3},{6,0},{7,1},{8,14},{9,15},{10,... | collective-permute-start | bytes 196616 | tf_op jit(solution)/shard_map/ppermute | solution.py:275
  221.4 5.8 %collective-permute-start.51 = (bf16[256,128]{1,0:T(8,128)(2,1)S(1)}, bf16[256,128]{1,0:T(8,128)(2,1)S(1)}, u32[]{:S(2)}, u32[]{:S(2)}) collective-permute-start(bf16[256,128]{1,0:T(8,128)(2,1)S(1)} %get-tuple-element.65), channel_id=1, source_target_pairs={{0,1},{1,0},{2,3},{3,2},{4,5},{5,4},{6,7},{7,6},{8,9},{9,8},{10,11... | collective-permute-start | bytes 196616 | tf_op jit(solution)/shard_map/ppermute | solution.py:275
  224.1 7.1 %collective-permute-start.52 = (bf16[256,128]{1,0:T(8,128)(2,1)S(1)}, bf16[256,128]{1,0:T(8,128)(2,1)S(1)}, u32[]{:S(2)}, u32[]{:S(2)}) collective-permute-start(bf16[256,128]{1,0:T(8,128)(2,1)S(1)} %get-tuple-element.66), channel_id=1, source_target_pairs={{0,3},{1,2},{2,1},{3,0},{4,7},{5,6},{6,5},{7,4},{8,11},{9,10},{10,... | collective-permute-start | bytes 196616 | tf_op jit(solution)/shard_map/ppermute | solution.py:275
  224.6 6.6 %collective-permute-start.53 = (bf16[256,128]{1,0:T(8,128)(2,1)S(1)}, bf16[256,128]{1,0:T(8,128)(2,1)S(1)}, u32[]{:S(2)}, u32[]{:S(2)}) collective-permute-start(bf16[256,128]{1,0:T(8,128)(2,1)S(1)} %get-tuple-element.67), channel_id=1, source_target_pairs={{0,5},{1,4},{2,7},{3,6},{4,1},{5,0},{6,3},{7,2},{8,13},{9,12},{10,... | collective-permute-start | bytes 196616 | tf_op jit(solution)/shard_map/ppermute | solution.py:275
  226.4 4.7 %collective-permute-start.54 = (bf16[256,128]{1,0:T(8,128)(2,1)S(1)}, bf16[256,128]{1,0:T(8,128)(2,1)S(1)}, u32[]{:S(2)}, u32[]{:S(2)}) collective-permute-start(bf16[256,128]{1,0:T(8,128)(2,1)S(1)} %get-tuple-element.68), channel_id=1, source_target_pairs={{0,7},{1,6},{2,5},{3,4},{4,3},{5,2},{6,1},{7,0},{8,15},{9,14},{10,... | collective-permute-start | bytes 196616 | tf_op jit(solution)/shard_map/ppermute | solution.py:275
  (27 other events, 122.8 us)

commit v2 on v0

v2 whole, which is shorter than its diff:
```python
import functools
import math

import jax
import jax.numpy as jnp
from jax import lax
from jax.experimental import pallas as pl
from jax.experimental.pallas import tpu as pltpu
from jax.sharding import PartitionSpec as P

HEAD = 128
NEGATIVE = -1e30
AXES = ("dense", "attn")
ANY = pl.BlockSpec(memory_space=pl.ANY)
SMEM = pl.BlockSpec(memory_space=pltpu.SMEM)
VMEM = pl.BlockSpec(memory_space=pltpu.VMEM)
LIGHT = pl.CostEstimate(flops=0, bytes_accessed=0, transcendentals=0)


def xor(a, b):
    return lax.bitwise_xor(a, jnp.int32(b))


def params(mib):
    return pltpu.CompilerParams(vmem_limit_bytes=mib * 2**20)


def place_in(group):
    device = lax.axis_index("dense").astype(jnp.int32)
    return device // group, lax.rem(device, jnp.int32(group)), lax.axis_index("attn").astype(jnp.int32)


def turn_of(z, y, planes, attn):
    return lax.bitwise_xor(z // (planes // attn), y)


def split_kv_kernel(group, *refs):
    g = place_in(group)[1]
    for core in range(2):
        k_ref, v_ref = refs[2 * core : 2 * core + 2]
        for o, out in enumerate(refs[4:]):
            at = pl.ds(pl.multiple_of(xor(g, 2 * o) * HEAD, HEAD), HEAD)
            out[core, :, :HEAD] = k_ref[:, at]
            out[core, :, HEAD:] = v_ref[:, at]


def split_q_kernel(group, *refs):
    g = place_in(group)[1]
    width = refs[2].shape[2]
    for core in range(2):
        for o, out in enumerate(refs[2:]):
            out[core] = refs[core][:, pl.ds(pl.multiple_of(xor(g, 2 * o) * width, width), width)]


def split_w_kernel(group, w_ref, *outs):
    g, y = place_in(group)[1:]
    rows, cols = outs[0].shape
    width = rows // group
    for m in range(len(outs)):
        at = pl.ds(pl.multiple_of(xor(y, m) * cols, cols), cols)
        for j in range(group):
            outs[m][j * width : (j + 1) * width, :] = w_ref[
                pl.ds(pl.multiple_of(xor(g, j) * width, width), width), at
            ]


def attention_kernel(group, heads, back, pairs, carried, final, seg_ref, segrow_ref, *refs):
    n_kv, n_q = len(back) * group, len(pairs) * 2
    refs = list(refs)
    take = lambda count: [refs.pop(0) for _ in range(count)]
    q_refs, kv_refs = take(len(pairs)), take(n_kv // 2)
    state_refs = [take(3) for _ in pairs] if carried else None
    out_refs = take(1 if final else 3)
    q_s, k_s, v_s, s_s, m_s, l_s, acc_s, seg_s, sem = refs
    n = segrow_ref.shape[1]
    rows = heads * n
    lanes = n // HEAD
    copies = []
    for k in range(n_q):
        for h in range(heads):
            q_part = q_refs[k // 2].at[k % 2, :, pl.ds(h * HEAD, HEAD)]
            copies.append((q_part, q_s.at[k, pl.ds(h * n, n), :]))
    for i in range(n_kv):
        kv = kv_refs[i // 2].at[i % 2]
        copies.append((kv.at[:, pl.ds(0, HEAD)], k_s.at[i]))
        copies.append((kv.at[:, pl.ds(HEAD, HEAD)], v_s.at[i]))
    copies = [pltpu.make_async_copy(a, b, sem.at[i]) for i, (a, b) in enumerate(copies)]
    for c in copies:
        c.start()
    for c in copies:
        c.wait()

    plane, g, _ = place_in(group)
    scale = math.log2(math.e) / math.sqrt(HEAD)

    def one_query_piece(pair, core, carry):
        at = 2 * pair + core
        given = [ref.at[core] for ref in state_refs[pair]] if carried else None
        qp = plane * group + lax.bitwise_xor(g, 2 * pairs[pair] + core)
        q_first, q_last = seg_ref[qp * n], seg_ref[qp * n + n - 1]

        def state(i):
            kp = (plane - back[0] - i // group) * group + lax.bitwise_xor(g, lax.rem(i, group))
            safe = jnp.maximum(kp, 0)
            active = (kp >= 0) & (kp <= qp) & (seg_ref[safe * n + n - 1] >= q_first)
            whole = (kp < qp) & (seg_ref[safe * n] == q_last)
            return kp, safe, active, whole

        def parts_of(i):
            return [s_s[i, :, t * HEAD : (t + 1) * HEAD] for t in range(lanes)]

        def score(i, carry):
            kp, safe, active, whole = state(i)

            @pl.when(active)
            def _():
                s_s[i] = lax.dot_general(
                    q_s[at], k_s[i], (((1,), (1,)), ((), ())), preferred_element_type=jnp.float32
                )

            @pl.when(active & whole)
            def _():
                m_s[...] = functools.reduce(jnp.maximum, parts_of(i), m_s[...])

            @pl.when(active & jnp.logical_not(whole))
            def _():
                seg_k = segrow_ref[pl.ds(safe, 1), :].astype(jnp.float32)
                ahead = lax.broadcasted_iota(jnp.int32, (n, HEAD), 1) - lax.broadcasted_iota(
                    jnp.int32, (n, HEAD), 0
                )
                for t in range(lanes):
                    lane = slice(t * HEAD, (t + 1) * HEAD)
                    seen = (ahead + t * HEAD <= (qp - kp) * n) & (seg_s[...] == seg_k[:, lane])
                    for h in range(heads):
                        row = slice(h * n, (h + 1) * n)
                        part = jnp.where(seen, s_s[i, row, lane], NEGATIVE)
                        s_s[i, row, lane] = part
                        m_s[row] = jnp.maximum(m_s[row], part)

            return carry

        def mix(i, carry):
            @pl.when(state(i)[2])
            def _():
                top = m_s[...]
                parts = [jnp.exp2((part - top) * scale) for part in parts_of(i)]
                l_s[...] += functools.reduce(jnp.add, parts)
                weights = jnp.concatenate([p.astype(jnp.bfloat16) for p in parts], axis=1)
                acc_s[...] += jnp.dot(weights, v_s[i], preferred_element_type=jnp.float32)

            return carry

        def both_passes():
            row = segrow_ref[pl.ds(qp, 1), :].astype(jnp.float32)
            seg_s[...] = jnp.broadcast_to(row, (HEAD, n)).T
            if carried:
                m_s[...] = given[0][...]
            else:
                m_s[...] = jnp.full(m_s.shape, NEGATIVE, jnp.float32)
            lax.fori_loop(0, n_kv, score, 0)
            top = jnp.broadcast_to(jnp.max(m_s[...], axis=1, keepdims=True), (rows, HEAD))
            if carried:
                shrink = jnp.exp2((given[0][...] - top) * scale)
                l_s[...] = given[1][...] * shrink
                acc_s[...] = given[2][...] * shrink
            else:
                l_s[...] = jnp.zeros(l_s.shape, jnp.float32)
                acc_s[...] = jnp.zeros(acc_s.shape, jnp.float32)
            m_s[...] = top
            lax.fori_loop(0, n_kv, mix, 0)

        def give(lane_sums, summed):
            for h in range(heads):
                row = slice(h * n, (h + 1) * n)
                total = jnp.sum(lane_sums[row], axis=1, keepdims=True)
                out_refs[0][at, :, h * HEAD : (h + 1) * HEAD] = (summed[row] / total).astype(jnp.bfloat16)

        if carried:
            needed = lax.fori_loop(
                0, n_kv, lambda i, seen: seen | state(i)[2].astype(jnp.int32), jnp.int32(0)
            )

            @pl.when(needed > 0)
            def _():
                both_passes()
                give(l_s[...], acc_s[...])

            @pl.when(needed == 0)
            def _():
                give(given[1][...], given[2][...])
        else:
            both_passes()
            if final:
                give(l_s[...], acc_s[...])
            else:
                for out_ref, value in zip(out_refs, (m_s, l_s, acc_s)):
                    out_ref[at] = value[...]
        return carry

    for pair in range(len(pairs)):
        lax.fori_loop(0, 2, functools.partial(one_query_piece, pair), 0)


def attention(group, heads, back, pairs, segments, q, kv, carried=None, final=True):
    n, width = q[0].shape[1:]
    rows, n_kv, n_q = heads * n, 2 * len(kv), 2 * len(pairs)
    state = jax.ShapeDtypeStruct((n_q, rows, HEAD), jnp.float32)
    if final:
        out_shape = [jax.ShapeDtypeStruct((n_q, n, width), jnp.bfloat16)]
    else:
        out_shape = [state] * 3
    carried = list(carried or ())
    found = pl.pallas_call(
        functools.partial(attention_kernel, group, heads, back, pairs, bool(carried), final),
        out_shape=out_shape,
        in_specs=[SMEM, VMEM] + [ANY] * (len(q) + len(kv)) + [VMEM] * len(carried),
        out_specs=[VMEM] * len(out_shape),
        scratch_shapes=[
            pltpu.VMEM((n_q, rows, HEAD), jnp.bfloat16),
            pltpu.VMEM((n_kv, n, HEAD), jnp.bfloat16),
            pltpu.VMEM((n_kv, n, HEAD), jnp.bfloat16),
            pltpu.VMEM((n_kv, rows, n), jnp.float32),
            pltpu.VMEM((rows, HEAD), jnp.float32),
            pltpu.VMEM((rows, HEAD), jnp.float32),
            pltpu.VMEM((rows, HEAD), jnp.float32),
            pltpu.VMEM((n, HEAD), jnp.float32),
            pltpu.SemaphoreType.DMA((n_q * heads + 2 * n_kv,)),
        ],
        compiler_params=params(28),
        cost_estimate=LIGHT,
        name="attention",
    )(segments, segments.reshape(-1, n), *q, *kv, *carried)
    return found[0] if final else found


def project_kernel(group, attn, planes, *refs):
    refs = list(refs)
    take = lambda count: [refs.pop(0) for _ in range(count)]
    w_refs, a_refs, out_refs = take(planes), take(group * attn), take(group * attn)
    a_s, w_s, a_sem, w_sem = refs
    z, _, y = place_in(group)
    n, width = a_refs[0].shape[1:]
    cols = w_refs[0].shape[1]
    rounds = planes // attn
    aligned = cols % HEAD == 0

    def a_copies(k):
        return [
            pltpu.make_async_copy(
                a_refs[i].at[(i % group) ^ k], a_s.at[k, :, pl.ds(i * width, width)], a_sem.at[k]
            )
            for i in range(attn * group)
        ]

    w_copies = []
    for turn in range(attn):
        to = xor(turn_of(z, y, planes, attn), turn)
        for r in range(rounds):
            place = to * rounds + r
            into = w_s.at[:, pl.ds(pl.multiple_of(place * cols, cols), cols)] if aligned else w_s.at[place]
            w_copies.append(pltpu.make_async_copy(w_refs[r + turn * rounds], into, w_sem))

    for copy in a_copies(0) + w_copies:
        copy.start()
    for k in range(1, group):
        for copy in a_copies(k):
            copy.start()
    for copy in w_copies:
        copy.wait()
    for k in range(group):
        for copy in a_copies(k):
            copy.wait()
        if aligned:
            found = jnp.dot(a_s[k], w_s[...], preferred_element_type=jnp.float32).astype(jnp.bfloat16)
            for to in range(attn):
                out_refs[to * group + k][...] = found[:, to * rounds * cols : (to + 1) * rounds * cols]
        else:
            for to in range(attn):
                for r in range(rounds):
                    out_refs[to * group + k][:, r * cols : (r + 1) * cols] = jnp.dot(
                        a_s[k], w_s[to * rounds + r], preferred_element_type=jnp.float32
                    ).astype(jnp.bfloat16)


def column_of(group, attn, planes, r, m, k, cols):
    z, g, y = place_in(group)
    rounds = planes // attn
    return ((xor(lax.rem(z, jnp.int32(rounds)), r) * group + xor(g, k)) * attn + xor(y, m)) * cols


def place_kernel(group, attn, planes, *refs):
    out_ref = refs[-1]
    rounds = planes // attn
    cols = refs[0].shape[1] // rounds
    for r in range(rounds):
        for m in range(attn):
            for k in range(group):
                at = pl.multiple_of(column_of(group, attn, planes, r, m, k, cols), cols)
                out_ref[:, pl.ds(at, cols)] = refs[m * group + k][:, r * cols : (r + 1) * cols]


def shards(dense, attn, queries, keys, values, segments, out_weight):
    n = queries.shape[0]
    tokens = segments.shape[0]
    group = keys.shape[1] // HEAD
    heads = queries.shape[1] // HEAD // group
    width = heads * HEAD
    planes = dense // group
    rounds = planes // attn
    hops = min(-(-(tokens // 2 - 1) // (n * group)), planes - 1)
    cols = out_weight.shape[1] // attn
    bf16 = lambda *shape: jax.ShapeDtypeStruct(shape, jnp.bfloat16)

    def number(z, g, y):
        return (z * group + g) * attn + y

    def pairs(move):
        found = []
        for z in range(planes):
            for g in range(group):
                for y in range(attn):
                    to = move(z, g, y)
                    if 0 <= to[0] < planes:
                        found.append((number(z, g, y), number(*to)))
        return found

    def across(array, j, m):
        with jax.named_scope(f"across_{j}_{m}"):
            return lax.ppermute(array, AXES, pairs(lambda z, g, y: (z, g ^ j, y ^ m)))

    def up(array, j=0):
        with jax.named_scope(f"up_{j}"):
            return lax.ppermute(array, AXES, pairs(lambda z, g, y: (z + 1, g ^ j, y)))

    def between(array, i):
        with jax.named_scope(f"between_{i}"):
            return lax.ppermute(array, AXES, pairs(lambda z, g, y: (z ^ i, g, y)))

    def with_other_core(arrays):
        return [which for array in arrays for which in (array, across(array, 1, 0))]

    after = lambda array, *others: lax.optimization_barrier((array, *others))

    pair = [bf16(2, n, 2 * HEAD)] * (group // 2)
    kv = pl.pallas_call(
        functools.partial(split_kv_kernel, group),
        out_shape=pair,
        in_specs=[VMEM] * 4,
        out_specs=[VMEM] * (group // 2),
        name="split_kv",
    )(keys, values, across(keys, 1, 0), across(values, 1, 0))
    links = [[kv[0]] + [across(kv[o], 2 * o, 0) for o in range(1, group // 2)]]
    links.append([up(kv[o], 2 * o) for o in range(group // 2)])

    queries, _ = after(queries, kv[0])
    q = pl.pallas_call(
        functools.partial(split_q_kernel, group),
        out_shape=[bf16(2, n, width)] * (group // 2),
        in_specs=[VMEM] * 2,
        out_specs=[VMEM] * (group // 2),
        name="split_q",
    )(queries, across(queries, 1, 0))
    out_weight, _ = after(out_weight, q[0])
    q = [q[0]] + [across(q[o], 2 * o, 0) for o in range(1, group // 2)]

    if cols % HEAD == 0:
        own = pl.pallas_call(
            functools.partial(split_w_kernel, group),
            out_shape=[bf16(out_weight.shape[0], cols)] * attn,
            in_specs=[VMEM],
            out_specs=[VMEM] * attn,
            name="split_w",
        )(out_weight)
    else:
        _, g, y = place_in(group)
        ordered = jnp.concatenate(
            [lax.dynamic_slice_in_dim(out_weight, xor(g, j) * width, width, 0) for j in range(group)]
        )
        own = [lax.dynamic_slice_in_dim(ordered, xor(y, m) * cols, cols, 1) for m in range(attn)]
    own = jnp.concatenate([own[0]] + [across(own[m], 0, m) for m in range(1, attn)])
    own, *links[1] = after(own, *links[1])
    for _ in range(1, hops):
        links.append([up(pair) for pair in links[-1]])
    blocks = {0: own}
    stride = planes // 2
    while stride:
        for i in list(blocks):
            blocks[i + stride] = between(blocks[i], stride)
        if stride == planes // 2:
            blocks[0], *links[-1] = after(own, *links[-1])
        stride //= 2

    near = [pair for pairs_of in links[:hops] for pair in pairs_of]
    carried = []
    for o in range(group // 2):
        carried += attention(group, heads, range(hops), [o], segments, [q[o]], near, final=False)
    attended = attention(
        group, heads, range(hops, hops + 1), range(group // 2), segments, q, links[hops], carried
    )

    everything = []
    for m in range(attn):
        everything += with_other_core(
            [attended if o == m == 0 else across(attended, 2 * o, m) for o in range(group // 2)]
        )

    w_shape = (attn * group * width, planes * cols) if cols % HEAD == 0 else (planes, attn * group * width, cols)
    found = pl.pallas_call(
        functools.partial(project_kernel, group, attn, planes),
        out_shape=[bf16(n, rounds * cols)] * (attn * group),
        in_specs=[ANY] * (planes + group * attn),
        out_specs=[VMEM] * (attn * group),
        scratch_shapes=[
            pltpu.VMEM((group, n, attn * group * width), jnp.bfloat16),
            pltpu.VMEM(w_shape, jnp.bfloat16),
            pltpu.SemaphoreType.DMA((group,)),
            pltpu.SemaphoreType.DMA,
        ],
        compiler_params=params(28),
        cost_estimate=LIGHT,
        name="project",
    )(*[blocks[i] for i in range(planes)], *everything)
    placed = []
    for m in range(attn):
        for k in range(group):
            piece = found[m * group + k]
            placed.append(piece if m == k == 0 else across(piece, k, m))

    if cols % HEAD == 0:
        return pl.pallas_call(
            functools.partial(place_kernel, group, attn, planes),
            out_shape=bf16(n, planes * group * cols),
            in_specs=[VMEM] * len(placed),
            out_specs=VMEM,
            name="place",
        )(*placed)
    out = jnp.zeros((n, planes * group * cols), jnp.bfloat16)
    for r in range(rounds):
        for m in range(attn):
            for k in range(group):
                part = placed[m * group + k][:, r * cols : (r + 1) * cols]
                at = column_of(group, attn, planes, r, m, k, cols)
                out = lax.dynamic_update_slice_in_dim(out, part, at, 1)
    return out


def solution(mesh):
    return jax.shard_map(
        functools.partial(shards, mesh.shape["dense"], mesh.shape["attn"]),
        mesh=mesh,
        in_specs=(
            P("dense", "attn"),
            P("dense", "attn"),
            P("dense", "attn"),
            P(),
            P("attn", "dense"),
        ),
        out_specs=P("dense", "attn"),
        check_vma=False,
    )
```

time: 299 us -> 158 us (0.53)
  the two profiles are of different devices: /device:TPU:25 before, /device:TPU:1 now
where the time goes in v2:
time: 158 us; the launch traced here: 159 us
  waiting for transfers between devices  73.7 us (47%)
  starting transfers between devices  47.2 us (30%)
  Pallas kernels  33.1 us (21%)
  local copies, waits for them, and re-layouts  3.39 us (2%)
    ppermute x3, waiting for transfers between devices, between(): return lax.ppermute(array, AXES, pairs(lambda z, g, y: (z ^ i, g, y)))  49.1 us
    ppermute x20, waiting for transfers between devices, across(): return lax.ppermute(array, AXES, pairs(lambda z, g, y: (z, g ^ j, y ^ m)))  23 us
    ppermute x20, starting transfers between devices, across(): return lax.ppermute(array, AXES, pairs(lambda z, g, y: (z, g ^ j, y ^ m)))  21.2 us
    pallas_call x3, Pallas kernels, attention(): pl.pallas_call(functools.partial(attention_kernel, group, heads, back, pa...  17.1 us
    ppermute x4, starting transfers between devices, up(): return lax.ppermute(array, AXES, pairs(lambda z, g, y: (z + 1, g ^ j, y)))  14.4 us
    ppermute x3, starting transfers between devices, between(): return lax.ppermute(array, AXES, pairs(lambda z, g, y: (z ^ i, g, y)))  11.6 us
    pallas_call x1, Pallas kernels, shards(): pl.pallas_call(functools.partial(project_kernel, group, attn, planes), ou...  6.39 us
    unnamed x30, local copies, waits for them, and re-layouts  3.39 us
  transfers between devices with their start and end apart: 27, of which 12 were waited for; matrix products, arithmetic and copies ran while one was open for 1% of the time, Pallas kernels for 11%

profile of v2, /device:TPU:1, one launch (start us, length us, event | category | flops | bytes accessed | tf_op | source)
XLA Modules:
  0.0 158.8 jit_solution(1361487762938407844)
XLA Ops:
  0.0 0.1 collective-permute-start
  0.1 0.5 collective-permute-start.1
  0.5 1.2 collective-permute-done.refs_2_
  1.8 0.4 collective-permute-done.1.refs_3_
  2.1 0.3 copy-done.6
  2.5 0.7 copy-done.7
  3.2 2.1 %split_kv.1 = (bf16[2,256,256]{2,1,0:T(8,128)(2,1)}, bf16[2,256,256]{2,1,0:T(8,128)(2,1)}) custom-call(bf16[256,512]{1,0:T(8,128)(2,1)} %refs_0_.1, bf16[256,512]{1,0:T(8,128)(2,1)} %refs_1_.1, bf16[256,512]{1,0:T(8,128)(2,1)} %copy-done.6, bf16[256,512]{1,0:T(8,128)(2,1)} %copy-done.7), custom_call_target="tpu_custom_call" | custom-call | tf_op jit(solution)/shard_map/split_kv/pallas_call | solution.py:345
  5.3 0.1 collective-permute-start.2
  5.4 2.5 %collective-permute-done.2.refs_1_ = bf16[256,2048]{1,0:T(8,128)(2,1)S(1)} collective-permute-done((bf16[256,2048]{1,0:T(8,128)(2,1)S(1)}, bf16[256,2048]{1,0:T(8,128)(2,1)S(1)}, u32[]{:S(2)}, u32[]{:S(2)}) %collective-permute-start.2) | collective-permute-done | bytes 1048608 | tf_op jit(solution)/shard_map/across_1_0/ppermute | solution.py:329
  7.9 1.0 copy-done.5
  8.9 2.6 %split_q.1 = (bf16[2,256,512]{2,1,0:T(8,128)(2,1)}, bf16[2,256,512]{2,1,0:T(8,128)(2,1)}) custom-call(bf16[256,2048]{1,0:T(8,128)(2,1)} %refs_0_.2, bf16[256,2048]{1,0:T(8,128)(2,1)} %copy-done.5), custom_call_target="tpu_custom_call" | custom-call | tf_op jit(solution)/shard_map/split_q/pallas_call | solution.py:356
  11.5 2.4 %split_w.1 = (bf16[2048,128]{1,0:T(8,128)(2,1)}, bf16[2048,128]{1,0:T(8,128)(2,1)}) custom-call(bf16[2048,256]{1,0:T(8,128)(2,1)} %w_ref), custom_call_target="tpu_custom_call" | custom-call | tf_op jit(solution)/shard_map/split_w/pallas_call | solution.py:367
  14.0 2.4 %collective-permute-start.3 = (bf16[2048,128]{1,0:T(8,128)(2,1)}, bf16[2048,128]{1,0:T(8,128)(2,1)S(1)}, u32[]{:S(2)}, u32[]{:S(2)}) collective-permute-start(bf16[2048,128]{1,0:T(8,128)(2,1)} %get-tuple-element.38), channel_id=1, source_target_pairs={{0,1},{1,0},{2,3},{3,2},{4,5},{5,4},{6,7},{7,6},{8,9},{9,8},{10,11... | collective-permute-start | bytes 1572872 | tf_op jit(solution)/shard_map/across_0_1/ppermute | solution.py:329
  16.3 1.2 collective-permute-start.12
  17.5 3.2 %collective-permute-start.5 = (bf16[2,256,256]{2,1,0:T(8,128)(2,1)}, bf16[2,256,256]{2,1,0:T(8,128)(2,1)S(1)}, u32[]{:S(2)}, u32[]{:S(2)}) collective-permute-start(bf16[2,256,256]{2,1,0:T(8,128)(2,1)} %get-tuple-element.39), channel_id=1, source_target_pairs={{0,12},{1,13},{2,14},{3,15},{4,8},{5,9},{6,10},{7,11},{8,20},{9,21... | collective-permute-start | bytes 786440 | tf_op jit(solution)/shard_map/up_2/ppermute | solution.py:333
  20.7 3.2 %collective-permute-start.4 = (bf16[2,256,256]{2,1,0:T(8,128)(2,1)S(1)}, bf16[2,256,256]{2,1,0:T(8,128)(2,1)S(1)}, u32[]{:S(2)}, u32[]{:S(2)}) collective-permute-start(bf16[2,256,256]{2,1,0:T(8,128)(2,1)S(1)} %copy-done.1), channel_id=1, source_target_pairs={{0,8},{1,9},{2,10},{3,11},{4,12},{5,13},{6,14},{7,15},{8,16},{9,17... | collective-permute-start | bytes 786440 | tf_op jit(solution)/shard_map/up_0/ppermute | solution.py:333
  23.9 1.3 collective-permute-start.11
  25.2 3.3 %collective-permute-done.3 = bf16[2048,128]{1,0:T(8,128)(2,1)S(1)} collective-permute-done((bf16[2048,128]{1,0:T(8,128)(2,1)}, bf16[2048,128]{1,0:T(8,128)(2,1)S(1)}, u32[]{:S(2)}, u32[]{:S(2)}) %collective-permute-start.3) | collective-permute-done | bytes 524320 | tf_op jit(solution)/shard_map/across_0_1/ppermute | solution.py:329
  28.5 1.2 pad_maximum_fusion.refs_0_
  29.7 0.0 collective-permute-done.5.refs_4_
  29.7 1.6 collective-permute-done.4.refs_3_
  31.3 4.1 %collective-permute-start.6 = (bf16[2,256,256]{2,1,0:T(8,128)(2,1)S(1)}, bf16[2,256,256]{2,1,0:T(8,128)(2,1)S(1)}, u32[]{:S(2)}, u32[]{:S(2)}) collective-permute-start(bf16[2,256,256]{2,1,0:T(8,128)(2,1)S(1)} %collective-permute-done.4.refs_3_), channel_id=1, source_target_pairs={{0,8},{1,9},{2,10},{3,11},{4,12},{5,13},{6,14},{7,15},{8,16},{9,17... | collective-permute-start | bytes 786440 | tf_op jit(solution)/shard_map/up_0/ppermute | solution.py:333
  35.4 3.9 %collective-permute-start.7 = (bf16[2,256,256]{2,1,0:T(8,128)(2,1)S(1)}, bf16[2,256,256]{2,1,0:T(8,128)(2,1)}, u32[]{:S(2)}, u32[]{:S(2)}) collective-permute-start(bf16[2,256,256]{2,1,0:T(8,128)(2,1)S(1)} %collective-permute-done.5.refs_4_), channel_id=1, source_target_pairs={{0,8},{1,9},{2,10},{3,11},{4,12},{5,13},{6,14},{7,15},{8,16},{9,17... | collective-permute-start | bytes 786440 | tf_op jit(solution)/shard_map/up_0/ppermute | solution.py:333
  39.3 0.4 collective-permute-start.9
  39.7 0.0 collective-permute-done.12.refs_2_
  39.7 5.5 %attention.3 = (f32[2,1024,128]{2,1,0:T(8,128)S(1)}, f32[2,1024,128]{2,1,0:T(8,128)S(1)}, f32[2,1024,128]{2,1,0:T(8,128)S(1)}) custom-call(s32[4096]{0:T(1024)S(1)} %copy-done.2, s32[16,256]{1,0:T(8,128)S(1)} %reshape.2.segrow_ref, bf16[2,256,512]{2,1,0:T(8,128)(2,1)S(1)} %copy-done, bf16[2,256,256]{2,1,0:T(8,128)(2,1)S(1)} %copy-done.1, ...), custom_call_target="tpu_custom_call" | custom-call | tf_op jit(solution)/shard_map/attention/pallas_call | solution.py:213
  45.2 0.0 collective-permute-done.11.refs_0_.refs_1_
  45.2 8.3 %attention.4 = (f32[2,1024,128]{2,1,0:T(8,128)S(1)}, f32[2,1024,128]{2,1,0:T(8,128)S(1)}, f32[2,1024,128]{2,1,0:T(8,128)S(1)}) custom-call(s32[4096]{0:T(1024)S(1)} %copy-done.2, s32[16,256]{1,0:T(8,128)S(1)} %reshape.2.segrow_ref, bf16[2,256,512]{2,1,0:T(8,128)(2,1)S(1)} %collective-permute-done.11.refs_0_.refs_1_, bf16[2,256,256]{2,1,0:T(8,128)(2,1)S(1)} %copy-done.1, ...), custom_call_target="tpu_custom_call" | custom-call | tf_op jit(solution)/shard_map/attention/pallas_call | solution.py:213
  53.5 0.0 collective-permute-done.6.refs_2_
  53.5 0.0 collective-permute-done.7.refs_3_
  53.5 11.2 %collective-permute-start.8 = (bf16[4096,128]{1,0:T(8,128)(2,1)S(1)}, bf16[4096,128]{1,0:T(8,128)(2,1)S(1)}, u32[]{:S(2)}, u32[]{:S(2)}) collective-permute-start(bf16[4096,128]{1,0:T(8,128)(2,1)S(1)} %pad_maximum_fusion.refs_0_), channel_id=1, source_target_pairs={{0,8},{1,9},{2,10},{3,11},{4,12},{5,13},{6,14},{7,15},{8,0},{9,1},... | collective-permute-start | bytes 3145736 | tf_op jit(solution)/shard_map/between_1/ppermute | solution.py:337
  64.8 3.3 %attention.5.refs_4_ = bf16[4,256,512]{2,1,0:T(8,128)(2,1)S(1)} custom-call(s32[4096]{0:T(1024)S(1)} %copy-done.2, s32[16,256]{1,0:T(8,128)S(1)} %reshape.2.segrow_ref, bf16[2,256,512]{2,1,0:T(8,128)(2,1)S(1)} %copy-done, bf16[2,256,512]{2,1,0:T(8,128)(2,1)S(1)} %collective-permute-done.11.refs_0_.refs_1_, ...), custom_call_target="tpu_custom_call" | custom-call | tf_op jit(solution)/shard_map/attention/pallas_call | solution.py:213
  68.1 1.2 collective-permute-start.18
  69.3 1.2 collective-permute-start.16
  70.5 0.3 collective-permute-start.14
  70.8 16.7 %collective-permute-done.9.refs_2_ = bf16[4096,128]{1,0:T(8,128)(2,1)S(1)} collective-permute-done((bf16[4096,128]{1,0:T(8,128)(2,1)S(1)}, bf16[4096,128]{1,0:T(8,128)(2,1)S(1)}, u32[]{:S(2)}, u32[]{:S(2)}) %collective-permute-start.9) | collective-permute-done | bytes 1048608 | tf_op jit(solution)/shard_map/between_2/ppermute | solution.py:337
  87.5 0.9 collective-permute-start.13
  88.4 19.2 %collective-permute-done.8.refs_1_ = bf16[4096,128]{1,0:T(8,128)(2,1)S(1)} collective-permute-done((bf16[4096,128]{1,0:T(8,128)(2,1)S(1)}, bf16[4096,128]{1,0:T(8,128)(2,1)S(1)}, u32[]{:S(2)}, u32[]{:S(2)}) %collective-permute-start.8) | collective-permute-done | bytes 1048608 | tf_op jit(solution)/shard_map/between_1/ppermute | solution.py:337
  107.6 0.0 collective-permute-start.10
  107.6 0.0 collective-permute-done.18.refs_10_
  107.6 1.9 %collective-permute-start.19 = (bf16[4,256,512]{2,1,0:T(8,128)(2,1)S(1)}, bf16[4,256,512]{2,1,0:T(8,128)(2,1)S(1)}, u32[]{:S(2)}, u32[]{:S(2)}) collective-permute-start(bf16[4,256,512]{2,1,0:T(8,128)(2,1)S(1)} %collective-permute-done.18.refs_10_), channel_id=1, source_target_pairs={{0,2},{1,3},{2,0},{3,1},{4,6},{5,7},{6,4},{7,5},{8,10},{9,11},{10,... | collective-permute-start | bytes 3145736 | tf_op jit(solution)/shard_map/across_1_0/ppermute | solution.py:329
  109.5 7.1 %collective-permute-done.16.refs_8_ = bf16[4,256,512]{2,1,0:T(8,128)(2,1)S(1)} collective-permute-done((bf16[4,256,512]{2,1,0:T(8,128)(2,1)S(1)}, bf16[4,256,512]{2,1,0:T(8,128)(2,1)S(1)}, u32[]{:S(2)}, u32[]{:S(2)}) %collective-permute-start.16) | collective-permute-done | bytes 1048608 | tf_op jit(solution)/shard_map/across_0_1/ppermute | solution.py:329
  116.6 0.5 collective-permute-start.17
  117.1 0.0 collective-permute-done.14.refs_6_
  117.1 0.0 collective-permute-start.15
  117.1 0.0 collective-permute-done.13.refs_5_
  117.1 13.2 %collective-permute-done.10.refs_3_ = bf16[4096,128]{1,0:T(8,128)(2,1)S(1)} collective-permute-done((bf16[4096,128]{1,0:T(8,128)(2,1)S(1)}, bf16[4096,128]{1,0:T(8,128)(2,1)S(1)}, u32[]{:S(2)}, u32[]{:S(2)}) %collective-permute-start.10) | collective-permute-done | bytes 1048608 | tf_op jit(solution)/shard_map/between_1/ppermute | solution.py:337
  130.4 6.4 %project.1 = (bf16[256,256]{1,0:T(8,128)(2,1)S(1)}, bf16[256,256]{1,0:T(8,128)(2,1)S(1)}, bf16[256,256]{1,0:T(8,128)(2,1)S(1)}, bf16[256,256]{1,0:T(8,128)(2,1)S...) custom-call(bf16[4096,128]{1,0:T(8,128)(2,1)S(1)} %pad_maximum_fusio, ...), custom_call_target="tpu_custom_call" | custom-call | tf_op jit(solution)/shard_map/project/pallas_call | solution.py:408
  136.8 0.6 copy-done.3
  137.4 2.8 %collective-permute-start.20 = (bf16[256,256]{1,0:T(8,128)(2,1)S(1)}, bf16[256,256]{1,0:T(8,128)(2,1)S(1)}, u32[]{:S(2)}, u32[]{:S(2)}) collective-permute-start(bf16[256,256]{1,0:T(8,128)(2,1)S(1)} %get-tuple-element.54), channel_id=1, source_target_pairs={{0,2},{1,3},{2,0},{3,1},{4,6},{5,7},{6,4},{7,5},{8,10},{9,11},{10,... | collective-permute-start | bytes 393224 | tf_op jit(solution)/shard_map/across_1_0/ppermute | solution.py:329
  140.2 1.2 collective-permute-start.21
  141.4 0.5 collective-permute-start.22
  141.8 0.2 collective-permute-start.23
  142.1 1.6 %collective-permute-start.24 = (bf16[256,256]{1,0:T(8,128)(2,1)S(1)}, bf16[256,256]{1,0:T(8,128)(2,1)S(1)}, u32[]{:S(2)}, u32[]{:S(2)}) collective-permute-start(bf16[256,256]{1,0:T(8,128)(2,1)S(1)} %get-tuple-element.58), channel_id=1, source_target_pairs={{0,3},{1,2},{2,1},{3,0},{4,7},{5,6},{6,5},{7,4},{8,11},{9,10},{10,... | collective-permute-start | bytes 393224 | tf_op jit(solution)/shard_map/across_1_1/ppermute | solution.py:329
  143.7 1.1 collective-permute-start.25
  144.9 0.5 collective-permute-done.21.refs_2_
  145.3 2.2 %collective-permute-start.26 = (bf16[256,256]{1,0:T(8,128)(2,1)S(1)}, bf16[256,256]{1,0:T(8,128)(2,1)S(1)}, u32[]{:S(2)}, u32[]{:S(2)}) collective-permute-start(bf16[256,256]{1,0:T(8,128)(2,1)S(1)} %get-tuple-element.60), channel_id=1, source_target_pairs={{0,7},{1,6},{2,5},{3,4},{4,3},{5,2},{6,1},{7,0},{8,15},{9,14},{10,... | collective-permute-start | bytes 393224 | tf_op jit(solution)/shard_map/across_3_1/ppermute | solution.py:329
  147.5 1.4 collective-permute-done.22.refs_3_
  148.9 0.0 collective-permute-done.23.refs_4_
  148.9 6.6 %collective-permute-done.24.refs_5_ = bf16[256,256]{1,0:T(8,128)(2,1)S(1)} collective-permute-done((bf16[256,256]{1,0:T(8,128)(2,1)S(1)}, bf16[256,256]{1,0:T(8,128)(2,1)S(1)}, u32[]{:S(2)}, u32[]{:S(2)}) %collective-permute-start.24) | collective-permute-done | bytes 131104 | tf_op jit(solution)/shard_map/across_1_1/ppermute | solution.py:329
  155.6 0.6 copy-done.12
  156.2 0.0 copy-done.13
  156.2 0.1 copy-done.14
  156.3 2.5 %place.1 = bf16[256,2048]{1,0:T(8,128)(2,1)} custom-call(bf16[256,256]{1,0:T(8,128)(2,1)} %copy-done.3, bf16[256,256]{1,0:T(8,128)(2,1)} %copy-done.8, bf16[256,256]{1,0:T(8,128)(2,1)} %copy-done.9, bf16[256,256]{1,0:T(8,128)(2,1)} %copy-done.10, bf16[256,256]{1,0:T(8,128)(2,1)} %copy-done.11, bf16[256,256]{1,0:T(8,128)(2,1)} %copy-done.12, ...), custom_call_target="tpu_custom_call" | custom-call | tf_op jit(solution)/shard_map/place/pallas_call | solution.py:430
  (30 shorter events, 0.1 us)
Async XLA Ops:
  0.0 5.3 %copy-start.4 = (bf16[256,2048]{1,0:T(8,128)(2,1)S(1)}, bf16[256,2048]{1,0:T(8,128)(2,1)}, u32[]{:S(2)}) copy-start(bf16[256,2048]{1,0:T(8,128)(2,1)} %refs_0_.2) | copy-start | bytes 3145732
  0.0 1.7 %collective-permute-start = (bf16[256,512]{1,0:T(8,128)(2,1)}, bf16[256,512]{1,0:T(8,128)(2,1)S(1)}, u32[]{:S(2)}, u32[]{:S(2)}) collective-permute-start(bf16[256,512]{1,0:T(8,128)(2,1)} %refs_0_.1), channel_id=1, source_target_pairs={{0,2},{1,3},{2,0},{3,1},{4,6},{5,7},{6,4},{7,5},{8,10},{9,11},{10,... | collective-permute-start | bytes 786440 | tf_op jit(solution)/shard_map/across_1_0/ppermute | solution.py:329
  0.1 2.1 %collective-permute-start.1 = (bf16[256,512]{1,0:T(8,128)(2,1)}, bf16[256,512]{1,0:T(8,128)(2,1)S(1)}, u32[]{:S(2)}, u32[]{:S(2)}) collective-permute-start(bf16[256,512]{1,0:T(8,128)(2,1)} %refs_1_.1), channel_id=1, source_target_pairs={{0,2},{1,3},{2,0},{3,1},{4,6},{5,7},{6,4},{7,5},{8,10},{9,11},{10,... | collective-permute-start | bytes 786440 | tf_op jit(solution)/shard_map/across_1_0/ppermute | solution.py:329
  1.7 0.7 copy-start.6
  2.5 0.7 copy-start.7
  5.3 2.7 %collective-permute-start.2 = (bf16[256,2048]{1,0:T(8,128)(2,1)S(1)}, bf16[256,2048]{1,0:T(8,128)(2,1)S(1)}, u32[]{:S(2)}, u32[]{:S(2)}) collective-permute-start(bf16[256,2048]{1,0:T(8,128)(2,1)S(1)} %copy-done.4), channel_id=1, source_target_pairs={{0,2},{1,3},{2,0},{3,1},{4,6},{5,7},{6,4},{7,5},{8,10},{9,11},{10,... | collective-permute-start | bytes 3145736 | tf_op jit(solution)/shard_map/across_1_0/ppermute | solution.py:329
  7.9 1.0 copy-start.5
  11.5 9.2 %copy-start.1 = (bf16[2,256,256]{2,1,0:T(8,128)(2,1)S(1)}, bf16[2,256,256]{2,1,0:T(8,128)(2,1)}, u32[]{:S(2)}) copy-start(bf16[2,256,256]{2,1,0:T(8,128)(2,1)} %get-tuple-element.33.refs_1_) | copy-start | bytes 786436
  14.0 14.6 %collective-permute-start.3 = (bf16[2048,128]{1,0:T(8,128)(2,1)}, bf16[2048,128]{1,0:T(8,128)(2,1)S(1)}, u32[]{:S(2)}, u32[]{:S(2)}) collective-permute-start(bf16[2048,128]{1,0:T(8,128)(2,1)} %get-tuple-element.38), channel_id=1, source_target_pairs={{0,1},{1,0},{2,3},{3,2},{4,5},{5,4},{6,7},{7,6},{8,9},{9,8},{10,11... | collective-permute-start | bytes 1572872 | tf_op jit(solution)/shard_map/across_0_1/ppermute | solution.py:329
  16.3 23.4 %collective-permute-start.12 = (bf16[2,256,256]{2,1,0:T(8,128)(2,1)}, bf16[2,256,256]{2,1,0:T(8,128)(2,1)S(1)}, u32[]{:S(2)}, u32[]{:S(2)}) collective-permute-start(bf16[2,256,256]{2,1,0:T(8,128)(2,1)} %get-tuple-element.39), channel_id=1, source_target_pairs={{0,4},{1,5},{2,6},{3,7},{4,0},{5,1},{6,2},{7,3},{8,12},{9,13},{10,... | collective-permute-start | bytes 786440 | tf_op jit(solution)/shard_map/across_2_0/ppermute | solution.py:329
  17.5 12.2 %collective-permute-start.5 = (bf16[2,256,256]{2,1,0:T(8,128)(2,1)}, bf16[2,256,256]{2,1,0:T(8,128)(2,1)S(1)}, u32[]{:S(2)}, u32[]{:S(2)}) collective-permute-start(bf16[2,256,256]{2,1,0:T(8,128)(2,1)} %get-tuple-element.39), channel_id=1, source_target_pairs={{0,12},{1,13},{2,14},{3,15},{4,8},{5,9},{6,10},{7,11},{8,20},{9,21... | collective-permute-start | bytes 786440 | tf_op jit(solution)/shard_map/up_2/ppermute | solution.py:333
  20.7 10.6 %collective-permute-start.4 = (bf16[2,256,256]{2,1,0:T(8,128)(2,1)S(1)}, bf16[2,256,256]{2,1,0:T(8,128)(2,1)S(1)}, u32[]{:S(2)}, u32[]{:S(2)}) collective-permute-start(bf16[2,256,256]{2,1,0:T(8,128)(2,1)S(1)} %copy-done.1), channel_id=1, source_target_pairs={{0,8},{1,9},{2,10},{3,11},{4,12},{5,13},{6,14},{7,15},{8,16},{9,17... | collective-permute-start | bytes 786440 | tf_op jit(solution)/shard_map/up_0/ppermute | solution.py:333
  23.9 21.3 %collective-permute-start.11 = (bf16[2,256,512]{2,1,0:T(8,128)(2,1)}, bf16[2,256,512]{2,1,0:T(8,128)(2,1)S(1)}, u32[]{:S(2)}, u32[]{:S(2)}) collective-permute-start(bf16[2,256,512]{2,1,0:T(8,128)(2,1)} %get-tuple-element.44), channel_id=1, source_target_pairs={{0,4},{1,5},{2,6},{3,7},{4,0},{5,1},{6,2},{7,3},{8,12},{9,13},{10,... | collective-permute-start | bytes 1572872 | tf_op jit(solution)/shard_map/across_2_0/ppermute | solution.py:329
  28.5 10.8 %copy-start.2 = (s32[4096]{0:T(1024)S(1)}, s32[4096]{0:T(1024)}, u32[]{:S(2)}) copy-start(s32[4096]{0:T(1024)} %seg_ref.5) | copy-start | bytes 49156
  28.5 11.2 %copy-start = (bf16[2,256,512]{2,1,0:T(8,128)(2,1)S(1)}, bf16[2,256,512]{2,1,0:T(8,128)(2,1)}, u32[]{:S(2)}) copy-start(bf16[2,256,512]{2,1,0:T(8,128)(2,1)} %get-tuple-element.35.refs_0_) | copy-start | bytes 1572868
  31.3 22.2 %collective-permute-start.6 = (bf16[2,256,256]{2,1,0:T(8,128)(2,1)S(1)}, bf16[2,256,256]{2,1,0:T(8,128)(2,1)S(1)}, u32[]{:S(2)}, u32[]{:S(2)}) collective-permute-start(bf16[2,256,256]{2,1,0:T(8,128)(2,1)S(1)} %collective-permute-done.4.refs_3_), channel_id=1, source_target_pairs={{0,8},{1,9},{2,10},{3,11},{4,12},{5,13},{6,14},{7,15},{8,16},{9,17... | collective-permute-start | bytes 786440 | tf_op jit(solution)/shard_map/up_0/ppermute | solution.py:333
  35.4 18.1 %collective-permute-start.7 = (bf16[2,256,256]{2,1,0:T(8,128)(2,1)S(1)}, bf16[2,256,256]{2,1,0:T(8,128)(2,1)}, u32[]{:S(2)}, u32[]{:S(2)}) collective-permute-start(bf16[2,256,256]{2,1,0:T(8,128)(2,1)S(1)} %collective-permute-done.5.refs_4_), channel_id=1, source_target_pairs={{0,8},{1,9},{2,10},{3,11},{4,12},{5,13},{6,14},{7,15},{8,16},{9,17... | collective-permute-start | bytes 786440 | tf_op jit(solution)/shard_map/up_0/ppermute | solution.py:333
  39.3 48.2 %collective-permute-start.9 = (bf16[4096,128]{1,0:T(8,128)(2,1)S(1)}, bf16[4096,128]{1,0:T(8,128)(2,1)S(1)}, u32[]{:S(2)}, u32[]{:S(2)}) collective-permute-start(bf16[4096,128]{1,0:T(8,128)(2,1)S(1)} %pad_maximum_fusion.refs_0_), channel_id=1, source_target_pairs={{0,16},{1,17},{2,18},{3,19},{4,20},{5,21},{6,22},{7,23},{8,24},{9,... | collective-permute-start | bytes 3145736 | tf_op jit(solution)/shard_map/between_2/ppermute | solution.py:337
  53.5 54.0 %collective-permute-start.8 = (bf16[4096,128]{1,0:T(8,128)(2,1)S(1)}, bf16[4096,128]{1,0:T(8,128)(2,1)S(1)}, u32[]{:S(2)}, u32[]{:S(2)}) collective-permute-start(bf16[4096,128]{1,0:T(8,128)(2,1)S(1)} %pad_maximum_fusion.refs_0_), channel_id=1, source_target_pairs={{0,8},{1,9},{2,10},{3,11},{4,12},{5,13},{6,14},{7,15},{8,0},{9,1},... | collective-permute-start | bytes 3145736 | tf_op jit(solution)/shard_map/between_1/ppermute | solution.py:337
  68.1 39.5 %collective-permute-start.18 = (bf16[4,256,512]{2,1,0:T(8,128)(2,1)S(1)}, bf16[4,256,512]{2,1,0:T(8,128)(2,1)S(1)}, u32[]{:S(2)}, u32[]{:S(2)}) collective-permute-start(bf16[4,256,512]{2,1,0:T(8,128)(2,1)S(1)} %attention.5.refs_4_), channel_id=1, source_target_pairs={{0,5},{1,4},{2,7},{3,6},{4,1},{5,0},{6,3},{7,2},{8,13},{9,12},{10,... | collective-permute-start | bytes 3145736 | tf_op jit(solution)/shard_map/across_2_1/ppermute | solution.py:329
  69.3 47.3 %collective-permute-start.16 = (bf16[4,256,512]{2,1,0:T(8,128)(2,1)S(1)}, bf16[4,256,512]{2,1,0:T(8,128)(2,1)S(1)}, u32[]{:S(2)}, u32[]{:S(2)}) collective-permute-start(bf16[4,256,512]{2,1,0:T(8,128)(2,1)S(1)} %attention.5.refs_4_), channel_id=1, source_target_pairs={{0,1},{1,0},{2,3},{3,2},{4,5},{5,4},{6,7},{7,6},{8,9},{9,8},{10,11... | collective-permute-start | bytes 3145736 | tf_op jit(solution)/shard_map/across_0_1/ppermute | solution.py:329
  70.5 46.6 %collective-permute-start.14 = (bf16[4,256,512]{2,1,0:T(8,128)(2,1)S(1)}, bf16[4,256,512]{2,1,0:T(8,128)(2,1)S(1)}, u32[]{:S(2)}, u32[]{:S(2)}) collective-permute-start(bf16[4,256,512]{2,1,0:T(8,128)(2,1)S(1)} %attention.5.refs_4_), channel_id=1, source_target_pairs={{0,4},{1,5},{2,6},{3,7},{4,0},{5,1},{6,2},{7,3},{8,12},{9,13},{10,... | collective-permute-start | bytes 3145736 | tf_op jit(solution)/shard_map/across_2_0/ppermute | solution.py:329
  87.5 29.6 %collective-permute-start.13 = (bf16[4,256,512]{2,1,0:T(8,128)(2,1)S(1)}, bf16[4,256,512]{2,1,0:T(8,128)(2,1)S(1)}, u32[]{:S(2)}, u32[]{:S(2)}) collective-permute-start(bf16[4,256,512]{2,1,0:T(8,128)(2,1)S(1)} %attention.5.refs_4_), channel_id=1, source_target_pairs={{0,2},{1,3},{2,0},{3,1},{4,6},{5,7},{6,4},{7,5},{8,10},{9,11},{10,... | collective-permute-start | bytes 3145736 | tf_op jit(solution)/shard_map/across_1_0/ppermute | solution.py:329
  107.6 22.8 %collective-permute-start.10 = (bf16[4096,128]{1,0:T(8,128)(2,1)S(1)}, bf16[4096,128]{1,0:T(8,128)(2,1)S(1)}, u32[]{:S(2)}, u32[]{:S(2)}) collective-permute-start(bf16[4096,128]{1,0:T(8,128)(2,1)S(1)} %collective-permute-done.9.refs_2_), channel_id=1, source_target_pairs={{0,8},{1,9},{2,10},{3,11},{4,12},{5,13},{6,14},{7,15},{8,0},{9,1},... | collective-permute-start | bytes 3145736 | tf_op jit(solution)/shard_map/between_1/ppermute | solution.py:337
  107.6 22.8 %collective-permute-start.19 = (bf16[4,256,512]{2,1,0:T(8,128)(2,1)S(1)}, bf16[4,256,512]{2,1,0:T(8,128)(2,1)S(1)}, u32[]{:S(2)}, u32[]{:S(2)}) collective-permute-start(bf16[4,256,512]{2,1,0:T(8,128)(2,1)S(1)} %collective-permute-done.18.refs_10_), channel_id=1, source_target_pairs={{0,2},{1,3},{2,0},{3,1},{4,6},{5,7},{6,4},{7,5},{8,10},{9,11},{10,... | collective-permute-start | bytes 3145736 | tf_op jit(solution)/shard_map/across_1_0/ppermute | solution.py:329
  116.6 13.8 %collective-permute-start.17 = (bf16[4,256,512]{2,1,0:T(8,128)(2,1)S(1)}, bf16[4,256,512]{2,1,0:T(8,128)(2,1)S(1)}, u32[]{:S(2)}, u32[]{:S(2)}) collective-permute-start(bf16[4,256,512]{2,1,0:T(8,128)(2,1)S(1)} %collective-permute-done.16.refs_8_), channel_id=1, source_target_pairs={{0,2},{1,3},{2,0},{3,1},{4,6},{5,7},{6,4},{7,5},{8,10},{9,11},{10,... | collective-permute-start | bytes 3145736 | tf_op jit(solution)/shard_map/across_1_0/ppermute | solution.py:329
  117.1 13.3 %collective-permute-start.15 = (bf16[4,256,512]{2,1,0:T(8,128)(2,1)S(1)}, bf16[4,256,512]{2,1,0:T(8,128)(2,1)S(1)}, u32[]{:S(2)}, u32[]{:S(2)}) collective-permute-start(bf16[4,256,512]{2,1,0:T(8,128)(2,1)S(1)} %collective-permute-done.14.refs_6_), channel_id=1, source_target_pairs={{0,2},{1,3},{2,0},{3,1},{4,6},{5,7},{6,4},{7,5},{8,10},{9,11},{10,... | collective-permute-start | bytes 3145736 | tf_op jit(solution)/shard_map/across_1_0/ppermute | solution.py:329
  136.8 0.7 copy-start.3
  137.4 6.3 %collective-permute-start.20 = (bf16[256,256]{1,0:T(8,128)(2,1)S(1)}, bf16[256,256]{1,0:T(8,128)(2,1)S(1)}, u32[]{:S(2)}, u32[]{:S(2)}) collective-permute-start(bf16[256,256]{1,0:T(8,128)(2,1)S(1)} %get-tuple-element.54), channel_id=1, source_target_pairs={{0,2},{1,3},{2,0},{3,1},{4,6},{5,7},{6,4},{7,5},{8,10},{9,11},{10,... | collective-permute-start | bytes 393224 | tf_op jit(solution)/shard_map/across_1_0/ppermute | solution.py:329
  140.2 5.1 %collective-permute-start.21 = (bf16[256,256]{1,0:T(8,128)(2,1)S(1)}, bf16[256,256]{1,0:T(8,128)(2,1)S(1)}, u32[]{:S(2)}, u32[]{:S(2)}) collective-permute-start(bf16[256,256]{1,0:T(8,128)(2,1)S(1)} %get-tuple-element.55), channel_id=1, source_target_pairs={{0,4},{1,5},{2,6},{3,7},{4,0},{5,1},{6,2},{7,3},{8,12},{9,13},{10,... | collective-permute-start | bytes 393224 | tf_op jit(solution)/shard_map/across_2_0/ppermute | solution.py:329
  141.4 7.5 %collective-permute-start.22 = (bf16[256,256]{1,0:T(8,128)(2,1)S(1)}, bf16[256,256]{1,0:T(8,128)(2,1)S(1)}, u32[]{:S(2)}, u32[]{:S(2)}) collective-permute-start(bf16[256,256]{1,0:T(8,128)(2,1)S(1)} %get-tuple-element.56), channel_id=1, source_target_pairs={{0,6},{1,7},{2,4},{3,5},{4,2},{5,3},{6,0},{7,1},{8,14},{9,15},{10,... | collective-permute-start | bytes 393224 | tf_op jit(solution)/shard_map/across_3_0/ppermute | solution.py:329
  141.8 7.1 %collective-permute-start.23 = (bf16[256,256]{1,0:T(8,128)(2,1)S(1)}, bf16[256,256]{1,0:T(8,128)(2,1)S(1)}, u32[]{:S(2)}, u32[]{:S(2)}) collective-permute-start(bf16[256,256]{1,0:T(8,128)(2,1)S(1)} %get-tuple-element.57), channel_id=1, source_target_pairs={{0,1},{1,0},{2,3},{3,2},{4,5},{5,4},{6,7},{7,6},{8,9},{9,8},{10,11... | collective-permute-start | bytes 393224 | tf_op jit(solution)/shard_map/across_0_1/ppermute | solution.py:329
  142.1 13.4 %collective-permute-start.24 = (bf16[256,256]{1,0:T(8,128)(2,1)S(1)}, bf16[256,256]{1,0:T(8,128)(2,1)S(1)}, u32[]{:S(2)}, u32[]{:S(2)}) collective-permute-start(bf16[256,256]{1,0:T(8,128)(2,1)S(1)} %get-tuple-element.58), channel_id=1, source_target_pairs={{0,3},{1,2},{2,1},{3,0},{4,7},{5,6},{6,5},{7,4},{8,11},{9,10},{10,... | collective-permute-start | bytes 393224 | tf_op jit(solution)/shard_map/across_1_1/ppermute | solution.py:329
  143.7 11.8 %copy-start.8 = (bf16[256,256]{1,0:T(8,128)(2,1)}, bf16[256,256]{1,0:T(8,128)(2,1)S(1)}, u32[]{:S(2)}) copy-start(bf16[256,256]{1,0:T(8,128)(2,1)S(1)} %collective-permute-done.20.refs_1_) | copy-start | bytes 393220
  143.7 11.8 %collective-permute-start.25 = (bf16[256,256]{1,0:T(8,128)(2,1)S(1)}, bf16[256,256]{1,0:T(8,128)(2,1)S(1)}, u32[]{:S(2)}, u32[]{:S(2)}) collective-permute-start(bf16[256,256]{1,0:T(8,128)(2,1)S(1)} %get-tuple-element.59), channel_id=1, source_target_pairs={{0,5},{1,4},{2,7},{3,6},{4,1},{5,0},{6,3},{7,2},{8,13},{9,12},{10,... | collective-permute-start | bytes 393224 | tf_op jit(solution)/shard_map/across_2_1/ppermute | solution.py:329
  145.3 10.2 %copy-start.9 = (bf16[256,256]{1,0:T(8,128)(2,1)}, bf16[256,256]{1,0:T(8,128)(2,1)S(1)}, u32[]{:S(2)}) copy-start(bf16[256,256]{1,0:T(8,128)(2,1)S(1)} %collective-permute-done.21.refs_2_) | copy-start | bytes 393220
  145.3 10.2 %collective-permute-start.26 = (bf16[256,256]{1,0:T(8,128)(2,1)S(1)}, bf16[256,256]{1,0:T(8,128)(2,1)S(1)}, u32[]{:S(2)}, u32[]{:S(2)}) collective-permute-start(bf16[256,256]{1,0:T(8,128)(2,1)S(1)} %get-tuple-element.60), channel_id=1, source_target_pairs={{0,7},{1,6},{2,5},{3,4},{4,3},{5,2},{6,1},{7,0},{8,15},{9,14},{10,... | collective-permute-start | bytes 393224 | tf_op jit(solution)/shard_map/across_3_1/ppermute | solution.py:329
  148.9 6.6 %copy-start.10 = (bf16[256,256]{1,0:T(8,128)(2,1)}, bf16[256,256]{1,0:T(8,128)(2,1)S(1)}, u32[]{:S(2)}) copy-start(bf16[256,256]{1,0:T(8,128)(2,1)S(1)} %collective-permute-done.22.refs_3_) | copy-start | bytes 393220
  148.9 6.6 %copy-start.11 = (bf16[256,256]{1,0:T(8,128)(2,1)}, bf16[256,256]{1,0:T(8,128)(2,1)S(1)}, u32[]{:S(2)}) copy-start(bf16[256,256]{1,0:T(8,128)(2,1)S(1)} %collective-permute-done.23.refs_4_) | copy-start | bytes 393220
  155.5 0.7 copy-start.12
  155.5 0.7 copy-start.13
  155.5 0.8 copy-start.14

commit v3 on v2

--- a/solution.py
+++ b/solution.py
@@ -34,34 +34,28 @@
     return lax.bitwise_xor(z // (planes // attn), y)
 
 
-def split_kv_kernel(group, *refs):
+def split_qkv_kernel(group, *refs):
     g = place_in(group)[1]
+    kv_outs, q_outs = refs[6 : 6 + group // 2], refs[6 + group // 2 :]
+    width = q_outs[0].shape[2]
     for core in range(2):
-        k_ref, v_ref = refs[2 * core : 2 * core + 2]
-        for o, out in enumerate(refs[4:]):
+        k_ref, v_ref, q_ref = refs[3 * core : 3 * core + 3]
+        for o in range(group // 2):
             at = pl.ds(pl.multiple_of(xor(g, 2 * o) * HEAD, HEAD), HEAD)
-            out[core, :, :HEAD] = k_ref[:, at]
-            out[core, :, HEAD:] = v_ref[:, at]
-
-
-def split_q_kernel(group, *refs):
-    g = place_in(group)[1]
-    width = refs[2].shape[2]
-    for core in range(2):
-        for o, out in enumerate(refs[2:]):
-            out[core] = refs[core][:, pl.ds(pl.multiple_of(xor(g, 2 * o) * width, width), width)]
+            kv_outs[o][core, :, :HEAD] = k_ref[:, at]
+            kv_outs[o][core, :, HEAD:] = v_ref[:, at]
+            q_outs[o][core] = q_ref[:, pl.ds(pl.multiple_of(xor(g, 2 * o) * width, width), width)]
 
 
 def split_w_kernel(group, w_ref, *outs):
     g, y = place_in(group)[1:]
     rows, cols = outs[0].shape
     width = rows // group
-    for m in range(len(outs)):
+    for m, out in enumerate(outs):
         at = pl.ds(pl.multiple_of(xor(y, m) * cols, cols), cols)
         for j in range(group):
-            outs[m][j * width : (j + 1) * width, :] = w_ref[
-                pl.ds(pl.multiple_of(xor(g, j) * width, width), width), at
-            ]
+            part = w_ref[pl.ds(pl.multiple_of(xor(g, j) * width, width), width), at]
+            out[j * width : (j + 1) * width, :] = part
 
 
 def attention_kernel(group, heads, back, pairs, carried, final, seg_ref, segrow_ref, *refs):
@@ -69,9 +63,9 @@
     refs = list(refs)
     take = lambda count: [refs.pop(0) for _ in range(count)]
     q_refs, kv_refs = take(len(pairs)), take(n_kv // 2)
-    state_refs = [take(3) for _ in pairs] if carried else None
-    out_refs = take(1 if final else 3)
-    q_s, k_s, v_s, s_s, m_s, l_s, acc_s, seg_s, sem = refs
+    state_refs = [take(2) for _ in pairs] if carried else None
+    out_refs = take(1 if final else 2)
+    q_s, k_s, v_s, m_own, acc_own, seg_s, sem = refs
     n = segrow_ref.shape[1]
     rows = heads * n
     lanes = n // HEAD
@@ -82,11 +76,13 @@
             copies.append((q_part, q_s.at[k, pl.ds(h * n, n), :]))
     for i in range(n_kv):
         kv = kv_refs[i // 2].at[i % 2]
-        copies.append((kv.at[:, pl.ds(0, HEAD)], k_s.at[i]))
-        copies.append((kv.at[:, pl.ds(HEAD, HEAD)], v_s.at[i]))
+        at = pl.ds(i % 2 * n, n)
+        copies.append((kv.at[:, pl.ds(0, HEAD)], k_s.at[i // 2, at, :]))
+        copies.append((kv.at[:, pl.ds(HEAD, HEAD)], v_s.at[i // 2, at, pl.ds(0, HEAD)]))
     copies = [pltpu.make_async_copy(a, b, sem.at[i]) for i, (a, b) in enumerate(copies)]
     for c in copies:
         c.start()
+    v_s[:, :, HEAD:] = jnp.ones((n_kv // 2, 2 * n, HEAD), jnp.bfloat16)
     for c in copies:
         c.wait()
 
@@ -96,105 +92,108 @@
     def one_query_piece(pair, core, carry):
         at = 2 * pair + core
         given = [ref.at[core] for ref in state_refs[pair]] if carried else None
+        m_s, acc_s = (m_own, acc_own) if final else (ref.at[at] for ref in out_refs)
         qp = plane * group + lax.bitwise_xor(g, 2 * pairs[pair] + core)
         q_first, q_last = seg_ref[qp * n], seg_ref[qp * n + n - 1]
 
-        def state(i):
-            kp = (plane - back[0] - i // group) * group + lax.bitwise_xor(g, lax.rem(i, group))
+        def piece(i, which):
+            place = lax.bitwise_xor(g, 2 * lax.rem(i, group // 2) + which)
+            kp = (plane - back[0] - i // (group // 2)) * group + place
             safe = jnp.maximum(kp, 0)
             active = (kp >= 0) & (kp <= qp) & (seg_ref[safe * n + n - 1] >= q_first)
-            whole = (kp < qp) & (seg_ref[safe * n] == q_last)
+            whole = (kp >= 0) & (kp < qp) & (seg_ref[safe * n] == q_last)
             return kp, safe, active, whole
 
-        def parts_of(i):
-            return [s_s[i, :, t * HEAD : (t + 1) * HEAD] for t in range(lanes)]
-
-        def score(i, carry):
-            kp, safe, active, whole = state(i)
-
-            @pl.when(active)
-            def _():
-                s_s[i] = lax.dot_general(
-                    q_s[at], k_s[i], (((1,), (1,)), ((), ())), preferred_element_type=jnp.float32
+        def needed(i):
+            return piece(i, 0)[2] | piece(i, 1)[2]
+
+        def mix(i, carry):
+            pieces = [piece(i, which) for which in range(2)]
+            active = pieces[0][2] | pieces[1][2]
+            whole = pieces[0][3] & pieces[1][3]
+
+            def scores(h):
+                return lax.dot_general(
+                    q_s[at, h * n : (h + 1) * n],
+                    k_s[i],
+                    (((1,), (1,)), ((), ())),
+                    preferred_element_type=jnp.float32,
                 )
+
+            def each_head(seen):
+                ahead = scores(0)
+                for h in range(heads):
+                    s, ahead = ahead, scores(h + 1) if h + 1 < heads else None
+                    head(h, s, seen)
+
+            def head(h, s, seen):
+                row = slice(h * n, (h + 1) * n)
+                if seen is not None:
+                    s = jnp.where(seen, s, NEGATIVE)
+                old = m_s[row]
+                top = jnp.maximum(old, jnp.max(s, axis=1, keepdims=True))
+                m_s[row] = top
+                shrink = jnp.exp2((old - top) * scale)
+                top = jnp.concatenate([top] * (2 * lanes), axis=1)
+                weights = jnp.exp2((s - top) * scale).astype(jnp.bfloat16)
+                found = jnp.dot(weights, v_s[i], preferred_element_type=jnp.float32)
+                acc_s[row] = acc_s[row] * jnp.concatenate([shrink] * 2, axis=1) + found
 
             @pl.when(active & whole)
             def _():
-                m_s[...] = functools.reduce(jnp.maximum, parts_of(i), m_s[...])
+                each_head(None)
 
             @pl.when(active & jnp.logical_not(whole))
             def _():
-                seg_k = segrow_ref[pl.ds(safe, 1), :].astype(jnp.float32)
                 ahead = lax.broadcasted_iota(jnp.int32, (n, HEAD), 1) - lax.broadcasted_iota(
                     jnp.int32, (n, HEAD), 0
                 )
-                for t in range(lanes):
-                    lane = slice(t * HEAD, (t + 1) * HEAD)
-                    seen = (ahead + t * HEAD <= (qp - kp) * n) & (seg_s[...] == seg_k[:, lane])
-                    for h in range(heads):
-                        row = slice(h * n, (h + 1) * n)
-                        part = jnp.where(seen, s_s[i, row, lane], NEGATIVE)
-                        s_s[i, row, lane] = part
-                        m_s[row] = jnp.maximum(m_s[row], part)
+                seen = []
+                for kp, safe, _, _ in pieces:
+                    seg_k = segrow_ref[pl.ds(safe, 1), :].astype(jnp.float32)
+                    for t in range(lanes):
+                        same = seg_s[...] == seg_k[:, t * HEAD : (t + 1) * HEAD]
+                        seen.append(same & (ahead + t * HEAD <= (qp - kp) * n) & (kp >= 0))
+                seen = jnp.concatenate(seen, axis=1)
+                each_head(seen)
 
             return carry
 
-        def mix(i, carry):
-            @pl.when(state(i)[2])
-            def _():
-                top = m_s[...]
-                parts = [jnp.exp2((part - top) * scale) for part in parts_of(i)]
-                l_s[...] += functools.reduce(jnp.add, parts)
-                weights = jnp.concatenate([p.astype(jnp.bfloat16) for p in parts], axis=1)
-                acc_s[...] += jnp.dot(weights, v_s[i], preferred_element_type=jnp.float32)
-
-            return carry
-
-        def both_passes():
-            row = segrow_ref[pl.ds(qp, 1), :].astype(jnp.float32)
-            seg_s[...] = jnp.broadcast_to(row, (HEAD, n)).T
+        def give(summed):
+            for h in range(heads):
+                row = slice(h * n, (h + 1) * n)
+                out_refs[0][at, :, h * HEAD : (h + 1) * HEAD] = (
+                    summed[row, :HEAD] / summed[row, HEAD:]
+                ).astype(jnp.bfloat16)
+
+        def all_keys():
+            seg_row = segrow_ref[pl.ds(qp, 1), :].astype(jnp.float32)
+            seg_s[...] = jnp.broadcast_to(seg_row, (HEAD, n)).T
             if carried:
                 m_s[...] = given[0][...]
+                acc_s[...] = given[1][...]
             else:
                 m_s[...] = jnp.full(m_s.shape, NEGATIVE, jnp.float32)
-            lax.fori_loop(0, n_kv, score, 0)
-            top = jnp.broadcast_to(jnp.max(m_s[...], axis=1, keepdims=True), (rows, HEAD))
-            if carried:
-                shrink = jnp.exp2((given[0][...] - top) * scale)
-                l_s[...] = given[1][...] * shrink
-                acc_s[...] = given[2][...] * shrink
-            else:
-                l_s[...] = jnp.zeros(l_s.shape, jnp.float32)
                 acc_s[...] = jnp.zeros(acc_s.shape, jnp.float32)
-            m_s[...] = top
-            lax.fori_loop(0, n_kv, mix, 0)
-
-        def give(lane_sums, summed):
-            for h in range(heads):
-                row = slice(h * n, (h + 1) * n)
-                total = jnp.sum(lane_sums[row], axis=1, keepdims=True)
-                out_refs[0][at, :, h * HEAD : (h + 1) * HEAD] = (summed[row] / total).astype(jnp.bfloat16)
+            lax.fori_loop(0, n_kv // 2, mix, 0)
 
         if carried:
-            needed = lax.fori_loop(
-                0, n_kv, lambda i, seen: seen | state(i)[2].astype(jnp.int32), jnp.int32(0)
+            any_needed = lax.fori_loop(
+                0, n_kv // 2, lambda i, seen: seen | needed(i).astype(jnp.int32), jnp.int32(0)
             )
 
-            @pl.when(needed > 0)
+            @pl.when(any_needed > 0)
             def _():
-                both_passes()
-                give(l_s[...], acc_s[...])
-
-            @pl.when(needed == 0)
+                all_keys()
+                give(acc_s)
+
+            @pl.when(any_needed == 0)
             def _():
-                give(given[1][...], given[2][...])
+                give(given[1])
         else:
-            both_passes()
+            all_keys()
             if final:
-                give(l_s[...], acc_s[...])
-            else:
-                for out_ref, value in zip(out_refs, (m_s, l_s, acc_s)):
-                    out_ref[at] = value[...]
+                give(acc_s)
         return carry
 
     for pair in range(len(pairs)):
@@ -204,11 +203,10 @@
 def attention(group, heads, back, pairs, segments, q, kv, carried=None, final=True):
     n, width = q[0].shape[1:]
     rows, n_kv, n_q = heads * n, 2 * len(kv), 2 * len(pairs)
-    state = jax.ShapeDtypeStruct((n_q, rows, HEAD), jnp.float32)
     if final:
         out_shape = [jax.ShapeDtypeStruct((n_q, n, width), jnp.bfloat16)]
     else:
-        out_shape = [state] * 3
+        out_shape = [jax.ShapeDtypeStruct((n_q, rows, lanes), jnp.float32) for lanes in (HEAD, 2 * HEAD)]
     carried = list(carried or ())
     found = pl.pallas_call(
         functools.partial(attention_kernel, group, heads, back, pairs, bool(carried), final),
@@ -217,12 +215,10 @@
         out_specs=[VMEM] * len(out_shape),
         scratch_shapes=[
             pltpu.VMEM((n_q, rows, HEAD), jnp.bfloat16),
-            pltpu.VMEM((n_kv, n, HEAD), jnp.bfloat16),
-            pltpu.VMEM((n_kv, n, HEAD), jnp.bfloat16),
-            pltpu.VMEM((n_kv, rows, n), jnp.float32),
+            pltpu.VMEM((n_kv // 2, 2 * n, HEAD), jnp.bfloat16),
+            pltpu.VMEM((n_kv // 2, 2 * n, 2 * HEAD), jnp.bfloat16),
             pltpu.VMEM((rows, HEAD), jnp.float32),
-            pltpu.VMEM((rows, HEAD), jnp.float32),
-            pltpu.VMEM((rows, HEAD), jnp.float32),
+            pltpu.VMEM((rows, 2 * HEAD), jnp.float32),
             pltpu.VMEM((n, HEAD), jnp.float32),
             pltpu.SemaphoreType.DMA((n_q * heads + 2 * n_kv,)),
         ],
@@ -341,28 +337,6 @@
 
     after = lambda array, *others: lax.optimization_barrier((array, *others))
 
-    pair = [bf16(2, n, 2 * HEAD)] * (group // 2)
-    kv = pl.pallas_call(
-        functools.partial(split_kv_kernel, group),
-        out_shape=pair,
-        in_specs=[VMEM] * 4,
-        out_specs=[VMEM] * (group // 2),
-        name="split_kv",
-    )(keys, values, across(keys, 1, 0), across(values, 1, 0))
-    links = [[kv[0]] + [across(kv[o], 2 * o, 0) for o in range(1, group // 2)]]
-    links.append([up(kv[o], 2 * o) for o in range(group // 2)])
-
-    queries, _ = after(queries, kv[0])
-    q = pl.pallas_call(
-        functools.partial(split_q_kernel, group),
-        out_shape=[bf16(2, n, width)] * (group // 2),
-        in_specs=[VMEM] * 2,
-        out_specs=[VMEM] * (group // 2),
-        name="split_q",
-    )(queries, across(queries, 1, 0))
-    out_weight, _ = after(out_weight, q[0])
-    q = [q[0]] + [across(q[o], 2 * o, 0) for o in range(1, group // 2)]
-
     if cols % HEAD == 0:
         own = pl.pallas_call(
             functools.partial(split_w_kernel, group),
@@ -377,7 +351,23 @@
             [lax.dynamic_slice_in_dim(out_weight, xor(g, j) * width, width, 0) for j in range(group)]
         )
         own = [lax.dynamic_slice_in_dim(ordered, xor(y, m) * cols, cols, 1) for m in range(attn)]
-    own = jnp.concatenate([own[0]] + [across(own[m], 0, m) for m in range(1, attn)])
+    others = [own[0]] + [across(own[m], 0, m) for m in range(1, attn)]
+
+    keys, *own = after(keys, *own)
+    near = [keys, values, queries]
+    split = pl.pallas_call(
+        functools.partial(split_qkv_kernel, group),
+        out_shape=[bf16(2, n, 2 * HEAD)] * (group // 2) + [bf16(2, n, width)] * (group // 2),
+        in_specs=[VMEM] * 6,
+        out_specs=[VMEM] * group,
+        name="split_qkv",
+    )(*near, *[across(array, 1, 0) for array in near])
+    kv, q = split[: group // 2], split[group // 2 :]
+    links = [[kv[0]] + [across(kv[o], 2 * o, 0) for o in range(1, group // 2)]]
+    links.append([up(kv[o], 2 * o) for o in range(group // 2)])
+    q = [q[0]] + [across(q[o], 2 * o, 0) for o in range(1, group // 2)]
+
+    own = jnp.concatenate(others)
     own, *links[1] = after(own, *links[1])
     for _ in range(1, hops):
         links.append([up(pair) for pair in links[-1]])
@@ -386,8 +376,6 @@
     while stride:
         for i in list(blocks):
             blocks[i + stride] = between(blocks[i], stride)
-        if stride == planes // 2:
-            blocks[0], *links[-1] = after(own, *links[-1])
         stride //= 2
 
     near = [pair for pairs_of in links[:hops] for pair in pairs_of]

time: 158 us -> 143 us (0.905)
  the two profiles are of different devices: /device:TPU:1 before, /device:TPU:25 now
where the time goes in v3:
time: 143 us; the launch traced here: 140 us
  waiting for transfers between devices  75.6 us (53%)
  Pallas kernels  34.7 us (24%)
  starting transfers between devices  25.7 us (18%)
  local copies, waits for them, and re-layouts  3.09 us (2%)
    ppermute x20, waiting for transfers between devices, across(): return lax.ppermute(array, AXES, pairs(lambda z, g, y: (z, g ^ j, y ^ m)))  37.9 us
    ppermute x3, waiting for transfers between devices, between(): return lax.ppermute(array, AXES, pairs(lambda z, g, y: (z ^ i, g, y)))  29.3 us
    pallas_call x3, Pallas kernels, attention(): pl.pallas_call(functools.partial(attention_kernel, group, heads, back, pa...  20 us
    ppermute x20, starting transfers between devices, across(): return lax.ppermute(array, AXES, pairs(lambda z, g, y: (z, g ^ j, y ^ m)))  16 us
    ppermute x4, waiting for transfers between devices, up(): return lax.ppermute(array, AXES, pairs(lambda z, g, y: (z + 1, g ^ j, y)))  8.43 us
    pallas_call x1, Pallas kernels, shards(): pl.pallas_call(functools.partial(project_kernel, group, attn, planes), ou...  6.57 us
    ppermute x4, starting transfers between devices, up(): return lax.ppermute(array, AXES, pairs(lambda z, g, y: (z + 1, g ^ j, y)))  5.28 us
    ppermute x3, starting transfers between devices, between(): return lax.ppermute(array, AXES, pairs(lambda z, g, y: (z ^ i, g, y)))  4.38 us
  transfers between devices with their start and end apart: 27, of which 12 were waited for; matrix products, arithmetic and copies ran while one was open for 1% of the time, Pallas kernels for 18%

profile of v3, /device:TPU:25, one launch (start us, length us, event | category | flops | bytes accessed | tf_op | source)
XLA Modules:
  0.0 140.4 jit_solution(18415970478756109349)
XLA Ops:
  0.0 0.7 collective-permute-start.3
  0.7 2.4 %split_w.1 = (bf16[2048,128]{1,0:T(8,128)(2,1)}, bf16[2048,128]{1,0:T(8,128)(2,1)}) custom-call(bf16[2048,256]{1,0:T(8,128)(2,1)} %w_ref.1), custom_call_target="tpu_custom_call" | custom-call | tf_op jit(solution)/shard_map/split_w/pallas_call | solution.py:341
  3.1 1.2 collective-permute-start
  4.3 0.3 collective-permute-start.2
  4.6 0.2 collective-permute-start.1
  4.9 1.2 collective-permute-done.2.refs_4_
  6.1 0.4 collective-permute-done.1.refs_3_
  6.5 0.0 collective-permute-done.3.refs_5_
  6.5 0.3 copy-done.6
  6.8 0.4 copy-done.7
  7.2 1.0 copy-done.4
  8.2 3.2 %split_qkv.1 = (bf16[2,256,256]{2,1,0:T(8,128)(2,1)}, bf16[2,256,256]{2,1,0:T(8,128)(2,1)}, bf16[2,256,512]{2,1,0:T(8,128)(2,1)}, bf16[2,256,512]{2,1,0:T(8,128)(2,1)}) custom-call(bf16[256,512]{1,0:T(8,128)(2,1)} %refs_0_, bf16[256,512]{1,0:T(8,128)(2,1)} %refs_1_.1, bf16[256,2048]{1,0:T(8,128)(2,1)} %refs_2_.1, bf16[256,512]{1,0:T(8,128)(2,1)} %copy-done.7, ...), custom_call_target="tpu_custom_call" | custom-call | tf_op jit(solution)/shard_map/split_qkv/pallas_call | solution.py:358
  11.4 1.4 %collective-permute-start.5 = (bf16[2,256,256]{2,1,0:T(8,128)(2,1)}, bf16[2,256,256]{2,1,0:T(8,128)(2,1)S(1)}, u32[]{:S(2)}, u32[]{:S(2)}) collective-permute-start(bf16[2,256,256]{2,1,0:T(8,128)(2,1)} %get-tuple-element.31), channel_id=1, source_target_pairs={{0,12},{1,13},{2,14},{3,15},{4,8},{5,9},{6,10},{7,11},{8,20},{9,21... | collective-permute-start | bytes 786440 | tf_op jit(solution)/shard_map/up_2/ppermute | solution.py:329
  12.8 1.3 collective-permute-start.4
  14.1 1.3 collective-permute-start.9
  15.3 1.6 %collective-permute-done = bf16[2048,128]{1,0:T(8,128)(2,1)} collective-permute-done((bf16[2048,128]{1,0:T(8,128)(2,1)}, bf16[2048,128]{1,0:T(8,128)(2,1)}, u32[]{:S(2)}, u32[]{:S(2)}) %collective-permute-start) | collective-permute-done | bytes 524320 | tf_op jit(solution)/shard_map/across_0_1/ppermute | solution.py:325
  17.0 1.1 pad_maximum_fusion.refs_0_
  18.1 1.3 collective-permute-start.12
  19.4 2.8 %collective-permute-done.5.refs_4_ = bf16[2,256,256]{2,1,0:T(8,128)(2,1)S(1)} collective-permute-done((bf16[2,256,256]{2,1,0:T(8,128)(2,1)}, bf16[2,256,256]{2,1,0:T(8,128)(2,1)S(1)}, u32[]{:S(2)}, u32[]{:S(2)}) %collective-permute-start.5) | collective-permute-done | bytes 262176 | tf_op jit(solution)/shard_map/up_2/ppermute | solution.py:329
  22.1 5.6 %collective-permute-done.4.refs_3_ = bf16[2,256,256]{2,1,0:T(8,128)(2,1)S(1)} collective-permute-done((bf16[2,256,256]{2,1,0:T(8,128)(2,1)}, bf16[2,256,256]{2,1,0:T(8,128)(2,1)S(1)}, u32[]{:S(2)}, u32[]{:S(2)}) %collective-permute-start.4) | collective-permute-done | bytes 262176 | tf_op jit(solution)/shard_map/up_0/ppermute | solution.py:329
  27.8 1.3 collective-permute-start.10
  29.1 1.3 collective-permute-start.11
  30.4 3.9 %collective-permute-start.7 = (bf16[4096,128]{1,0:T(8,128)(2,1)S(1)}, bf16[4096,128]{1,0:T(8,128)(2,1)S(1)}, u32[]{:S(2)}, u32[]{:S(2)}) collective-permute-start(bf16[4096,128]{1,0:T(8,128)(2,1)S(1)} %pad_maximum_fusion.refs_0_), channel_id=1, source_target_pairs={{0,16},{1,17},{2,18},{3,19},{4,20},{5,21},{6,22},{7,23},{8,24},{9,... | collective-permute-start | bytes 3145736 | tf_op jit(solution)/shard_map/between_2/ppermute | solution.py:333
  34.3 4.9 %collective-permute-done.12.refs_2_ = bf16[2,256,256]{2,1,0:T(8,128)(2,1)S(1)} collective-permute-done((bf16[2,256,256]{2,1,0:T(8,128)(2,1)}, bf16[2,256,256]{2,1,0:T(8,128)(2,1)S(1)}, u32[]{:S(2)}, u32[]{:S(2)}) %collective-permute-start.12) | collective-permute-done | bytes 262176 | tf_op jit(solution)/shard_map/across_2_0/ppermute | solution.py:325
  39.3 0.4 collective-permute-start.6
  39.7 7.7 %attention.3 = (f32[2,1024,128]{2,1,0:T(8,128)S(1)}, f32[2,1024,256]{2,1,0:T(8,128)S(1)}) custom-call(s32[4096]{0:T(1024)S(1)} %copy-done.2, s32[16,256]{1,0:T(8,128)S(1)} %reshape.2.segrow_ref, bf16[2,256,512]{2,1,0:T(8,128)(2,1)S(1)} %copy-done, bf16[2,256,256]{2,1,0:T(8,128)(2,1)S(1)} %copy-done.1, ...), custom_call_target="tpu_custom_call" | custom-call | tf_op jit(solution)/shard_map/attention/pallas_call | solution.py:211
  47.5 0.0 collective-permute-done.9.refs_0_.refs_1_
  47.5 9.6 %attention.4 = (f32[2,1024,128]{2,1,0:T(8,128)S(1)}, f32[2,1024,256]{2,1,0:T(8,128)S(1)}) custom-call(s32[4096]{0:T(1024)S(1)} %copy-done.2, s32[16,256]{1,0:T(8,128)S(1)} %reshape.2.segrow_ref, bf16[2,256,512]{2,1,0:T(8,128)(2,1)S(1)} %collective-permute-done.9.refs_0_.refs_1_, bf16[2,256,256]{2,1,0:T(8,128)(2,1)S(1)} %copy-done.1, ...), custom_call_target="tpu_custom_call" | custom-call | tf_op jit(solution)/shard_map/attention/pallas_call | solution.py:211
  57.1 0.0 collective-permute-done.10.refs_2_
  57.1 0.0 collective-permute-done.11.refs_3_
  57.1 2.7 %attention.5.refs_4_ = bf16[4,256,512]{2,1,0:T(8,128)(2,1)S(1)} custom-call(s32[4096]{0:T(1024)S(1)} %copy-done.2, s32[16,256]{1,0:T(8,128)S(1)} %reshape.2.segrow_ref, bf16[2,256,512]{2,1,0:T(8,128)(2,1)S(1)} %copy-done, bf16[2,256,512]{2,1,0:T(8,128)(2,1)S(1)} %collective-permute-done.9.refs_0_.refs_1_, ...), custom_call_target="tpu_custom_call" | custom-call | tf_op jit(solution)/shard_map/attention/pallas_call | solution.py:211
  59.8 1.3 collective-permute-start.18
  61.1 1.2 collective-permute-start.16
  62.3 0.2 collective-permute-start.14
  62.5 24.4 %collective-permute-done.7.refs_2_ = bf16[4096,128]{1,0:T(8,128)(2,1)S(1)} collective-permute-done((bf16[4096,128]{1,0:T(8,128)(2,1)S(1)}, bf16[4096,128]{1,0:T(8,128)(2,1)S(1)}, u32[]{:S(2)}, u32[]{:S(2)}) %collective-permute-start.7) | collective-permute-done | bytes 1048608 | tf_op jit(solution)/shard_map/between_2/ppermute | solution.py:333
  86.9 2.1 %collective-permute-start.13 = (bf16[4,256,512]{2,1,0:T(8,128)(2,1)S(1)}, bf16[4,256,512]{2,1,0:T(8,128)(2,1)S(1)}, u32[]{:S(2)}, u32[]{:S(2)}) collective-permute-start(bf16[4,256,512]{2,1,0:T(8,128)(2,1)S(1)} %attention.5.refs_4_), channel_id=1, source_target_pairs={{0,2},{1,3},{2,0},{3,1},{4,6},{5,7},{6,4},{7,5},{8,10},{9,11},{10,... | collective-permute-start | bytes 3145736 | tf_op jit(solution)/shard_map/across_1_0/ppermute | solution.py:325
  88.9 0.0 collective-permute-done.6.refs_1_
  88.9 0.0 collective-permute-start.8
  88.9 0.0 collective-permute-done.18.refs_10_
  89.0 0.1 collective-permute-start.19
  89.0 19.3 %collective-permute-done.16.refs_8_ = bf16[4,256,512]{2,1,0:T(8,128)(2,1)S(1)} collective-permute-done((bf16[4,256,512]{2,1,0:T(8,128)(2,1)S(1)}, bf16[4,256,512]{2,1,0:T(8,128)(2,1)S(1)}, u32[]{:S(2)}, u32[]{:S(2)}) %collective-permute-start.16) | collective-permute-done | bytes 1048608 | tf_op jit(solution)/shard_map/across_0_1/ppermute | solution.py:325
  108.3 0.5 collective-permute-start.17
  108.8 0.0 collective-permute-start.15
  108.8 0.0 collective-permute-done.13.refs_5_
  108.8 4.9 %collective-permute-done.8.refs_3_ = bf16[4096,128]{1,0:T(8,128)(2,1)S(1)} collective-permute-done((bf16[4096,128]{1,0:T(8,128)(2,1)S(1)}, bf16[4096,128]{1,0:T(8,128)(2,1)S(1)}, u32[]{:S(2)}, u32[]{:S(2)}) %collective-permute-start.8) | collective-permute-done | bytes 1048608 | tf_op jit(solution)/shard_map/between_1/ppermute | solution.py:333
  113.7 6.6 %project.1 = (bf16[256,256]{1,0:T(8,128)(2,1)S(1)}, bf16[256,256]{1,0:T(8,128)(2,1)S(1)}, bf16[256,256]{1,0:T(8,128)(2,1)S(1)}, bf16[256,256]{1,0:T(8,128)(2,1)S...) custom-call(bf16[4096,128]{1,0:T(8,128)(2,1)S(1)} %pad_maximum_fusio, ...), custom_call_target="tpu_custom_call" | custom-call | tf_op jit(solution)/shard_map/project/pallas_call | solution.py:396
  120.3 0.6 copy-done.3
  121.0 0.8 collective-permute-start.20
  121.8 0.2 collective-permute-start.21
  122.0 1.4 %collective-permute-start.22 = (bf16[256,256]{1,0:T(8,128)(2,1)S(1)}, bf16[256,256]{1,0:T(8,128)(2,1)S(1)}, u32[]{:S(2)}, u32[]{:S(2)}) collective-permute-start(bf16[256,256]{1,0:T(8,128)(2,1)S(1)} %get-tuple-element.44), channel_id=1, source_target_pairs={{0,6},{1,7},{2,4},{3,5},{4,2},{5,3},{6,0},{7,1},{8,14},{9,15},{10,... | collective-permute-start | bytes 393224 | tf_op jit(solution)/shard_map/across_3_0/ppermute | solution.py:325
  123.4 0.2 collective-permute-start.23
  123.6 1.6 %collective-permute-start.24 = (bf16[256,256]{1,0:T(8,128)(2,1)S(1)}, bf16[256,256]{1,0:T(8,128)(2,1)S(1)}, u32[]{:S(2)}, u32[]{:S(2)}) collective-permute-start(bf16[256,256]{1,0:T(8,128)(2,1)S(1)} %get-tuple-element.46), channel_id=1, source_target_pairs={{0,3},{1,2},{2,1},{3,0},{4,7},{5,6},{6,5},{7,4},{8,11},{9,10},{10,... | collective-permute-start | bytes 393224 | tf_op jit(solution)/shard_map/across_1_1/ppermute | solution.py:325
  125.2 0.0 collective-permute-done.20.refs_1_
  125.3 0.2 collective-permute-start.25
  125.4 1.5 %collective-permute-done.21.refs_2_ = bf16[256,256]{1,0:T(8,128)(2,1)S(1)} collective-permute-done((bf16[256,256]{1,0:T(8,128)(2,1)S(1)}, bf16[256,256]{1,0:T(8,128)(2,1)S(1)}, u32[]{:S(2)}, u32[]{:S(2)}) %collective-permute-start.21) | collective-permute-done | bytes 131104 | tf_op jit(solution)/shard_map/across_2_0/ppermute | solution.py:325
  126.9 1.2 collective-permute-start.26
  128.1 2.4 %collective-permute-done.22.refs_3_ = bf16[256,256]{1,0:T(8,128)(2,1)S(1)} collective-permute-done((bf16[256,256]{1,0:T(8,128)(2,1)S(1)}, bf16[256,256]{1,0:T(8,128)(2,1)S(1)}, u32[]{:S(2)}, u32[]{:S(2)}) %collective-permute-start.22) | collective-permute-done | bytes 131104 | tf_op jit(solution)/shard_map/across_3_0/ppermute | solution.py:325
  130.5 6.6 %collective-permute-done.24.refs_5_ = bf16[256,256]{1,0:T(8,128)(2,1)S(1)} collective-permute-done((bf16[256,256]{1,0:T(8,128)(2,1)S(1)}, bf16[256,256]{1,0:T(8,128)(2,1)S(1)}, u32[]{:S(2)}, u32[]{:S(2)}) %collective-permute-start.24) | collective-permute-done | bytes 131104 | tf_op jit(solution)/shard_map/across_1_1/ppermute | solution.py:325
  137.0 0.0 collective-permute-done.25.refs_6_
  137.0 0.0 collective-permute-done.26.refs_7_
  137.1 0.6 copy-done.12
  137.7 0.0 copy-done.13
  137.7 0.1 copy-done.14
  137.8 2.5 %place.1 = bf16[256,2048]{1,0:T(8,128)(2,1)} custom-call(bf16[256,256]{1,0:T(8,128)(2,1)} %copy-done.3, bf16[256,256]{1,0:T(8,128)(2,1)} %copy-done.8, bf16[256,256]{1,0:T(8,128)(2,1)} %copy-done.9, bf16[256,256]{1,0:T(8,128)(2,1)} %copy-done.10, bf16[256,256]{1,0:T(8,128)(2,1)} %copy-done.11, bf16[256,256]{1,0:T(8,128)(2,1)} %copy-done.12, ...), custom_call_target="tpu_custom_call" | custom-call | tf_op jit(solution)/shard_map/place/pallas_call | solution.py:418
  (29 shorter events, 0.1 us)
Async XLA Ops:
  0.0 6.5 %collective-permute-start.3 = (bf16[256,2048]{1,0:T(8,128)(2,1)}, bf16[256,2048]{1,0:T(8,128)(2,1)S(1)}, u32[]{:S(2)}, u32[]{:S(2)}) collective-permute-start(bf16[256,2048]{1,0:T(8,128)(2,1)} %refs_2_.1), channel_id=1, source_target_pairs={{0,2},{1,3},{2,0},{3,1},{4,6},{5,7},{6,4},{7,5},{8,10},{9,11},{10,... | collective-permute-start | bytes 3145736 | tf_op jit(solution)/shard_map/across_1_0/ppermute | solution.py:325
  3.1 13.9 %copy-start.5 = (bf16[2048,128]{1,0:T(8,128)(2,1)S(1)}, bf16[2048,128]{1,0:T(8,128)(2,1)}, u32[]{:S(2)}) copy-start(bf16[2048,128]{1,0:T(8,128)(2,1)} %get-tuple-element.27) | copy-start | bytes 1572868
  3.1 13.9 %collective-permute-start = (bf16[2048,128]{1,0:T(8,128)(2,1)}, bf16[2048,128]{1,0:T(8,128)(2,1)}, u32[]{:S(2)}, u32[]{:S(2)}) collective-permute-start(bf16[2048,128]{1,0:T(8,128)(2,1)} %get-tuple-element.28), channel_id=1, source_target_pairs={{0,1},{1,0},{2,3},{3,2},{4,5},{5,4},{6,7},{7,6},{8,9},{9,8},{10,11... | collective-permute-start | bytes 1572872 | tf_op jit(solution)/shard_map/across_0_1/ppermute | solution.py:325
  4.3 1.7 %collective-permute-start.2 = (bf16[256,512]{1,0:T(8,128)(2,1)}, bf16[256,512]{1,0:T(8,128)(2,1)S(1)}, u32[]{:S(2)}, u32[]{:S(2)}) collective-permute-start(bf16[256,512]{1,0:T(8,128)(2,1)} %refs_1_.1), channel_id=1, source_target_pairs={{0,2},{1,3},{2,0},{3,1},{4,6},{5,7},{6,4},{7,5},{8,10},{9,11},{10,... | collective-permute-start | bytes 786440 | tf_op jit(solution)/shard_map/across_1_0/ppermute | solution.py:325
  4.6 25.8 %copy-start.2 = (s32[4096]{0:T(1024)S(1)}, s32[4096]{0:T(1024)}, u32[]{:S(2)}) copy-start(s32[4096]{0:T(1024)} %seg_ref.5) | copy-start | bytes 49156
  4.6 1.8 %collective-permute-start.1 = (bf16[256,512]{1,0:T(8,128)(2,1)}, bf16[256,512]{1,0:T(8,128)(2,1)S(1)}, u32[]{:S(2)}, u32[]{:S(2)}) collective-permute-start(bf16[256,512]{1,0:T(8,128)(2,1)} %refs_0_), channel_id=1, source_target_pairs={{0,2},{1,3},{2,0},{3,1},{4,6},{5,7},{6,4},{7,5},{8,10},{9,11},{10,... | collective-permute-start | bytes 786440 | tf_op jit(solution)/shard_map/across_1_0/ppermute | solution.py:325
  6.1 0.7 copy-start.6
  6.5 0.7 copy-start.7
  7.2 1.0 copy-start.4
  11.3 28.4 %copy-start = (bf16[2,256,512]{2,1,0:T(8,128)(2,1)S(1)}, bf16[2,256,512]{2,1,0:T(8,128)(2,1)}, u32[]{:S(2)}) copy-start(bf16[2,256,512]{2,1,0:T(8,128)(2,1)} %get-tuple-element.33.refs_0_) | copy-start | bytes 1572868
  11.3 28.4 %copy-start.1 = (bf16[2,256,256]{2,1,0:T(8,128)(2,1)S(1)}, bf16[2,256,256]{2,1,0:T(8,128)(2,1)}, u32[]{:S(2)}) copy-start(bf16[2,256,256]{2,1,0:T(8,128)(2,1)} %get-tuple-element.30.refs_1_) | copy-start | bytes 786436
  11.4 10.8 %collective-permute-start.5 = (bf16[2,256,256]{2,1,0:T(8,128)(2,1)}, bf16[2,256,256]{2,1,0:T(8,128)(2,1)S(1)}, u32[]{:S(2)}, u32[]{:S(2)}) collective-permute-start(bf16[2,256,256]{2,1,0:T(8,128)(2,1)} %get-tuple-element.31), channel_id=1, source_target_pairs={{0,12},{1,13},{2,14},{3,15},{4,8},{5,9},{6,10},{7,11},{8,20},{9,21... | collective-permute-start | bytes 786440 | tf_op jit(solution)/shard_map/up_2/ppermute | solution.py:329
  12.8 15.0 %collective-permute-start.4 = (bf16[2,256,256]{2,1,0:T(8,128)(2,1)}, bf16[2,256,256]{2,1,0:T(8,128)(2,1)S(1)}, u32[]{:S(2)}, u32[]{:S(2)}) collective-permute-start(bf16[2,256,256]{2,1,0:T(8,128)(2,1)} %get-tuple-element.30.refs_1_), channel_id=1, source_target_pairs={{0,8},{1,9},{2,10},{3,11},{4,12},{5,13},{6,14},{7,15},{8,16},{9,17... | collective-permute-start | bytes 786440 | tf_op jit(solution)/shard_map/up_0/ppermute | solution.py:329
  14.1 33.4 %collective-permute-start.9 = (bf16[2,256,512]{2,1,0:T(8,128)(2,1)}, bf16[2,256,512]{2,1,0:T(8,128)(2,1)S(1)}, u32[]{:S(2)}, u32[]{:S(2)}) collective-permute-start(bf16[2,256,512]{2,1,0:T(8,128)(2,1)} %get-tuple-element.34), channel_id=1, source_target_pairs={{0,4},{1,5},{2,6},{3,7},{4,0},{5,1},{6,2},{7,3},{8,12},{9,13},{10,... | collective-permute-start | bytes 1572872 | tf_op jit(solution)/shard_map/across_2_0/ppermute | solution.py:325
  18.1 21.2 %collective-permute-start.12 = (bf16[2,256,256]{2,1,0:T(8,128)(2,1)}, bf16[2,256,256]{2,1,0:T(8,128)(2,1)S(1)}, u32[]{:S(2)}, u32[]{:S(2)}) collective-permute-start(bf16[2,256,256]{2,1,0:T(8,128)(2,1)} %get-tuple-element.31), channel_id=1, source_target_pairs={{0,4},{1,5},{2,6},{3,7},{4,0},{5,1},{6,2},{7,3},{8,12},{9,13},{10,... | collective-permute-start | bytes 786440 | tf_op jit(solution)/shard_map/across_2_0/ppermute | solution.py:325
  27.8 29.3 %collective-permute-start.10 = (bf16[2,256,256]{2,1,0:T(8,128)(2,1)S(1)}, bf16[2,256,256]{2,1,0:T(8,128)(2,1)S(1)}, u32[]{:S(2)}, u32[]{:S(2)}) collective-permute-start(bf16[2,256,256]{2,1,0:T(8,128)(2,1)S(1)} %collective-permute-done.4.refs_3_), channel_id=1, source_target_pairs={{0,8},{1,9},{2,10},{3,11},{4,12},{5,13},{6,14},{7,15},{8,16},{9,17... | collective-permute-start | bytes 786440 | tf_op jit(solution)/shard_map/up_0/ppermute | solution.py:329
  29.1 28.0 %collective-permute-start.11 = (bf16[2,256,256]{2,1,0:T(8,128)(2,1)S(1)}, bf16[2,256,256]{2,1,0:T(8,128)(2,1)}, u32[]{:S(2)}, u32[]{:S(2)}) collective-permute-start(bf16[2,256,256]{2,1,0:T(8,128)(2,1)S(1)} %collective-permute-done.5.refs_4_), channel_id=1, source_target_pairs={{0,8},{1,9},{2,10},{3,11},{4,12},{5,13},{6,14},{7,15},{8,16},{9,17... | collective-permute-start | bytes 786440 | tf_op jit(solution)/shard_map/up_0/ppermute | solution.py:329
  30.4 56.5 %collective-permute-start.7 = (bf16[4096,128]{1,0:T(8,128)(2,1)S(1)}, bf16[4096,128]{1,0:T(8,128)(2,1)S(1)}, u32[]{:S(2)}, u32[]{:S(2)}) collective-permute-start(bf16[4096,128]{1,0:T(8,128)(2,1)S(1)} %pad_maximum_fusion.refs_0_), channel_id=1, source_target_pairs={{0,16},{1,17},{2,18},{3,19},{4,20},{5,21},{6,22},{7,23},{8,24},{9,... | collective-permute-start | bytes 3145736 | tf_op jit(solution)/shard_map/between_2/ppermute | solution.py:333
  39.3 49.6 %collective-permute-start.6 = (bf16[4096,128]{1,0:T(8,128)(2,1)S(1)}, bf16[4096,128]{1,0:T(8,128)(2,1)S(1)}, u32[]{:S(2)}, u32[]{:S(2)}) collective-permute-start(bf16[4096,128]{1,0:T(8,128)(2,1)S(1)} %pad_maximum_fusion.refs_0_), channel_id=1, source_target_pairs={{0,8},{1,9},{2,10},{3,11},{4,12},{5,13},{6,14},{7,15},{8,0},{9,1},... | collective-permute-start | bytes 3145736 | tf_op jit(solution)/shard_map/between_1/ppermute | solution.py:333
  59.8 29.2 %collective-permute-start.18 = (bf16[4,256,512]{2,1,0:T(8,128)(2,1)S(1)}, bf16[4,256,512]{2,1,0:T(8,128)(2,1)S(1)}, u32[]{:S(2)}, u32[]{:S(2)}) collective-permute-start(bf16[4,256,512]{2,1,0:T(8,128)(2,1)S(1)} %attention.5.refs_4_), channel_id=1, source_target_pairs={{0,5},{1,4},{2,7},{3,6},{4,1},{5,0},{6,3},{7,2},{8,13},{9,12},{10,... | collective-permute-start | bytes 3145736 | tf_op jit(solution)/shard_map/across_2_1/ppermute | solution.py:325
  61.1 47.2 %collective-permute-start.16 = (bf16[4,256,512]{2,1,0:T(8,128)(2,1)S(1)}, bf16[4,256,512]{2,1,0:T(8,128)(2,1)S(1)}, u32[]{:S(2)}, u32[]{:S(2)}) collective-permute-start(bf16[4,256,512]{2,1,0:T(8,128)(2,1)S(1)} %attention.5.refs_4_), channel_id=1, source_target_pairs={{0,1},{1,0},{2,3},{3,2},{4,5},{5,4},{6,7},{7,6},{8,9},{9,8},{10,11... | collective-permute-start | bytes 3145736 | tf_op jit(solution)/shard_map/across_0_1/ppermute | solution.py:325
  62.3 46.4 %collective-permute-start.14 = (bf16[4,256,512]{2,1,0:T(8,128)(2,1)S(1)}, bf16[4,256,512]{2,1,0:T(8,128)(2,1)S(1)}, u32[]{:S(2)}, u32[]{:S(2)}) collective-permute-start(bf16[4,256,512]{2,1,0:T(8,128)(2,1)S(1)} %attention.5.refs_4_), channel_id=1, source_target_pairs={{0,4},{1,5},{2,6},{3,7},{4,0},{5,1},{6,2},{7,3},{8,12},{9,13},{10,... | collective-permute-start | bytes 3145736 | tf_op jit(solution)/shard_map/across_2_0/ppermute | solution.py:325
  86.9 22.0 %collective-permute-start.13 = (bf16[4,256,512]{2,1,0:T(8,128)(2,1)S(1)}, bf16[4,256,512]{2,1,0:T(8,128)(2,1)S(1)}, u32[]{:S(2)}, u32[]{:S(2)}) collective-permute-start(bf16[4,256,512]{2,1,0:T(8,128)(2,1)S(1)} %attention.5.refs_4_), channel_id=1, source_target_pairs={{0,2},{1,3},{2,0},{3,1},{4,6},{5,7},{6,4},{7,5},{8,10},{9,11},{10,... | collective-permute-start | bytes 3145736 | tf_op jit(solution)/shard_map/across_1_0/ppermute | solution.py:325
  88.9 24.8 %collective-permute-start.8 = (bf16[4096,128]{1,0:T(8,128)(2,1)S(1)}, bf16[4096,128]{1,0:T(8,128)(2,1)S(1)}, u32[]{:S(2)}, u32[]{:S(2)}) collective-permute-start(bf16[4096,128]{1,0:T(8,128)(2,1)S(1)} %collective-permute-done.7.refs_2_), channel_id=1, source_target_pairs={{0,8},{1,9},{2,10},{3,11},{4,12},{5,13},{6,14},{7,15},{8,0},{9,1},... | collective-permute-start | bytes 3145736 | tf_op jit(solution)/shard_map/between_1/ppermute | solution.py:333
  89.0 24.8 %collective-permute-start.19 = (bf16[4,256,512]{2,1,0:T(8,128)(2,1)S(1)}, bf16[4,256,512]{2,1,0:T(8,128)(2,1)S(1)}, u32[]{:S(2)}, u32[]{:S(2)}) collective-permute-start(bf16[4,256,512]{2,1,0:T(8,128)(2,1)S(1)} %collective-permute-done.18.refs_10_), channel_id=1, source_target_pairs={{0,2},{1,3},{2,0},{3,1},{4,6},{5,7},{6,4},{7,5},{8,10},{9,11},{10,... | collective-permute-start | bytes 3145736 | tf_op jit(solution)/shard_map/across_1_0/ppermute | solution.py:325
  108.3 5.4 %collective-permute-start.17 = (bf16[4,256,512]{2,1,0:T(8,128)(2,1)S(1)}, bf16[4,256,512]{2,1,0:T(8,128)(2,1)S(1)}, u32[]{:S(2)}, u32[]{:S(2)}) collective-permute-start(bf16[4,256,512]{2,1,0:T(8,128)(2,1)S(1)} %collective-permute-done.16.refs_8_), channel_id=1, source_target_pairs={{0,2},{1,3},{2,0},{3,1},{4,6},{5,7},{6,4},{7,5},{8,10},{9,11},{10,... | collective-permute-start | bytes 3145736 | tf_op jit(solution)/shard_map/across_1_0/ppermute | solution.py:325
  108.8 4.9 %collective-permute-start.15 = (bf16[4,256,512]{2,1,0:T(8,128)(2,1)S(1)}, bf16[4,256,512]{2,1,0:T(8,128)(2,1)S(1)}, u32[]{:S(2)}, u32[]{:S(2)}) collective-permute-start(bf16[4,256,512]{2,1,0:T(8,128)(2,1)S(1)} %collective-permute-done.14.refs_6_), channel_id=1, source_target_pairs={{0,2},{1,3},{2,0},{3,1},{4,6},{5,7},{6,4},{7,5},{8,10},{9,11},{10,... | collective-permute-start | bytes 3145736 | tf_op jit(solution)/shard_map/across_1_0/ppermute | solution.py:325
  120.3 0.7 copy-start.3
  121.0 4.3 %collective-permute-start.20 = (bf16[256,256]{1,0:T(8,128)(2,1)S(1)}, bf16[256,256]{1,0:T(8,128)(2,1)S(1)}, u32[]{:S(2)}, u32[]{:S(2)}) collective-permute-start(bf16[256,256]{1,0:T(8,128)(2,1)S(1)} %get-tuple-element.42), channel_id=1, source_target_pairs={{0,2},{1,3},{2,0},{3,1},{4,6},{5,7},{6,4},{7,5},{8,10},{9,11},{10,... | collective-permute-start | bytes 393224 | tf_op jit(solution)/shard_map/across_1_0/ppermute | solution.py:325
  121.8 5.1 %collective-permute-start.21 = (bf16[256,256]{1,0:T(8,128)(2,1)S(1)}, bf16[256,256]{1,0:T(8,128)(2,1)S(1)}, u32[]{:S(2)}, u32[]{:S(2)}) collective-permute-start(bf16[256,256]{1,0:T(8,128)(2,1)S(1)} %get-tuple-element.43), channel_id=1, source_target_pairs={{0,4},{1,5},{2,6},{3,7},{4,0},{5,1},{6,2},{7,3},{8,12},{9,13},{10,... | collective-permute-start | bytes 393224 | tf_op jit(solution)/shard_map/across_2_0/ppermute | solution.py:325
  122.0 8.5 %collective-permute-start.22 = (bf16[256,256]{1,0:T(8,128)(2,1)S(1)}, bf16[256,256]{1,0:T(8,128)(2,1)S(1)}, u32[]{:S(2)}, u32[]{:S(2)}) collective-permute-start(bf16[256,256]{1,0:T(8,128)(2,1)S(1)} %get-tuple-element.44), channel_id=1, source_target_pairs={{0,6},{1,7},{2,4},{3,5},{4,2},{5,3},{6,0},{7,1},{8,14},{9,15},{10,... | collective-permute-start | bytes 393224 | tf_op jit(solution)/shard_map/across_3_0/ppermute | solution.py:325
  123.4 7.1 %collective-permute-start.23 = (bf16[256,256]{1,0:T(8,128)(2,1)S(1)}, bf16[256,256]{1,0:T(8,128)(2,1)S(1)}, u32[]{:S(2)}, u32[]{:S(2)}) collective-permute-start(bf16[256,256]{1,0:T(8,128)(2,1)S(1)} %get-tuple-element.45), channel_id=1, source_target_pairs={{0,1},{1,0},{2,3},{3,2},{4,5},{5,4},{6,7},{7,6},{8,9},{9,8},{10,11... | collective-permute-start | bytes 393224 | tf_op jit(solution)/shard_map/across_0_1/ppermute | solution.py:325
  123.6 13.4 %collective-permute-start.24 = (bf16[256,256]{1,0:T(8,128)(2,1)S(1)}, bf16[256,256]{1,0:T(8,128)(2,1)S(1)}, u32[]{:S(2)}, u32[]{:S(2)}) collective-permute-start(bf16[256,256]{1,0:T(8,128)(2,1)S(1)} %get-tuple-element.46), channel_id=1, source_target_pairs={{0,3},{1,2},{2,1},{3,0},{4,7},{5,6},{6,5},{7,4},{8,11},{9,10},{10,... | collective-permute-start | bytes 393224 | tf_op jit(solution)/shard_map/across_1_1/ppermute | solution.py:325
  125.3 11.8 %copy-start.8 = (bf16[256,256]{1,0:T(8,128)(2,1)}, bf16[256,256]{1,0:T(8,128)(2,1)S(1)}, u32[]{:S(2)}) copy-start(bf16[256,256]{1,0:T(8,128)(2,1)S(1)} %collective-permute-done.20.refs_1_) | copy-start | bytes 393220
  125.3 11.8 %collective-permute-start.25 = (bf16[256,256]{1,0:T(8,128)(2,1)S(1)}, bf16[256,256]{1,0:T(8,128)(2,1)S(1)}, u32[]{:S(2)}, u32[]{:S(2)}) collective-permute-start(bf16[256,256]{1,0:T(8,128)(2,1)S(1)} %get-tuple-element.47), channel_id=1, source_target_pairs={{0,5},{1,4},{2,7},{3,6},{4,1},{5,0},{6,3},{7,2},{8,13},{9,12},{10,... | collective-permute-start | bytes 393224 | tf_op jit(solution)/shard_map/across_2_1/ppermute | solution.py:325
  126.9 10.2 %copy-start.9 = (bf16[256,256]{1,0:T(8,128)(2,1)}, bf16[256,256]{1,0:T(8,128)(2,1)S(1)}, u32[]{:S(2)}) copy-start(bf16[256,256]{1,0:T(8,128)(2,1)S(1)} %collective-permute-done.21.refs_2_) | copy-start | bytes 393220
  126.9 10.2 %collective-permute-start.26 = (bf16[256,256]{1,0:T(8,128)(2,1)S(1)}, bf16[256,256]{1,0:T(8,128)(2,1)S(1)}, u32[]{:S(2)}, u32[]{:S(2)}) collective-permute-start(bf16[256,256]{1,0:T(8,128)(2,1)S(1)} %get-tuple-element.48), channel_id=1, source_target_pairs={{0,7},{1,6},{2,5},{3,4},{4,3},{5,2},{6,1},{7,0},{8,15},{9,14},{10,... | collective-permute-start | bytes 393224 | tf_op jit(solution)/shard_map/across_3_1/ppermute | solution.py:325
  130.5 6.6 %copy-start.10 = (bf16[256,256]{1,0:T(8,128)(2,1)}, bf16[256,256]{1,0:T(8,128)(2,1)S(1)}, u32[]{:S(2)}) copy-start(bf16[256,256]{1,0:T(8,128)(2,1)S(1)} %collective-permute-done.22.refs_3_) | copy-start | bytes 393220
  130.5 6.6 %copy-start.11 = (bf16[256,256]{1,0:T(8,128)(2,1)}, bf16[256,256]{1,0:T(8,128)(2,1)S(1)}, u32[]{:S(2)}) copy-start(bf16[256,256]{1,0:T(8,128)(2,1)S(1)} %collective-permute-done.23.refs_4_) | copy-start | bytes 393220
  137.0 0.7 copy-start.12
  137.0 0.7 copy-start.13
  137.1 0.8 copy-start.14

commit v4 on v3

--- a/solution.py
+++ b/solution.py
@@ -34,17 +34,22 @@
     return lax.bitwise_xor(z // (planes // attn), y)
 
 
-def split_qkv_kernel(group, *refs):
+def split_kv_kernel(group, *refs):
     g = place_in(group)[1]
-    kv_outs, q_outs = refs[6 : 6 + group // 2], refs[6 + group // 2 :]
-    width = q_outs[0].shape[2]
     for core in range(2):
-        k_ref, v_ref, q_ref = refs[3 * core : 3 * core + 3]
-        for o in range(group // 2):
+        k_ref, v_ref = refs[2 * core : 2 * core + 2]
+        for o, out in enumerate(refs[4:]):
             at = pl.ds(pl.multiple_of(xor(g, 2 * o) * HEAD, HEAD), HEAD)
-            kv_outs[o][core, :, :HEAD] = k_ref[:, at]
-            kv_outs[o][core, :, HEAD:] = v_ref[:, at]
-            q_outs[o][core] = q_ref[:, pl.ds(pl.multiple_of(xor(g, 2 * o) * width, width), width)]
+            out[core, :, :HEAD] = k_ref[:, at]
+            out[core, :, HEAD:] = v_ref[:, at]
+
+
+def split_q_kernel(group, *refs):
+    g = place_in(group)[1]
+    width = refs[2].shape[2]
+    for core in range(2):
+        for o, out in enumerate(refs[2:]):
+            out[core] = refs[core][:, pl.ds(pl.multiple_of(xor(g, 2 * o) * width, width), width)]
 
 
 def split_w_kernel(group, w_ref, *outs):
@@ -66,6 +71,7 @@
     state_refs = [take(2) for _ in pairs] if carried else None
     out_refs = take(1 if final else 2)
     q_s, k_s, v_s, m_own, acc_own, seg_s, sem = refs
+    unit = k_s.shape[1] // segrow_ref.shape[1]
     n = segrow_ref.shape[1]
     rows = heads * n
     lanes = n // HEAD
@@ -76,13 +82,13 @@
             copies.append((q_part, q_s.at[k, pl.ds(h * n, n), :]))
     for i in range(n_kv):
         kv = kv_refs[i // 2].at[i % 2]
-        at = pl.ds(i % 2 * n, n)
-        copies.append((kv.at[:, pl.ds(0, HEAD)], k_s.at[i // 2, at, :]))
-        copies.append((kv.at[:, pl.ds(HEAD, HEAD)], v_s.at[i // 2, at, pl.ds(0, HEAD)]))
+        at = pl.ds(i % unit * n, n)
+        copies.append((kv.at[:, pl.ds(0, HEAD)], k_s.at[i // unit, at, :]))
+        copies.append((kv.at[:, pl.ds(HEAD, HEAD)], v_s.at[i // unit, at, pl.ds(0, HEAD)]))
     copies = [pltpu.make_async_copy(a, b, sem.at[i]) for i, (a, b) in enumerate(copies)]
     for c in copies:
         c.start()
-    v_s[:, :, HEAD:] = jnp.ones((n_kv // 2, 2 * n, HEAD), jnp.bfloat16)
+    v_s[:, :, HEAD:] = jnp.ones((n_kv // unit, unit * n, HEAD), jnp.bfloat16)
     for c in copies:
         c.wait()
 
@@ -97,20 +103,20 @@
         q_first, q_last = seg_ref[qp * n], seg_ref[qp * n + n - 1]
 
         def piece(i, which):
-            place = lax.bitwise_xor(g, 2 * lax.rem(i, group // 2) + which)
-            kp = (plane - back[0] - i // (group // 2)) * group + place
+            i = i * unit + which
+            kp = (plane - back[0] - i // group) * group + lax.bitwise_xor(g, lax.rem(i, group))
             safe = jnp.maximum(kp, 0)
             active = (kp >= 0) & (kp <= qp) & (seg_ref[safe * n + n - 1] >= q_first)
             whole = (kp >= 0) & (kp < qp) & (seg_ref[safe * n] == q_last)
             return kp, safe, active, whole
 
         def needed(i):
-            return piece(i, 0)[2] | piece(i, 1)[2]
+            return functools.reduce(jnp.logical_or, [piece(i, which)[2] for which in range(unit)])
 
         def mix(i, carry):
-            pieces = [piece(i, which) for which in range(2)]
-            active = pieces[0][2] | pieces[1][2]
-            whole = pieces[0][3] & pieces[1][3]
+            pieces = [piece(i, which) for which in range(unit)]
+            active = needed(i)
+            whole = functools.reduce(jnp.logical_and, [p[3] for p in pieces])
 
             def scores(h):
                 return lax.dot_general(
@@ -134,7 +140,7 @@
                 top = jnp.maximum(old, jnp.max(s, axis=1, keepdims=True))
                 m_s[row] = top
                 shrink = jnp.exp2((old - top) * scale)
-                top = jnp.concatenate([top] * (2 * lanes), axis=1)
+                top = jnp.concatenate([top] * (unit * lanes), axis=1)
                 weights = jnp.exp2((s - top) * scale).astype(jnp.bfloat16)
                 found = jnp.dot(weights, v_s[i], preferred_element_type=jnp.float32)
                 acc_s[row] = acc_s[row] * jnp.concatenate([shrink] * 2, axis=1) + found
@@ -175,11 +181,11 @@
             else:
                 m_s[...] = jnp.full(m_s.shape, NEGATIVE, jnp.float32)
                 acc_s[...] = jnp.zeros(acc_s.shape, jnp.float32)
-            lax.fori_loop(0, n_kv // 2, mix, 0)
+            lax.fori_loop(0, n_kv // unit, mix, 0)
 
         if carried:
             any_needed = lax.fori_loop(
-                0, n_kv // 2, lambda i, seen: seen | needed(i).astype(jnp.int32), jnp.int32(0)
+                0, n_kv // unit, lambda i, seen: seen | needed(i).astype(jnp.int32), jnp.int32(0)
             )
 
             @pl.when(any_needed > 0)
@@ -208,6 +214,7 @@
     else:
         out_shape = [jax.ShapeDtypeStruct((n_q, rows, lanes), jnp.float32) for lanes in (HEAD, 2 * HEAD)]
     carried = list(carried or ())
+    unit = 1 if carried else 2
     found = pl.pallas_call(
         functools.partial(attention_kernel, group, heads, back, pairs, bool(carried), final),
         out_shape=out_shape,
@@ -215,8 +222,8 @@
         out_specs=[VMEM] * len(out_shape),
         scratch_shapes=[
             pltpu.VMEM((n_q, rows, HEAD), jnp.bfloat16),
-            pltpu.VMEM((n_kv // 2, 2 * n, HEAD), jnp.bfloat16),
-            pltpu.VMEM((n_kv // 2, 2 * n, 2 * HEAD), jnp.bfloat16),
+            pltpu.VMEM((n_kv // unit, unit * n, HEAD), jnp.bfloat16),
+            pltpu.VMEM((n_kv // unit, unit * n, 2 * HEAD), jnp.bfloat16),
             pltpu.VMEM((rows, HEAD), jnp.float32),
             pltpu.VMEM((rows, 2 * HEAD), jnp.float32),
             pltpu.VMEM((n, HEAD), jnp.float32),
@@ -233,49 +240,33 @@
     refs = list(refs)
     take = lambda count: [refs.pop(0) for _ in range(count)]
     w_refs, a_refs, out_refs = take(planes), take(group * attn), take(group * attn)
-    a_s, w_s, a_sem, w_sem = refs
     z, _, y = place_in(group)
-    n, width = a_refs[0].shape[1:]
     cols = w_refs[0].shape[1]
     rounds = planes // attn
-    aligned = cols % HEAD == 0
-
-    def a_copies(k):
-        return [
-            pltpu.make_async_copy(
-                a_refs[i].at[(i % group) ^ k], a_s.at[k, :, pl.ds(i * width, width)], a_sem.at[k]
-            )
-            for i in range(attn * group)
-        ]
-
-    w_copies = []
-    for turn in range(attn):
-        to = xor(turn_of(z, y, planes, attn), turn)
-        for r in range(rounds):
-            place = to * rounds + r
-            into = w_s.at[:, pl.ds(pl.multiple_of(place * cols, cols), cols)] if aligned else w_s.at[place]
-            w_copies.append(pltpu.make_async_copy(w_refs[r + turn * rounds], into, w_sem))
-
-    for copy in a_copies(0) + w_copies:
-        copy.start()
-    for k in range(1, group):
-        for copy in a_copies(k):
-            copy.start()
-    for copy in w_copies:
-        copy.wait()
+    turn = turn_of(z, y, planes, attn)
     for k in range(group):
-        for copy in a_copies(k):
-            copy.wait()
-        if aligned:
-            found = jnp.dot(a_s[k], w_s[...], preferred_element_type=jnp.float32).astype(jnp.bfloat16)
-            for to in range(attn):
-                out_refs[to * group + k][...] = found[:, to * rounds * cols : (to + 1) * rounds * cols]
+        rows = jnp.concatenate([a_refs[i][(i % group) ^ k] for i in range(attn * group)], axis=1)
+        dot = lambda weights: jnp.dot(rows, weights, preferred_element_type=jnp.float32).astype(jnp.bfloat16)
+        if cols % HEAD == 0:
+            found = dot(jnp.concatenate([w_ref[...] for w_ref in w_refs], axis=1))
+            found = [found[:, t * rounds * cols : (t + 1) * rounds * cols] for t in range(attn)]
         else:
-            for to in range(attn):
-                for r in range(rounds):
-                    out_refs[to * group + k][:, r * cols : (r + 1) * cols] = jnp.dot(
-                        a_s[k], w_s[to * rounds + r], preferred_element_type=jnp.float32
-                    ).astype(jnp.bfloat16)
+            found = [
+                jnp.concatenate([dot(w_ref[...]) for w_ref in w_refs[t * rounds : (t + 1) * rounds]], axis=1)
+                for t in range(attn)
+            ]
+        for to in range(attn):
+            here = xor(turn, to)
+            mine = found[0]
+            for t in range(1, attn):
+                mine = jnp.where(here == t, found[t], mine)
+            out_refs[to * group + k][...] = mine
+
+
+def farthest_first(attn, group):
+    return sorted(((m, k) for m in range(attn) for k in range(group)), key=lambda at: (at[1] > 1, at[0] > 0, at[1]))[
+        ::-1
+    ]
 
 
 def column_of(group, attn, planes, r, m, k, cols):
@@ -289,10 +280,9 @@
     rounds = planes // attn
     cols = refs[0].shape[1] // rounds
     for r in range(rounds):
-        for m in range(attn):
-            for k in range(group):
-                at = pl.multiple_of(column_of(group, attn, planes, r, m, k, cols), cols)
-                out_ref[:, pl.ds(at, cols)] = refs[m * group + k][:, r * cols : (r + 1) * cols]
+        for (m, k), ref in zip(farthest_first(attn, group), refs):
+            at = pl.multiple_of(column_of(group, attn, planes, r, m, k, cols), cols)
+            out_ref[:, pl.ds(at, cols)] = ref[:, r * cols : (r + 1) * cols]
 
 
 def shards(dense, attn, queries, keys, values, segments, out_weight):
@@ -354,17 +344,24 @@
     others = [own[0]] + [across(own[m], 0, m) for m in range(1, attn)]
 
     keys, *own = after(keys, *own)
-    near = [keys, values, queries]
-    split = pl.pallas_call(
-        functools.partial(split_qkv_kernel, group),
-        out_shape=[bf16(2, n, 2 * HEAD)] * (group // 2) + [bf16(2, n, width)] * (group // 2),
-        in_specs=[VMEM] * 6,
-        out_specs=[VMEM] * group,
-        name="split_qkv",
-    )(*near, *[across(array, 1, 0) for array in near])
-    kv, q = split[: group // 2], split[group // 2 :]
+    kv = pl.pallas_call(
+        functools.partial(split_kv_kernel, group),
+        out_shape=[bf16(2, n, 2 * HEAD)] * (group // 2),
+        in_specs=[VMEM] * 4,
+        out_specs=[VMEM] * (group // 2),
+        name="split_kv",
+    )(keys, values, across(keys, 1, 0), across(values, 1, 0))
     links = [[kv[0]] + [across(kv[o], 2 * o, 0) for o in range(1, group // 2)]]
     links.append([up(kv[o], 2 * o) for o in range(group // 2)])
+
+    queries, far_queries, *others = after(queries, across(queries, 1, 0), *others)
+    q = pl.pallas_call(
+        functools.partial(split_q_kernel, group),
+        out_shape=[bf16(2, n, width)] * (group // 2),
+        in_specs=[VMEM] * 2,
+        out_specs=[VMEM] * (group // 2),
+        name="split_q",
+    )(queries, far_queries)
     q = [q[0]] + [across(q[o], 2 * o, 0) for o in range(1, group // 2)]
 
     own = jnp.concatenate(others)
@@ -392,27 +389,19 @@
             [attended if o == m == 0 else across(attended, 2 * o, m) for o in range(group // 2)]
         )
 
-    w_shape = (attn * group * width, planes * cols) if cols % HEAD == 0 else (planes, attn * group * width, cols)
     found = pl.pallas_call(
         functools.partial(project_kernel, group, attn, planes),
         out_shape=[bf16(n, rounds * cols)] * (attn * group),
-        in_specs=[ANY] * (planes + group * attn),
+        in_specs=[VMEM] * (planes + group * attn),
         out_specs=[VMEM] * (attn * group),
-        scratch_shapes=[
-            pltpu.VMEM((group, n, attn * group * width), jnp.bfloat16),
-            pltpu.VMEM(w_shape, jnp.bfloat16),
-            pltpu.SemaphoreType.DMA((group,)),
-            pltpu.SemaphoreType.DMA,
-        ],
         compiler_params=params(28),
         cost_estimate=LIGHT,
         name="project",
     )(*[blocks[i] for i in range(planes)], *everything)
-    placed = []
-    for m in range(attn):
-        for k in range(group):
-            piece = found[m * group + k]
-            placed.append(piece if m == k == 0 else across(piece, k, m))
+    placed = [
+        found[m * group + k] if m == k == 0 else across(found[m * group + k], k, m)
+        for m, k in farthest_first(attn, group)
+    ]
 
     if cols % HEAD == 0:
         return pl.pallas_call(
@@ -424,11 +413,9 @@
         )(*placed)
     out = jnp.zeros((n, planes * group * cols), jnp.bfloat16)
     for r in range(rounds):
-        for m in range(attn):
-            for k in range(group):
-                part = placed[m * group + k][:, r * cols : (r + 1) * cols]
-                at = column_of(group, attn, planes, r, m, k, cols)
-                out = lax.dynamic_update_slice_in_dim(out, part, at, 1)
+        for (m, k), piece in zip(farthest_first(attn, group), placed):
+            at = column_of(group, attn, planes, r, m, k, cols)
+            out = lax.dynamic_update_slice_in_dim(out, piece[:, r * cols : (r + 1) * cols], at, 1)
     return out
 
 

time: 143 us -> 136 us (0.951); the launches traced: 140 us -> 136 us
  waiting for transfers between devices: 75.6 us -> 71.3 us
  Pallas kernels: 34.7 us -> 32 us
    ppermute x3, waiting for transfers between devices: 29.3 us -> 42.2 us  [between(): return lax.ppermute(array, AXES, pairs(lambda z, g, y: (z ^ i, g, y)))]
    ppermute x20, waiting for transfers between devices: 37.9 us -> 26.9 us  [across(): return lax.ppermute(array, AXES, pairs(lambda z, g, y: (z, g ^ j, y ^ m)))]
    ppermute x4, waiting for transfers between devices: 8.43 us -> 2.14 us  [up(): return lax.ppermute(array, AXES, pairs(lambda z, g, y: (z + 1, g ^ j, y)))]
    pallas_call x3, Pallas kernels: 20 us -> 17.9 us  [attention(): pl.pallas_call(functools.partial(attention_kernel, group, heads, back, pa...]
    pallas_call x1, Pallas kernels: 6.57 us -> 4.49 us  [shards(): pl.pallas_call(functools.partial(project_kernel, group, attn, planes), ou...]
    pallas_call x1 -> x2, Pallas kernels: 3.18 us -> 4.71 us  [the longest x1 2.61 us: shards(): pl.pallas_call(functools.partial(split_q_kernel, group), out_shape=[bf16(...]
where the time goes in v4:
time: 136 us
  waiting for transfers between devices  71.3 us (52%)
  Pallas kernels  32 us (24%)
  starting transfers between devices  26.7 us (20%)
  local copies, waits for them, and re-layouts  4.14 us (3%)
    ppermute x3, waiting for transfers between devices, between(): return lax.ppermute(array, AXES, pairs(lambda z, g, y: (z ^ i, g, y)))  42.2 us
    ppermute x20, waiting for transfers between devices, across(): return lax.ppermute(array, AXES, pairs(lambda z, g, y: (z, g ^ j, y ^ m)))  26.9 us
    pallas_call x3, Pallas kernels, attention(): pl.pallas_call(functools.partial(attention_kernel, group, heads, back, pa...  17.9 us
    ppermute x20, starting transfers between devices, across(): return lax.ppermute(array, AXES, pairs(lambda z, g, y: (z, g ^ j, y ^ m)))  16.6 us
    ppermute x4, starting transfers between devices, up(): return lax.ppermute(array, AXES, pairs(lambda z, g, y: (z + 1, g ^ j, y)))  5.28 us
    ppermute x3, starting transfers between devices, between(): return lax.ppermute(array, AXES, pairs(lambda z, g, y: (z ^ i, g, y)))  4.81 us
    pallas_call x1, Pallas kernels, shards(): pl.pallas_call(functools.partial(project_kernel, group, attn, planes), ou...  4.49 us
    unnamed x30, local copies, waits for them, and re-layouts  4.13 us
  transfers between devices with their start and end apart: 27, of which 12 were waited for; matrix products, arithmetic and copies ran while one was open for 1% of the time, Pallas kernels for 18%

profile of v4, /device:TPU:25, one launch (start us, length us, event | category | flops | bytes accessed | tf_op | source)
XLA Modules:
  0.0 135.6 jit_solution(11993555602312605800)
XLA Ops:
  0.0 0.7 collective-permute-start
  0.7 2.4 %split_w.1 = (bf16[2048,128]{1,0:T(8,128)(2,1)}, bf16[2048,128]{1,0:T(8,128)(2,1)}) custom-call(bf16[2048,256]{1,0:T(8,128)(2,1)} %w_ref.1), custom_call_target="tpu_custom_call" | custom-call | tf_op jit(solution)/shard_map/split_w/pallas_call | solution.py:331
  3.0 1.2 collective-permute-start.1
  4.3 0.3 collective-permute-start.3
  4.6 0.2 collective-permute-start.2
  4.8 1.2 collective-permute-done.3.refs_3_
  6.0 0.4 collective-permute-done.2.refs_2_
  6.4 0.3 copy-done.6
  6.7 0.7 copy-done.7
  7.5 2.1 %split_kv.1 = (bf16[2,256,256]{2,1,0:T(8,128)(2,1)}, bf16[2,256,256]{2,1,0:T(8,128)(2,1)}) custom-call(bf16[256,512]{1,0:T(8,128)(2,1)} %refs_0_, bf16[256,512]{1,0:T(8,128)(2,1)} %refs_1_.1, bf16[256,512]{1,0:T(8,128)(2,1)} %copy-done.7, bf16[256,512]{1,0:T(8,128)(2,1)} %copy-done.6), custom_call_target="tpu_custom_call" | custom-call | tf_op jit(solution)/shard_map/split_kv/pallas_call | solution.py:347
  9.5 1.2 collective-permute-start.12
  10.8 1.3 collective-permute-start.5
  12.0 0.0 copy-start.2
  12.1 1.4 %collective-permute-start.4 = (bf16[2,256,256]{2,1,0:T(8,128)(2,1)}, bf16[2,256,256]{2,1,0:T(8,128)(2,1)S(1)}, u32[]{:S(2)}, u32[]{:S(2)}) collective-permute-start(bf16[2,256,256]{2,1,0:T(8,128)(2,1)} %get-tuple-element.36.refs_1_), channel_id=1, source_target_pairs={{0,8},{1,9},{2,10},{3,11},{4,12},{5,13},{6,14},{7,15},{8,16},{9,17... | collective-permute-start | bytes 786440 | tf_op jit(solution)/shard_map/up_0/ppermute | solution.py:319
  13.5 3.3 %collective-permute-done.1 = bf16[2048,128]{1,0:T(8,128)(2,1)S(1)} collective-permute-done((bf16[2048,128]{1,0:T(8,128)(2,1)}, bf16[2048,128]{1,0:T(8,128)(2,1)S(1)}, u32[]{:S(2)}, u32[]{:S(2)}) %collective-permute-start.1) | collective-permute-done | bytes 524320 | tf_op jit(solution)/shard_map/across_0_1/ppermute | solution.py:315
  16.8 0.0 collective-permute-done.refs_1_
  16.8 0.8 copy-done.5
  17.6 1.0 copy-done.4
  18.6 2.6 %split_q.1 = (bf16[2,256,512]{2,1,0:T(8,128)(2,1)}, bf16[2,256,512]{2,1,0:T(8,128)(2,1)}) custom-call(bf16[256,2048]{1,0:T(8,128)(2,1)} %refs_0_.1, bf16[256,2048]{1,0:T(8,128)(2,1)} %copy-done.4), custom_call_target="tpu_custom_call" | custom-call | tf_op jit(solution)/shard_map/split_q/pallas_call | solution.py:358
  21.2 1.2 collective-permute-start.9
  22.4 1.3 pad_maximum_fusion.refs_0_
  23.7 2.1 %collective-permute-done.4.refs_3_ = bf16[2,256,256]{2,1,0:T(8,128)(2,1)S(1)} collective-permute-done((bf16[2,256,256]{2,1,0:T(8,128)(2,1)}, bf16[2,256,256]{2,1,0:T(8,128)(2,1)S(1)}, u32[]{:S(2)}, u32[]{:S(2)}) %collective-permute-start.4) | collective-permute-done | bytes 262176 | tf_op jit(solution)/shard_map/up_0/ppermute | solution.py:319
  25.8 1.3 collective-permute-start.10
  27.1 1.3 collective-permute-start.11
  28.4 3.9 %collective-permute-start.7 = (bf16[4096,128]{1,0:T(8,128)(2,1)S(1)}, bf16[4096,128]{1,0:T(8,128)(2,1)S(1)}, u32[]{:S(2)}, u32[]{:S(2)}) collective-permute-start(bf16[4096,128]{1,0:T(8,128)(2,1)S(1)} %pad_maximum_fusion.refs_0_), channel_id=1, source_target_pairs={{0,16},{1,17},{2,18},{3,19},{4,20},{5,21},{6,22},{7,23},{8,24},{9,... | collective-permute-start | bytes 3145736 | tf_op jit(solution)/shard_map/between_2/ppermute | solution.py:323
  32.4 0.9 collective-permute-start.6
  33.3 6.1 %attention.3 = (f32[2,1024,128]{2,1,0:T(8,128)S(1)}, f32[2,1024,256]{2,1,0:T(8,128)S(1)}) custom-call(s32[4096]{0:T(1024)S(1)} %copy-done.2, s32[16,256]{1,0:T(8,128)S(1)} %reshape.2.segrow_ref, bf16[2,256,512]{2,1,0:T(8,128)(2,1)S(1)} %copy-done, bf16[2,256,256]{2,1,0:T(8,128)(2,1)S(1)} %copy-done.1, ...), custom_call_target="tpu_custom_call" | custom-call | tf_op jit(solution)/shard_map/attention/pallas_call | solution.py:218
  39.3 0.0 collective-permute-done.9.refs_0_.refs_1_
  39.4 6.1 %attention.4 = (f32[2,1024,128]{2,1,0:T(8,128)S(1)}, f32[2,1024,256]{2,1,0:T(8,128)S(1)}) custom-call(s32[4096]{0:T(1024)S(1)} %copy-done.2, s32[16,256]{1,0:T(8,128)S(1)} %reshape.2.segrow_ref, bf16[2,256,512]{2,1,0:T(8,128)(2,1)S(1)} %collective-permute-done.9.refs_0_.refs_1_, bf16[2,256,256]{2,1,0:T(8,128)(2,1)S(1)} %copy-done.1, ...), custom_call_target="tpu_custom_call" | custom-call | tf_op jit(solution)/shard_map/attention/pallas_call | solution.py:218
  45.5 0.0 collective-permute-done.11.refs_3_
  45.5 5.8 %attention.5.refs_4_ = bf16[4,256,512]{2,1,0:T(8,128)(2,1)S(1)} custom-call(s32[4096]{0:T(1024)S(1)} %copy-done.2, s32[16,256]{1,0:T(8,128)S(1)} %reshape.2.segrow_ref, bf16[2,256,512]{2,1,0:T(8,128)(2,1)S(1)} %copy-done, bf16[2,256,512]{2,1,0:T(8,128)(2,1)S(1)} %collective-permute-done.9.refs_0_.refs_1_, ...), custom_call_target="tpu_custom_call" | custom-call | tf_op jit(solution)/shard_map/attention/pallas_call | solution.py:218
  51.2 1.2 collective-permute-start.18
  52.4 1.2 collective-permute-start.16
  53.7 0.3 collective-permute-start.14
  53.9 30.7 %collective-permute-done.7.refs_2_ = bf16[4096,128]{1,0:T(8,128)(2,1)S(1)} collective-permute-done((bf16[4096,128]{1,0:T(8,128)(2,1)S(1)}, bf16[4096,128]{1,0:T(8,128)(2,1)S(1)}, u32[]{:S(2)}, u32[]{:S(2)}) %collective-permute-start.7) | collective-permute-done | bytes 1048608 | tf_op jit(solution)/shard_map/between_2/ppermute | solution.py:323
  84.6 2.4 %collective-permute-start.13 = (bf16[4,256,512]{2,1,0:T(8,128)(2,1)S(1)}, bf16[4,256,512]{2,1,0:T(8,128)(2,1)S(1)}, u32[]{:S(2)}, u32[]{:S(2)}) collective-permute-start(bf16[4,256,512]{2,1,0:T(8,128)(2,1)S(1)} %attention.5.refs_4_), channel_id=1, source_target_pairs={{0,2},{1,3},{2,0},{3,1},{4,6},{5,7},{6,4},{7,5},{8,10},{9,11},{10,... | collective-permute-start | bytes 3145736 | tf_op jit(solution)/shard_map/across_1_0/ppermute | solution.py:315
  87.0 0.0 collective-permute-done.6.refs_1_
  87.0 0.0 collective-permute-start.8
  87.0 0.1 collective-permute-start.19
  87.1 12.7 %collective-permute-done.16.refs_8_ = bf16[4,256,512]{2,1,0:T(8,128)(2,1)S(1)} collective-permute-done((bf16[4,256,512]{2,1,0:T(8,128)(2,1)S(1)}, bf16[4,256,512]{2,1,0:T(8,128)(2,1)S(1)}, u32[]{:S(2)}, u32[]{:S(2)}) %collective-permute-start.16) | collective-permute-done | bytes 1048608 | tf_op jit(solution)/shard_map/across_0_1/ppermute | solution.py:315
  99.7 0.5 collective-permute-start.17
  100.2 0.0 collective-permute-done.14.refs_6_
  100.2 0.0 collective-permute-start.15
  100.3 0.0 collective-permute-done.13.refs_5_
  100.3 11.5 %collective-permute-done.8.refs_3_ = bf16[4096,128]{1,0:T(8,128)(2,1)S(1)} collective-permute-done((bf16[4096,128]{1,0:T(8,128)(2,1)S(1)}, bf16[4096,128]{1,0:T(8,128)(2,1)S(1)}, u32[]{:S(2)}, u32[]{:S(2)}) %collective-permute-start.8) | collective-permute-done | bytes 1048608 | tf_op jit(solution)/shard_map/between_1/ppermute | solution.py:323
  111.8 0.0 collective-permute-done.15.refs_7_
  111.8 4.5 %project.1 = (bf16[256,256]{1,0:T(8,128)(2,1)S(1)}, bf16[256,256]{1,0:T(8,128)(2,1)S(1)}, bf16[256,256]{1,0:T(8,128)(2,1)S(1)}, bf16[256,256]{1,0:T(8,128)(2,1)S...) custom-call(bf16[4096,128]{1,0:T(8,128)(2,1)S(1)} %pad_maximum_fusio, ...), custom_call_target="tpu_custom_call" | custom-call | tf_op jit(solution)/shard_map/project/pallas_call | solution.py:392
  116.3 0.6 copy-done.3
  117.0 1.8 %collective-permute-start.20 = (bf16[256,256]{1,0:T(8,128)(2,1)S(1)}, bf16[256,256]{1,0:T(8,128)(2,1)S(1)}, u32[]{:S(2)}, u32[]{:S(2)}) collective-permute-start(bf16[256,256]{1,0:T(8,128)(2,1)S(1)} %get-tuple-element.49), channel_id=1, source_target_pairs={{0,7},{1,6},{2,5},{3,4},{4,3},{5,2},{6,1},{7,0},{8,15},{9,14},{10,... | collective-permute-start | bytes 393224 | tf_op jit(solution)/shard_map/across_3_1/ppermute | solution.py:315
  118.8 1.2 collective-permute-start.21
  120.0 1.1 collective-permute-start.22
  121.1 0.3 collective-permute-start.23
  121.3 0.9 collective-permute-start.24
  122.2 1.6 %collective-permute-done.20.refs_0_ = bf16[256,256]{1,0:T(8,128)(2,1)S(1)} collective-permute-done((bf16[256,256]{1,0:T(8,128)(2,1)S(1)}, bf16[256,256]{1,0:T(8,128)(2,1)S(1)}, u32[]{:S(2)}, u32[]{:S(2)}) %collective-permute-start.20) | collective-permute-done | bytes 131104 | tf_op jit(solution)/shard_map/across_3_1/ppermute | solution.py:315
  123.8 0.3 collective-permute-start.25
  124.2 2.5 %collective-permute-done.21.refs_1_ = bf16[256,256]{1,0:T(8,128)(2,1)S(1)} collective-permute-done((bf16[256,256]{1,0:T(8,128)(2,1)S(1)}, bf16[256,256]{1,0:T(8,128)(2,1)S(1)}, u32[]{:S(2)}, u32[]{:S(2)}) %collective-permute-start.21) | collective-permute-done | bytes 131104 | tf_op jit(solution)/shard_map/across_2_1/ppermute | solution.py:315
  126.7 0.5 collective-permute-start.26
  127.2 1.7 %collective-permute-done.22.refs_2_ = bf16[256,256]{1,0:T(8,128)(2,1)S(1)} collective-permute-done((bf16[256,256]{1,0:T(8,128)(2,1)S(1)}, bf16[256,256]{1,0:T(8,128)(2,1)S(1)}, u32[]{:S(2)}, u32[]{:S(2)}) %collective-permute-start.22) | collective-permute-done | bytes 131104 | tf_op jit(solution)/shard_map/across_3_0/ppermute | solution.py:315
  128.8 2.6 %collective-permute-done.23.refs_3_ = bf16[256,256]{1,0:T(8,128)(2,1)S(1)} collective-permute-done((bf16[256,256]{1,0:T(8,128)(2,1)S(1)}, bf16[256,256]{1,0:T(8,128)(2,1)S(1)}, u32[]{:S(2)}, u32[]{:S(2)}) %collective-permute-start.23) | collective-permute-done | bytes 131104 | tf_op jit(solution)/shard_map/across_2_0/ppermute | solution.py:315
  131.5 0.0 collective-permute-done.24.refs_4_
  131.5 0.9 collective-permute-done.25.refs_5_
  132.4 0.6 copy-done.13
  133.0 0.0 copy-done.14
  133.1 2.6 %place.1 = bf16[256,2048]{1,0:T(8,128)(2,1)} custom-call(bf16[256,256]{1,0:T(8,128)(2,1)} %copy-done.8, bf16[256,256]{1,0:T(8,128)(2,1)} %copy-done.9, bf16[256,256]{1,0:T(8,128)(2,1)} %copy-done.10, bf16[256,256]{1,0:T(8,128)(2,1)} %copy-done.11, bf16[256,256]{1,0:T(8,128)(2,1)} %copy-done.12, bf16[256,256]{1,0:T(8,128)(2,1)} %copy-done.13, ...), custom_call_target="tpu_custom_call" | custom-call | tf_op jit(solution)/shard_map/place/pallas_call | solution.py:407
  (30 shorter events, 0.1 us)
Async XLA Ops:
  0.0 16.8 %collective-permute-start = (bf16[256,2048]{1,0:T(8,128)(2,1)}, bf16[256,2048]{1,0:T(8,128)(2,1)S(1)}, u32[]{:S(2)}, u32[]{:S(2)}) collective-permute-start(bf16[256,2048]{1,0:T(8,128)(2,1)} %refs_0_.1), channel_id=1, source_target_pairs={{0,2},{1,3},{2,0},{3,1},{4,6},{5,7},{6,4},{7,5},{8,10},{9,11},{10,... | collective-permute-start | bytes 3145736 | tf_op jit(solution)/shard_map/across_1_0/ppermute | solution.py:315
  3.0 13.8 %collective-permute-start.1 = (bf16[2048,128]{1,0:T(8,128)(2,1)}, bf16[2048,128]{1,0:T(8,128)(2,1)S(1)}, u32[]{:S(2)}, u32[]{:S(2)}) collective-permute-start(bf16[2048,128]{1,0:T(8,128)(2,1)} %get-tuple-element.32), channel_id=1, source_target_pairs={{0,1},{1,0},{2,3},{3,2},{4,5},{5,4},{6,7},{7,6},{8,9},{9,8},{10,11... | collective-permute-start | bytes 1572872 | tf_op jit(solution)/shard_map/across_0_1/ppermute | solution.py:315
  4.3 1.7 %collective-permute-start.3 = (bf16[256,512]{1,0:T(8,128)(2,1)}, bf16[256,512]{1,0:T(8,128)(2,1)S(1)}, u32[]{:S(2)}, u32[]{:S(2)}) collective-permute-start(bf16[256,512]{1,0:T(8,128)(2,1)} %refs_1_.1), channel_id=1, source_target_pairs={{0,2},{1,3},{2,0},{3,1},{4,6},{5,7},{6,4},{7,5},{8,10},{9,11},{10,... | collective-permute-start | bytes 786440 | tf_op jit(solution)/shard_map/across_1_0/ppermute | solution.py:315
  4.6 1.8 %collective-permute-start.2 = (bf16[256,512]{1,0:T(8,128)(2,1)}, bf16[256,512]{1,0:T(8,128)(2,1)S(1)}, u32[]{:S(2)}, u32[]{:S(2)}) collective-permute-start(bf16[256,512]{1,0:T(8,128)(2,1)} %refs_0_), channel_id=1, source_target_pairs={{0,2},{1,3},{2,0},{3,1},{4,6},{5,7},{6,4},{7,5},{8,10},{9,11},{10,... | collective-permute-start | bytes 786440 | tf_op jit(solution)/shard_map/across_1_0/ppermute | solution.py:315
  6.0 0.7 copy-start.6
  6.7 0.7 copy-start.7
  9.5 22.9 %collective-permute-start.12 = (bf16[2,256,256]{2,1,0:T(8,128)(2,1)}, bf16[2,256,256]{2,1,0:T(8,128)(2,1)S(1)}, u32[]{:S(2)}, u32[]{:S(2)}) collective-permute-start(bf16[2,256,256]{2,1,0:T(8,128)(2,1)} %get-tuple-element.37), channel_id=1, source_target_pairs={{0,4},{1,5},{2,6},{3,7},{4,0},{5,1},{6,2},{7,3},{8,12},{9,13},{10,... | collective-permute-start | bytes 786440 | tf_op jit(solution)/shard_map/across_2_0/ppermute | solution.py:315
  10.8 12.9 %collective-permute-start.5 = (bf16[2,256,256]{2,1,0:T(8,128)(2,1)}, bf16[2,256,256]{2,1,0:T(8,128)(2,1)S(1)}, u32[]{:S(2)}, u32[]{:S(2)}) collective-permute-start(bf16[2,256,256]{2,1,0:T(8,128)(2,1)} %get-tuple-element.37), channel_id=1, source_target_pairs={{0,12},{1,13},{2,14},{3,15},{4,8},{5,9},{6,10},{7,11},{8,20},{9,21... | collective-permute-start | bytes 786440 | tf_op jit(solution)/shard_map/up_2/ppermute | solution.py:319
  12.0 16.4 %copy-start.2 = (s32[4096]{0:T(1024)S(1)}, s32[4096]{0:T(1024)}, u32[]{:S(2)}) copy-start(s32[4096]{0:T(1024)} %seg_ref.5) | copy-start | bytes 49156
  12.1 21.2 %copy-start.1 = (bf16[2,256,256]{2,1,0:T(8,128)(2,1)S(1)}, bf16[2,256,256]{2,1,0:T(8,128)(2,1)}, u32[]{:S(2)}) copy-start(bf16[2,256,256]{2,1,0:T(8,128)(2,1)} %get-tuple-element.36.refs_1_) | copy-start | bytes 786436
  12.1 13.8 %collective-permute-start.4 = (bf16[2,256,256]{2,1,0:T(8,128)(2,1)}, bf16[2,256,256]{2,1,0:T(8,128)(2,1)S(1)}, u32[]{:S(2)}, u32[]{:S(2)}) collective-permute-start(bf16[2,256,256]{2,1,0:T(8,128)(2,1)} %get-tuple-element.36.refs_1_), channel_id=1, source_target_pairs={{0,8},{1,9},{2,10},{3,11},{4,12},{5,13},{6,14},{7,15},{8,16},{9,17... | collective-permute-start | bytes 786440 | tf_op jit(solution)/shard_map/up_0/ppermute | solution.py:319
  16.8 0.8 copy-start.5
  17.6 1.0 copy-start.4
  21.2 12.1 %copy-start = (bf16[2,256,512]{2,1,0:T(8,128)(2,1)S(1)}, bf16[2,256,512]{2,1,0:T(8,128)(2,1)}, u32[]{:S(2)}) copy-start(bf16[2,256,512]{2,1,0:T(8,128)(2,1)} %get-tuple-element.41.refs_0_) | copy-start | bytes 1572868
  21.2 18.1 %collective-permute-start.9 = (bf16[2,256,512]{2,1,0:T(8,128)(2,1)}, bf16[2,256,512]{2,1,0:T(8,128)(2,1)S(1)}, u32[]{:S(2)}, u32[]{:S(2)}) collective-permute-start(bf16[2,256,512]{2,1,0:T(8,128)(2,1)} %get-tuple-element.42), channel_id=1, source_target_pairs={{0,4},{1,5},{2,6},{3,7},{4,0},{5,1},{6,2},{7,3},{8,12},{9,13},{10,... | collective-permute-start | bytes 1572872 | tf_op jit(solution)/shard_map/across_2_0/ppermute | solution.py:315
  25.8 19.6 %collective-permute-start.10 = (bf16[2,256,256]{2,1,0:T(8,128)(2,1)S(1)}, bf16[2,256,256]{2,1,0:T(8,128)(2,1)S(1)}, u32[]{:S(2)}, u32[]{:S(2)}) collective-permute-start(bf16[2,256,256]{2,1,0:T(8,128)(2,1)S(1)} %collective-permute-done.4.refs_3_), channel_id=1, source_target_pairs={{0,8},{1,9},{2,10},{3,11},{4,12},{5,13},{6,14},{7,15},{8,16},{9,17... | collective-permute-start | bytes 786440 | tf_op jit(solution)/shard_map/up_0/ppermute | solution.py:319
  27.1 18.3 %collective-permute-start.11 = (bf16[2,256,256]{2,1,0:T(8,128)(2,1)S(1)}, bf16[2,256,256]{2,1,0:T(8,128)(2,1)}, u32[]{:S(2)}, u32[]{:S(2)}) collective-permute-start(bf16[2,256,256]{2,1,0:T(8,128)(2,1)S(1)} %collective-permute-done.5.refs_4_), channel_id=1, source_target_pairs={{0,8},{1,9},{2,10},{3,11},{4,12},{5,13},{6,14},{7,15},{8,16},{9,17... | collective-permute-start | bytes 786440 | tf_op jit(solution)/shard_map/up_0/ppermute | solution.py:319
  28.4 56.2 %collective-permute-start.7 = (bf16[4096,128]{1,0:T(8,128)(2,1)S(1)}, bf16[4096,128]{1,0:T(8,128)(2,1)S(1)}, u32[]{:S(2)}, u32[]{:S(2)}) collective-permute-start(bf16[4096,128]{1,0:T(8,128)(2,1)S(1)} %pad_maximum_fusion.refs_0_), channel_id=1, source_target_pairs={{0,16},{1,17},{2,18},{3,19},{4,20},{5,21},{6,22},{7,23},{8,24},{9,... | collective-permute-start | bytes 3145736 | tf_op jit(solution)/shard_map/between_2/ppermute | solution.py:323
  32.4 54.6 %collective-permute-start.6 = (bf16[4096,128]{1,0:T(8,128)(2,1)S(1)}, bf16[4096,128]{1,0:T(8,128)(2,1)S(1)}, u32[]{:S(2)}, u32[]{:S(2)}) collective-permute-start(bf16[4096,128]{1,0:T(8,128)(2,1)S(1)} %pad_maximum_fusion.refs_0_), channel_id=1, source_target_pairs={{0,8},{1,9},{2,10},{3,11},{4,12},{5,13},{6,14},{7,15},{8,0},{9,1},... | collective-permute-start | bytes 3145736 | tf_op jit(solution)/shard_map/between_1/ppermute | solution.py:323
  51.2 35.8 %collective-permute-start.18 = (bf16[4,256,512]{2,1,0:T(8,128)(2,1)S(1)}, bf16[4,256,512]{2,1,0:T(8,128)(2,1)S(1)}, u32[]{:S(2)}, u32[]{:S(2)}) collective-permute-start(bf16[4,256,512]{2,1,0:T(8,128)(2,1)S(1)} %attention.5.refs_4_), channel_id=1, source_target_pairs={{0,5},{1,4},{2,7},{3,6},{4,1},{5,0},{6,3},{7,2},{8,13},{9,12},{10,... | collective-permute-start | bytes 3145736 | tf_op jit(solution)/shard_map/across_2_1/ppermute | solution.py:315
  52.4 47.3 %collective-permute-start.16 = (bf16[4,256,512]{2,1,0:T(8,128)(2,1)S(1)}, bf16[4,256,512]{2,1,0:T(8,128)(2,1)S(1)}, u32[]{:S(2)}, u32[]{:S(2)}) collective-permute-start(bf16[4,256,512]{2,1,0:T(8,128)(2,1)S(1)} %attention.5.refs_4_), channel_id=1, source_target_pairs={{0,1},{1,0},{2,3},{3,2},{4,5},{5,4},{6,7},{7,6},{8,9},{9,8},{10,11... | collective-permute-start | bytes 3145736 | tf_op jit(solution)/shard_map/across_0_1/ppermute | solution.py:315
  53.7 46.6 %collective-permute-start.14 = (bf16[4,256,512]{2,1,0:T(8,128)(2,1)S(1)}, bf16[4,256,512]{2,1,0:T(8,128)(2,1)S(1)}, u32[]{:S(2)}, u32[]{:S(2)}) collective-permute-start(bf16[4,256,512]{2,1,0:T(8,128)(2,1)S(1)} %attention.5.refs_4_), channel_id=1, source_target_pairs={{0,4},{1,5},{2,6},{3,7},{4,0},{5,1},{6,2},{7,3},{8,12},{9,13},{10,... | collective-permute-start | bytes 3145736 | tf_op jit(solution)/shard_map/across_2_0/ppermute | solution.py:315
  84.6 15.6 %collective-permute-start.13 = (bf16[4,256,512]{2,1,0:T(8,128)(2,1)S(1)}, bf16[4,256,512]{2,1,0:T(8,128)(2,1)S(1)}, u32[]{:S(2)}, u32[]{:S(2)}) collective-permute-start(bf16[4,256,512]{2,1,0:T(8,128)(2,1)S(1)} %attention.5.refs_4_), channel_id=1, source_target_pairs={{0,2},{1,3},{2,0},{3,1},{4,6},{5,7},{6,4},{7,5},{8,10},{9,11},{10,... | collective-permute-start | bytes 3145736 | tf_op jit(solution)/shard_map/across_1_0/ppermute | solution.py:315
  87.0 24.8 %collective-permute-start.8 = (bf16[4096,128]{1,0:T(8,128)(2,1)S(1)}, bf16[4096,128]{1,0:T(8,128)(2,1)S(1)}, u32[]{:S(2)}, u32[]{:S(2)}) collective-permute-start(bf16[4096,128]{1,0:T(8,128)(2,1)S(1)} %collective-permute-done.7.refs_2_), channel_id=1, source_target_pairs={{0,8},{1,9},{2,10},{3,11},{4,12},{5,13},{6,14},{7,15},{8,0},{9,1},... | collective-permute-start | bytes 3145736 | tf_op jit(solution)/shard_map/between_1/ppermute | solution.py:323
  87.0 24.8 %collective-permute-start.19 = (bf16[4,256,512]{2,1,0:T(8,128)(2,1)S(1)}, bf16[4,256,512]{2,1,0:T(8,128)(2,1)S(1)}, u32[]{:S(2)}, u32[]{:S(2)}) collective-permute-start(bf16[4,256,512]{2,1,0:T(8,128)(2,1)S(1)} %collective-permute-done.18.refs_10_), channel_id=1, source_target_pairs={{0,2},{1,3},{2,0},{3,1},{4,6},{5,7},{6,4},{7,5},{8,10},{9,11},{10,... | collective-permute-start | bytes 3145736 | tf_op jit(solution)/shard_map/across_1_0/ppermute | solution.py:315
  99.7 12.0 %collective-permute-start.17 = (bf16[4,256,512]{2,1,0:T(8,128)(2,1)S(1)}, bf16[4,256,512]{2,1,0:T(8,128)(2,1)S(1)}, u32[]{:S(2)}, u32[]{:S(2)}) collective-permute-start(bf16[4,256,512]{2,1,0:T(8,128)(2,1)S(1)} %collective-permute-done.16.refs_8_), channel_id=1, source_target_pairs={{0,2},{1,3},{2,0},{3,1},{4,6},{5,7},{6,4},{7,5},{8,10},{9,11},{10,... | collective-permute-start | bytes 3145736 | tf_op jit(solution)/shard_map/across_1_0/ppermute | solution.py:315
  100.2 11.6 %collective-permute-start.15 = (bf16[4,256,512]{2,1,0:T(8,128)(2,1)S(1)}, bf16[4,256,512]{2,1,0:T(8,128)(2,1)S(1)}, u32[]{:S(2)}, u32[]{:S(2)}) collective-permute-start(bf16[4,256,512]{2,1,0:T(8,128)(2,1)S(1)} %collective-permute-done.14.refs_6_), channel_id=1, source_target_pairs={{0,2},{1,3},{2,0},{3,1},{4,6},{5,7},{6,4},{7,5},{8,10},{9,11},{10,... | collective-permute-start | bytes 3145736 | tf_op jit(solution)/shard_map/across_1_0/ppermute | solution.py:315
  116.3 0.7 copy-start.3
  117.0 6.9 %collective-permute-start.20 = (bf16[256,256]{1,0:T(8,128)(2,1)S(1)}, bf16[256,256]{1,0:T(8,128)(2,1)S(1)}, u32[]{:S(2)}, u32[]{:S(2)}) collective-permute-start(bf16[256,256]{1,0:T(8,128)(2,1)S(1)} %get-tuple-element.49), channel_id=1, source_target_pairs={{0,7},{1,6},{2,5},{3,4},{4,3},{5,2},{6,1},{7,0},{8,15},{9,14},{10,... | collective-permute-start | bytes 393224 | tf_op jit(solution)/shard_map/across_3_1/ppermute | solution.py:315
  118.8 7.9 %collective-permute-start.21 = (bf16[256,256]{1,0:T(8,128)(2,1)S(1)}, bf16[256,256]{1,0:T(8,128)(2,1)S(1)}, u32[]{:S(2)}, u32[]{:S(2)}) collective-permute-start(bf16[256,256]{1,0:T(8,128)(2,1)S(1)} %get-tuple-element.50), channel_id=1, source_target_pairs={{0,5},{1,4},{2,7},{3,6},{4,1},{5,0},{6,3},{7,2},{8,13},{9,12},{10,... | collective-permute-start | bytes 393224 | tf_op jit(solution)/shard_map/across_2_1/ppermute | solution.py:315
  120.0 8.8 %collective-permute-start.22 = (bf16[256,256]{1,0:T(8,128)(2,1)S(1)}, bf16[256,256]{1,0:T(8,128)(2,1)S(1)}, u32[]{:S(2)}, u32[]{:S(2)}) collective-permute-start(bf16[256,256]{1,0:T(8,128)(2,1)S(1)} %get-tuple-element.51), channel_id=1, source_target_pairs={{0,6},{1,7},{2,4},{3,5},{4,2},{5,3},{6,0},{7,1},{8,14},{9,15},{10,... | collective-permute-start | bytes 393224 | tf_op jit(solution)/shard_map/across_3_0/ppermute | solution.py:315
  121.1 10.4 %collective-permute-start.23 = (bf16[256,256]{1,0:T(8,128)(2,1)S(1)}, bf16[256,256]{1,0:T(8,128)(2,1)S(1)}, u32[]{:S(2)}, u32[]{:S(2)}) collective-permute-start(bf16[256,256]{1,0:T(8,128)(2,1)S(1)} %get-tuple-element.52), channel_id=1, source_target_pairs={{0,4},{1,5},{2,6},{3,7},{4,0},{5,1},{6,2},{7,3},{8,12},{9,13},{10,... | collective-permute-start | bytes 393224 | tf_op jit(solution)/shard_map/across_2_0/ppermute | solution.py:315
  121.3 10.1 %collective-permute-start.24 = (bf16[256,256]{1,0:T(8,128)(2,1)S(1)}, bf16[256,256]{1,0:T(8,128)(2,1)S(1)}, u32[]{:S(2)}, u32[]{:S(2)}) collective-permute-start(bf16[256,256]{1,0:T(8,128)(2,1)S(1)} %get-tuple-element.53), channel_id=1, source_target_pairs={{0,3},{1,2},{2,1},{3,0},{4,7},{5,6},{6,5},{7,4},{8,11},{9,10},{10,... | collective-permute-start | bytes 393224 | tf_op jit(solution)/shard_map/across_1_1/ppermute | solution.py:315
  123.8 8.5 %copy-start.8 = (bf16[256,256]{1,0:T(8,128)(2,1)}, bf16[256,256]{1,0:T(8,128)(2,1)S(1)}, u32[]{:S(2)}) copy-start(bf16[256,256]{1,0:T(8,128)(2,1)S(1)} %collective-permute-done.20.refs_0_) | copy-start | bytes 393220
  123.8 8.5 %collective-permute-start.25 = (bf16[256,256]{1,0:T(8,128)(2,1)S(1)}, bf16[256,256]{1,0:T(8,128)(2,1)S(1)}, u32[]{:S(2)}, u32[]{:S(2)}) collective-permute-start(bf16[256,256]{1,0:T(8,128)(2,1)S(1)} %get-tuple-element.54), channel_id=1, source_target_pairs={{0,1},{1,0},{2,3},{3,2},{4,5},{5,4},{6,7},{7,6},{8,9},{9,8},{10,11... | collective-permute-start | bytes 393224 | tf_op jit(solution)/shard_map/across_0_1/ppermute | solution.py:315
  126.7 5.7 %copy-start.9 = (bf16[256,256]{1,0:T(8,128)(2,1)}, bf16[256,256]{1,0:T(8,128)(2,1)S(1)}, u32[]{:S(2)}) copy-start(bf16[256,256]{1,0:T(8,128)(2,1)S(1)} %collective-permute-done.21.refs_1_) | copy-start | bytes 393220
  126.7 5.7 %collective-permute-start.26 = (bf16[256,256]{1,0:T(8,128)(2,1)S(1)}, bf16[256,256]{1,0:T(8,128)(2,1)S(1)}, u32[]{:S(2)}, u32[]{:S(2)}) collective-permute-start(bf16[256,256]{1,0:T(8,128)(2,1)S(1)} %get-tuple-element.55), channel_id=1, source_target_pairs={{0,2},{1,3},{2,0},{3,1},{4,6},{5,7},{6,4},{7,5},{8,10},{9,11},{10,... | collective-permute-start | bytes 393224 | tf_op jit(solution)/shard_map/across_1_0/ppermute | solution.py:315
  128.8 3.6 %copy-start.10 = (bf16[256,256]{1,0:T(8,128)(2,1)}, bf16[256,256]{1,0:T(8,128)(2,1)S(1)}, u32[]{:S(2)}) copy-start(bf16[256,256]{1,0:T(8,128)(2,1)S(1)} %collective-permute-done.22.refs_2_) | copy-start | bytes 393220
  131.5 0.9 copy-start.11
  131.5 0.9 copy-start.12
  132.4 0.7 copy-start.13
  132.4 0.7 copy-start.14

commit v5 on v4

--- a/solution.py
+++ b/solution.py
@@ -365,15 +365,10 @@
     q = [q[0]] + [across(q[o], 2 * o, 0) for o in range(1, group // 2)]
 
     own = jnp.concatenate(others)
-    own, *links[1] = after(own, *links[1])
+    own, links[1][-1] = after(own, links[1][-1])
     for _ in range(1, hops):
         links.append([up(pair) for pair in links[-1]])
-    blocks = {0: own}
-    stride = planes // 2
-    while stride:
-        for i in list(blocks):
-            blocks[i + stride] = between(blocks[i], stride)
-        stride //= 2
+    blocks = {0: own, planes // 2: between(own, planes // 2), planes // 4: between(own, planes // 4)}
 
     near = [pair for pairs_of in links[:hops] for pair in pairs_of]
     carried = []
@@ -388,6 +383,13 @@
         everything += with_other_core(
             [attended if o == m == 0 else across(attended, 2 * o, m) for o in range(group // 2)]
         )
+
+    stride = planes // 2
+    while stride:
+        for i in range(0, planes, 2 * stride):
+            if i + stride not in blocks:
+                blocks[i + stride] = between(blocks[i], stride)
+        stride //= 2
 
     found = pl.pallas_call(
         functools.partial(project_kernel, group, attn, planes),

time: 136 us -> 133 us (0.978)
  Pallas kernels: 32 us -> 29.2 us
  waiting for transfers between devices: 71.3 us -> 68.6 us
  starting transfers between devices: 26.7 us -> 28.5 us
    ppermute x20, waiting for transfers between devices: 26.9 us -> 20.5 us  [across(): return lax.ppermute(array, AXES, pairs(lambda z, g, y: (z, g ^ j, y ^ m)))]
    ppermute x4, waiting for transfers between devices: 2.14 us -> 5.84 us  [up(): return lax.ppermute(array, AXES, pairs(lambda z, g, y: (z + 1, g ^ j, y)))]
    pallas_call x3, Pallas kernels: 17.9 us -> 15.1 us  [attention(): pl.pallas_call(functools.partial(attention_kernel, group, heads, back, pa...]
    ppermute x20, starting transfers between devices: 16.6 us -> 18.5 us  [across(): return lax.ppermute(array, AXES, pairs(lambda z, g, y: (z, g ^ j, y ^ m)))]
  transfers between devices with their start and end apart: 27 -> 27, of which waited for: 12 -> 10; matrix products, arithmetic and copies ran while one was open for 1% -> 1% of each run, Pallas kernels for 18% -> 17%
where the time goes in v5:
time: 133 us; the launch traced here: 132 us
  waiting for transfers between devices  68.6 us (52%)
  Pallas kernels  29.2 us (22%)
  starting transfers between devices  28.5 us (21%)
  local copies, waits for them, and re-layouts  4.39 us (3%)
    ppermute x3, waiting for transfers between devices, between(): return lax.ppermute(array, AXES, pairs(lambda z, g, y: (z ^ i, g, y)))  42.3 us
    ppermute x20, waiting for transfers between devices, across(): return lax.ppermute(array, AXES, pairs(lambda z, g, y: (z, g ^ j, y ^ m)))  20.5 us
    ppermute x20, starting transfers between devices, across(): return lax.ppermute(array, AXES, pairs(lambda z, g, y: (z, g ^ j, y ^ m)))  18.5 us
    pallas_call x3, Pallas kernels, attention(): pl.pallas_call(functools.partial(attention_kernel, group, heads, back, pa...  15.1 us
    ppermute x4, waiting for transfers between devices, up(): return lax.ppermute(array, AXES, pairs(lambda z, g, y: (z + 1, g ^ j, y)))  5.84 us
    ppermute x4, starting transfers between devices, up(): return lax.ppermute(array, AXES, pairs(lambda z, g, y: (z + 1, g ^ j, y)))  5.13 us
    ppermute x3, starting transfers between devices, between(): return lax.ppermute(array, AXES, pairs(lambda z, g, y: (z ^ i, g, y)))  4.81 us
    pallas_call x1, Pallas kernels, shards(): pl.pallas_call(functools.partial(project_kernel, group, attn, planes), ou...  4.49 us
  transfers between devices with their start and end apart: 27, of which 10 were waited for; matrix products, arithmetic and copies ran while one was open for 1% of the time, Pallas kernels for 17%

profile of v5, /device:TPU:25, one launch (start us, length us, event | category | flops | bytes accessed | tf_op | source)
XLA Modules:
  0.0 132.2 jit_solution(11806721097841187411)
XLA Ops:
  0.0 0.7 collective-permute-start
  0.7 0.0 collective-permute-start.3
  0.7 2.4 %split_w.1 = (bf16[2048,128]{1,0:T(8,128)(2,1)}, bf16[2048,128]{1,0:T(8,128)(2,1)}) custom-call(bf16[2048,256]{1,0:T(8,128)(2,1)} %w_ref.1), custom_call_target="tpu_custom_call" | custom-call | tf_op jit(solution)/shard_map/split_w/pallas_call | solution.py:331
  3.1 0.5 collective-permute-start.2
  3.6 1.2 collective-permute-start.1
  4.8 0.0 collective-permute-done.3.refs_3_
  4.8 0.1 collective-permute-done.2.refs_2_
  4.9 0.6 copy-done.6
  5.5 0.7 copy-done.7
  6.2 2.1 %split_kv.1 = (bf16[2,256,256]{2,1,0:T(8,128)(2,1)}, bf16[2,256,256]{2,1,0:T(8,128)(2,1)}) custom-call(bf16[256,512]{1,0:T(8,128)(2,1)} %refs_0_, bf16[256,512]{1,0:T(8,128)(2,1)} %refs_1_.1, bf16[256,512]{1,0:T(8,128)(2,1)} %copy-done.7, bf16[256,512]{1,0:T(8,128)(2,1)} %copy-done.6), custom_call_target="tpu_custom_call" | custom-call | tf_op jit(solution)/shard_map/split_kv/pallas_call | solution.py:347
  8.3 1.3 collective-permute-start.9
  9.6 0.0 copy-start.2
  9.6 1.3 collective-permute-start.12
  10.9 1.3 collective-permute-start.4
  12.2 5.8 %collective-permute-done.9.refs_3_ = bf16[2,256,256]{2,1,0:T(8,128)(2,1)S(1)} collective-permute-done((bf16[2,256,256]{2,1,0:T(8,128)(2,1)}, bf16[2,256,256]{2,1,0:T(8,128)(2,1)S(1)}, u32[]{:S(2)}, u32[]{:S(2)}) %collective-permute-start.9) | collective-permute-done | bytes 262176 | tf_op jit(solution)/shard_map/up_0/ppermute | solution.py:319
  18.0 1.3 collective-permute-start.10
  19.3 0.0 collective-permute-done.refs_1_
  19.3 0.8 copy-done.5
  20.1 1.0 copy-done.4
  21.1 2.6 %split_q.1 = (bf16[2,256,512]{2,1,0:T(8,128)(2,1)}, bf16[2,256,512]{2,1,0:T(8,128)(2,1)}) custom-call(bf16[256,2048]{1,0:T(8,128)(2,1)} %refs_0_.1, bf16[256,2048]{1,0:T(8,128)(2,1)} %copy-done.4), custom_call_target="tpu_custom_call" | custom-call | tf_op jit(solution)/shard_map/split_q/pallas_call | solution.py:358
  23.7 1.2 collective-permute-start.8
  24.9 1.3 pad_maximum_fusion.refs_0_
  26.2 1.3 collective-permute-start.11
  27.5 3.9 %collective-permute-start.6 = (bf16[4096,128]{1,0:T(8,128)(2,1)S(1)}, bf16[4096,128]{1,0:T(8,128)(2,1)S(1)}, u32[]{:S(2)}, u32[]{:S(2)}) collective-permute-start(bf16[4096,128]{1,0:T(8,128)(2,1)S(1)} %pad_maximum_fusion.refs_0_), channel_id=1, source_target_pairs={{0,16},{1,17},{2,18},{3,19},{4,20},{5,21},{6,22},{7,23},{8,24},{9,... | collective-permute-start | bytes 3145736 | tf_op jit(solution)/shard_map/between_2/ppermute | solution.py:323
  31.5 0.0 collective-permute-done.12.refs_2_
  31.5 0.9 collective-permute-start.5
  32.4 6.1 %attention.3 = (f32[2,1024,128]{2,1,0:T(8,128)S(1)}, f32[2,1024,256]{2,1,0:T(8,128)S(1)}) custom-call(s32[4096]{0:T(1024)S(1)} %copy-done.2, s32[16,256]{1,0:T(8,128)S(1)} %reshape.2.segrow_ref, bf16[2,256,512]{2,1,0:T(8,128)(2,1)S(1)} %copy-done, bf16[2,256,256]{2,1,0:T(8,128)(2,1)S(1)} %copy-done.1, ...), custom_call_target="tpu_custom_call" | custom-call | tf_op jit(solution)/shard_map/attention/pallas_call | solution.py:218
  38.4 0.0 collective-permute-done.8.refs_0_.refs_1_
  38.4 6.1 %attention.4 = (f32[2,1024,128]{2,1,0:T(8,128)S(1)}, f32[2,1024,256]{2,1,0:T(8,128)S(1)}) custom-call(s32[4096]{0:T(1024)S(1)} %copy-done.2, s32[16,256]{1,0:T(8,128)S(1)} %reshape.2.segrow_ref, bf16[2,256,512]{2,1,0:T(8,128)(2,1)S(1)} %collective-permute-done.8.refs_0_.refs_1_, bf16[2,256,256]{2,1,0:T(8,128)(2,1)S(1)} %copy-done.1, ...), custom_call_target="tpu_custom_call" | custom-call | tf_op jit(solution)/shard_map/attention/pallas_call | solution.py:218
  44.5 0.0 collective-permute-done.10.refs_2_
  44.5 0.0 collective-permute-done.11.refs_3_
  44.5 2.9 %attention.5.refs_4_ = bf16[4,256,512]{2,1,0:T(8,128)(2,1)S(1)} custom-call(s32[4096]{0:T(1024)S(1)} %copy-done.2, s32[16,256]{1,0:T(8,128)S(1)} %reshape.2.segrow_ref, bf16[2,256,512]{2,1,0:T(8,128)(2,1)S(1)} %copy-done, bf16[2,256,512]{2,1,0:T(8,128)(2,1)S(1)} %collective-permute-done.8.refs_0_.refs_1_, ...), custom_call_target="tpu_custom_call" | custom-call | tf_op jit(solution)/shard_map/attention/pallas_call | solution.py:218
  47.5 0.6 collective-permute-start.18
  48.1 0.9 collective-permute-start.16
  49.0 1.2 collective-permute-start.14
  50.2 30.1 %collective-permute-done.6.refs_2_ = bf16[4096,128]{1,0:T(8,128)(2,1)S(1)} collective-permute-done((bf16[4096,128]{1,0:T(8,128)(2,1)S(1)}, bf16[4096,128]{1,0:T(8,128)(2,1)S(1)}, u32[]{:S(2)}, u32[]{:S(2)}) %collective-permute-start.6) | collective-permute-done | bytes 1048608 | tf_op jit(solution)/shard_map/between_2/ppermute | solution.py:323
  80.3 3.3 %collective-permute-start.13 = (bf16[4,256,512]{2,1,0:T(8,128)(2,1)S(1)}, bf16[4,256,512]{2,1,0:T(8,128)(2,1)S(1)}, u32[]{:S(2)}, u32[]{:S(2)}) collective-permute-start(bf16[4,256,512]{2,1,0:T(8,128)(2,1)S(1)} %attention.5.refs_4_), channel_id=1, source_target_pairs={{0,2},{1,3},{2,0},{3,1},{4,6},{5,7},{6,4},{7,5},{8,10},{9,11},{10,... | collective-permute-start | bytes 3145736 | tf_op jit(solution)/shard_map/across_1_0/ppermute | solution.py:315
  83.6 0.0 collective-permute-done.5.refs_1_
  83.6 0.0 collective-permute-start.7
  83.6 0.0 collective-permute-done.18.refs_10_
  83.6 0.1 collective-permute-start.19
  83.7 11.6 %collective-permute-done.16.refs_8_ = bf16[4,256,512]{2,1,0:T(8,128)(2,1)S(1)} collective-permute-done((bf16[4,256,512]{2,1,0:T(8,128)(2,1)S(1)}, bf16[4,256,512]{2,1,0:T(8,128)(2,1)S(1)}, u32[]{:S(2)}, u32[]{:S(2)}) %collective-permute-start.16) | collective-permute-done | bytes 1048608 | tf_op jit(solution)/shard_map/across_0_1/ppermute | solution.py:315
  95.2 0.9 collective-permute-start.17
  96.1 0.0 collective-permute-start.15
  96.2 12.2 %collective-permute-done.7.refs_3_ = bf16[4096,128]{1,0:T(8,128)(2,1)S(1)} collective-permute-done((bf16[4096,128]{1,0:T(8,128)(2,1)S(1)}, bf16[4096,128]{1,0:T(8,128)(2,1)S(1)}, u32[]{:S(2)}, u32[]{:S(2)}) %collective-permute-start.7) | collective-permute-done | bytes 1048608 | tf_op jit(solution)/shard_map/between_1/ppermute | solution.py:323
  108.4 4.5 %project.1 = (bf16[256,256]{1,0:T(8,128)(2,1)S(1)}, bf16[256,256]{1,0:T(8,128)(2,1)S(1)}, bf16[256,256]{1,0:T(8,128)(2,1)S(1)}, bf16[256,256]{1,0:T(8,128)(2,1)S...) custom-call(bf16[4096,128]{1,0:T(8,128)(2,1)S(1)} %pad_maximum_fusio, ...), custom_call_target="tpu_custom_call" | custom-call | tf_op jit(solution)/shard_map/project/pallas_call | solution.py:394
  112.9 0.6 copy-done.3
  113.5 1.2 collective-permute-start.20
  114.7 1.8 %collective-permute-start.21 = (bf16[256,256]{1,0:T(8,128)(2,1)S(1)}, bf16[256,256]{1,0:T(8,128)(2,1)S(1)}, u32[]{:S(2)}, u32[]{:S(2)}) collective-permute-start(bf16[256,256]{1,0:T(8,128)(2,1)S(1)} %get-tuple-element.48), channel_id=1, source_target_pairs={{0,5},{1,4},{2,7},{3,6},{4,1},{5,0},{6,3},{7,2},{8,13},{9,12},{10,... | collective-permute-start | bytes 393224 | tf_op jit(solution)/shard_map/across_2_1/ppermute | solution.py:315
  116.6 0.1 collective-permute-start.22
  116.7 1.2 collective-permute-start.23
  117.9 1.2 collective-permute-start.24
  119.2 1.3 collective-permute-done.20.refs_0_
  120.4 0.6 collective-permute-start.25
  121.0 2.3 %collective-permute-done.21.refs_1_ = bf16[256,256]{1,0:T(8,128)(2,1)S(1)} collective-permute-done((bf16[256,256]{1,0:T(8,128)(2,1)S(1)}, bf16[256,256]{1,0:T(8,128)(2,1)S(1)}, u32[]{:S(2)}, u32[]{:S(2)}) %collective-permute-start.21) | collective-permute-done | bytes 131104 | tf_op jit(solution)/shard_map/across_2_1/ppermute | solution.py:315
  123.3 0.5 collective-permute-start.26
  123.7 1.7 %collective-permute-done.22.refs_2_ = bf16[256,256]{1,0:T(8,128)(2,1)S(1)} collective-permute-done((bf16[256,256]{1,0:T(8,128)(2,1)S(1)}, bf16[256,256]{1,0:T(8,128)(2,1)S(1)}, u32[]{:S(2)}, u32[]{:S(2)}) %collective-permute-start.22) | collective-permute-done | bytes 131104 | tf_op jit(solution)/shard_map/across_3_0/ppermute | solution.py:315
  125.5 2.9 %collective-permute-done.23.refs_3_ = bf16[256,256]{1,0:T(8,128)(2,1)S(1)} collective-permute-done((bf16[256,256]{1,0:T(8,128)(2,1)S(1)}, bf16[256,256]{1,0:T(8,128)(2,1)S(1)}, u32[]{:S(2)}, u32[]{:S(2)}) %collective-permute-start.23) | collective-permute-done | bytes 131104 | tf_op jit(solution)/shard_map/across_2_0/ppermute | solution.py:315
  128.4 0.6 collective-permute-done.25.refs_5_
  129.0 0.1 copy-done.11
  129.0 0.0 copy-done.12
  129.1 0.5 copy-done.13
  129.6 0.0 copy-done.14
  129.6 2.6 %place.1 = bf16[256,2048]{1,0:T(8,128)(2,1)} custom-call(bf16[256,256]{1,0:T(8,128)(2,1)} %copy-done.8, bf16[256,256]{1,0:T(8,128)(2,1)} %copy-done.9, bf16[256,256]{1,0:T(8,128)(2,1)} %copy-done.10, bf16[256,256]{1,0:T(8,128)(2,1)} %copy-done.11, bf16[256,256]{1,0:T(8,128)(2,1)} %copy-done.12, bf16[256,256]{1,0:T(8,128)(2,1)} %copy-done.13, ...), custom_call_target="tpu_custom_call" | custom-call | tf_op jit(solution)/shard_map/place/pallas_call | solution.py:409
  (30 shorter events, 0.1 us)
Async XLA Ops:
  0.0 19.3 %collective-permute-start = (bf16[256,2048]{1,0:T(8,128)(2,1)}, bf16[256,2048]{1,0:T(8,128)(2,1)S(1)}, u32[]{:S(2)}, u32[]{:S(2)}) collective-permute-start(bf16[256,2048]{1,0:T(8,128)(2,1)} %refs_0_.1), channel_id=1, source_target_pairs={{0,2},{1,3},{2,0},{3,1},{4,6},{5,7},{6,4},{7,5},{8,10},{9,11},{10,... | collective-permute-start | bytes 3145736 | tf_op jit(solution)/shard_map/across_1_0/ppermute | solution.py:315
  0.7 4.1 %collective-permute-start.3 = (bf16[256,512]{1,0:T(8,128)(2,1)}, bf16[256,512]{1,0:T(8,128)(2,1)S(1)}, u32[]{:S(2)}, u32[]{:S(2)}) collective-permute-start(bf16[256,512]{1,0:T(8,128)(2,1)} %refs_1_.1), channel_id=1, source_target_pairs={{0,2},{1,3},{2,0},{3,1},{4,6},{5,7},{6,4},{7,5},{8,10},{9,11},{10,... | collective-permute-start | bytes 786440 | tf_op jit(solution)/shard_map/across_1_0/ppermute | solution.py:315
  3.1 1.9 %collective-permute-start.2 = (bf16[256,512]{1,0:T(8,128)(2,1)}, bf16[256,512]{1,0:T(8,128)(2,1)S(1)}, u32[]{:S(2)}, u32[]{:S(2)}) collective-permute-start(bf16[256,512]{1,0:T(8,128)(2,1)} %refs_0_), channel_id=1, source_target_pairs={{0,2},{1,3},{2,0},{3,1},{4,6},{5,7},{6,4},{7,5},{8,10},{9,11},{10,... | collective-permute-start | bytes 786440 | tf_op jit(solution)/shard_map/across_1_0/ppermute | solution.py:315
  3.6 15.8 %collective-permute-start.1 = (bf16[2048,128]{1,0:T(8,128)(2,1)}, bf16[2048,128]{1,0:T(8,128)(2,1)S(1)}, u32[]{:S(2)}, u32[]{:S(2)}) collective-permute-start(bf16[2048,128]{1,0:T(8,128)(2,1)} %get-tuple-element.31), channel_id=1, source_target_pairs={{0,1},{1,0},{2,3},{3,2},{4,5},{5,4},{6,7},{7,6},{8,9},{9,8},{10,11... | collective-permute-start | bytes 1572872 | tf_op jit(solution)/shard_map/across_0_1/ppermute | solution.py:315
  4.8 0.7 copy-start.6
  5.5 0.7 copy-start.7
  8.3 9.7 %collective-permute-start.9 = (bf16[2,256,256]{2,1,0:T(8,128)(2,1)}, bf16[2,256,256]{2,1,0:T(8,128)(2,1)S(1)}, u32[]{:S(2)}, u32[]{:S(2)}) collective-permute-start(bf16[2,256,256]{2,1,0:T(8,128)(2,1)} %get-tuple-element.41.refs_1_), channel_id=1, source_target_pairs={{0,8},{1,9},{2,10},{3,11},{4,12},{5,13},{6,14},{7,15},{8,16},{9,17... | collective-permute-start | bytes 786440 | tf_op jit(solution)/shard_map/up_0/ppermute | solution.py:319
  9.6 17.9 %copy-start.2 = (s32[4096]{0:T(1024)S(1)}, s32[4096]{0:T(1024)}, u32[]{:S(2)}) copy-start(s32[4096]{0:T(1024)} %seg_ref.5) | copy-start | bytes 49156
  9.6 22.7 %copy-start.1 = (bf16[2,256,256]{2,1,0:T(8,128)(2,1)S(1)}, bf16[2,256,256]{2,1,0:T(8,128)(2,1)}, u32[]{:S(2)}) copy-start(bf16[2,256,256]{2,1,0:T(8,128)(2,1)} %get-tuple-element.41.refs_1_) | copy-start | bytes 786436
  9.6 21.9 %collective-permute-start.12 = (bf16[2,256,256]{2,1,0:T(8,128)(2,1)}, bf16[2,256,256]{2,1,0:T(8,128)(2,1)S(1)}, u32[]{:S(2)}, u32[]{:S(2)}) collective-permute-start(bf16[2,256,256]{2,1,0:T(8,128)(2,1)} %get-tuple-element.35), channel_id=1, source_target_pairs={{0,4},{1,5},{2,6},{3,7},{4,0},{5,1},{6,2},{7,3},{8,12},{9,13},{10,... | collective-permute-start | bytes 786440 | tf_op jit(solution)/shard_map/across_2_0/ppermute | solution.py:315
  10.9 15.3 %collective-permute-start.4 = (bf16[2,256,256]{2,1,0:T(8,128)(2,1)}, bf16[2,256,256]{2,1,0:T(8,128)(2,1)S(1)}, u32[]{:S(2)}, u32[]{:S(2)}) collective-permute-start(bf16[2,256,256]{2,1,0:T(8,128)(2,1)} %get-tuple-element.35), channel_id=1, source_target_pairs={{0,12},{1,13},{2,14},{3,15},{4,8},{5,9},{6,10},{7,11},{8,20},{9,21... | collective-permute-start | bytes 786440 | tf_op jit(solution)/shard_map/up_2/ppermute | solution.py:319
  18.0 26.5 %collective-permute-start.10 = (bf16[2,256,256]{2,1,0:T(8,128)(2,1)S(1)}, bf16[2,256,256]{2,1,0:T(8,128)(2,1)S(1)}, u32[]{:S(2)}, u32[]{:S(2)}) collective-permute-start(bf16[2,256,256]{2,1,0:T(8,128)(2,1)S(1)} %collective-permute-done.9.refs_3_), channel_id=1, source_target_pairs={{0,8},{1,9},{2,10},{3,11},{4,12},{5,13},{6,14},{7,15},{8,16},{9,17... | collective-permute-start | bytes 786440 | tf_op jit(solution)/shard_map/up_0/ppermute | solution.py:319
  19.3 0.8 copy-start.5
  20.1 1.0 copy-start.4
  23.7 8.6 %copy-start = (bf16[2,256,512]{2,1,0:T(8,128)(2,1)S(1)}, bf16[2,256,512]{2,1,0:T(8,128)(2,1)}, u32[]{:S(2)}) copy-start(bf16[2,256,512]{2,1,0:T(8,128)(2,1)} %get-tuple-element.39.refs_0_) | copy-start | bytes 1572868
  23.7 14.7 %collective-permute-start.8 = (bf16[2,256,512]{2,1,0:T(8,128)(2,1)}, bf16[2,256,512]{2,1,0:T(8,128)(2,1)S(1)}, u32[]{:S(2)}, u32[]{:S(2)}) collective-permute-start(bf16[2,256,512]{2,1,0:T(8,128)(2,1)} %get-tuple-element.40), channel_id=1, source_target_pairs={{0,4},{1,5},{2,6},{3,7},{4,0},{5,1},{6,2},{7,3},{8,12},{9,13},{10,... | collective-permute-start | bytes 1572872 | tf_op jit(solution)/shard_map/across_2_0/ppermute | solution.py:315
  26.2 18.3 %collective-permute-start.11 = (bf16[2,256,256]{2,1,0:T(8,128)(2,1)S(1)}, bf16[2,256,256]{2,1,0:T(8,128)(2,1)}, u32[]{:S(2)}, u32[]{:S(2)}) collective-permute-start(bf16[2,256,256]{2,1,0:T(8,128)(2,1)S(1)} %collective-permute-done.4.refs_4_), channel_id=1, source_target_pairs={{0,8},{1,9},{2,10},{3,11},{4,12},{5,13},{6,14},{7,15},{8,16},{9,17... | collective-permute-start | bytes 786440 | tf_op jit(solution)/shard_map/up_0/ppermute | solution.py:319
  27.5 52.8 %collective-permute-start.6 = (bf16[4096,128]{1,0:T(8,128)(2,1)S(1)}, bf16[4096,128]{1,0:T(8,128)(2,1)S(1)}, u32[]{:S(2)}, u32[]{:S(2)}) collective-permute-start(bf16[4096,128]{1,0:T(8,128)(2,1)S(1)} %pad_maximum_fusion.refs_0_), channel_id=1, source_target_pairs={{0,16},{1,17},{2,18},{3,19},{4,20},{5,21},{6,22},{7,23},{8,24},{9,... | collective-permute-start | bytes 3145736 | tf_op jit(solution)/shard_map/between_2/ppermute | solution.py:323
  31.5 52.1 %collective-permute-start.5 = (bf16[4096,128]{1,0:T(8,128)(2,1)S(1)}, bf16[4096,128]{1,0:T(8,128)(2,1)S(1)}, u32[]{:S(2)}, u32[]{:S(2)}) collective-permute-start(bf16[4096,128]{1,0:T(8,128)(2,1)S(1)} %pad_maximum_fusion.refs_0_), channel_id=1, source_target_pairs={{0,8},{1,9},{2,10},{3,11},{4,12},{5,13},{6,14},{7,15},{8,0},{9,1},... | collective-permute-start | bytes 3145736 | tf_op jit(solution)/shard_map/between_1/ppermute | solution.py:323
  47.5 36.1 %collective-permute-start.18 = (bf16[4,256,512]{2,1,0:T(8,128)(2,1)S(1)}, bf16[4,256,512]{2,1,0:T(8,128)(2,1)S(1)}, u32[]{:S(2)}, u32[]{:S(2)}) collective-permute-start(bf16[4,256,512]{2,1,0:T(8,128)(2,1)S(1)} %attention.5.refs_4_), channel_id=1, source_target_pairs={{0,5},{1,4},{2,7},{3,6},{4,1},{5,0},{6,3},{7,2},{8,13},{9,12},{10,... | collective-permute-start | bytes 3145736 | tf_op jit(solution)/shard_map/across_2_1/ppermute | solution.py:315
  48.1 47.1 %collective-permute-start.16 = (bf16[4,256,512]{2,1,0:T(8,128)(2,1)S(1)}, bf16[4,256,512]{2,1,0:T(8,128)(2,1)S(1)}, u32[]{:S(2)}, u32[]{:S(2)}) collective-permute-start(bf16[4,256,512]{2,1,0:T(8,128)(2,1)S(1)} %attention.5.refs_4_), channel_id=1, source_target_pairs={{0,1},{1,0},{2,3},{3,2},{4,5},{5,4},{6,7},{7,6},{8,9},{9,8},{10,11... | collective-permute-start | bytes 3145736 | tf_op jit(solution)/shard_map/across_0_1/ppermute | solution.py:315
  49.0 47.2 %collective-permute-start.14 = (bf16[4,256,512]{2,1,0:T(8,128)(2,1)S(1)}, bf16[4,256,512]{2,1,0:T(8,128)(2,1)S(1)}, u32[]{:S(2)}, u32[]{:S(2)}) collective-permute-start(bf16[4,256,512]{2,1,0:T(8,128)(2,1)S(1)} %attention.5.refs_4_), channel_id=1, source_target_pairs={{0,4},{1,5},{2,6},{3,7},{4,0},{5,1},{6,2},{7,3},{8,12},{9,13},{10,... | collective-permute-start | bytes 3145736 | tf_op jit(solution)/shard_map/across_2_0/ppermute | solution.py:315
  80.3 15.8 %collective-permute-start.13 = (bf16[4,256,512]{2,1,0:T(8,128)(2,1)S(1)}, bf16[4,256,512]{2,1,0:T(8,128)(2,1)S(1)}, u32[]{:S(2)}, u32[]{:S(2)}) collective-permute-start(bf16[4,256,512]{2,1,0:T(8,128)(2,1)S(1)} %attention.5.refs_4_), channel_id=1, source_target_pairs={{0,2},{1,3},{2,0},{3,1},{4,6},{5,7},{6,4},{7,5},{8,10},{9,11},{10,... | collective-permute-start | bytes 3145736 | tf_op jit(solution)/shard_map/across_1_0/ppermute | solution.py:315
  83.6 24.8 %collective-permute-start.7 = (bf16[4096,128]{1,0:T(8,128)(2,1)S(1)}, bf16[4096,128]{1,0:T(8,128)(2,1)S(1)}, u32[]{:S(2)}, u32[]{:S(2)}) collective-permute-start(bf16[4096,128]{1,0:T(8,128)(2,1)S(1)} %collective-permute-done.6.refs_2_), channel_id=1, source_target_pairs={{0,8},{1,9},{2,10},{3,11},{4,12},{5,13},{6,14},{7,15},{8,0},{9,1},... | collective-permute-start | bytes 3145736 | tf_op jit(solution)/shard_map/between_1/ppermute | solution.py:323
  83.6 24.8 %collective-permute-start.19 = (bf16[4,256,512]{2,1,0:T(8,128)(2,1)S(1)}, bf16[4,256,512]{2,1,0:T(8,128)(2,1)S(1)}, u32[]{:S(2)}, u32[]{:S(2)}) collective-permute-start(bf16[4,256,512]{2,1,0:T(8,128)(2,1)S(1)} %collective-permute-done.18.refs_10_), channel_id=1, source_target_pairs={{0,2},{1,3},{2,0},{3,1},{4,6},{5,7},{6,4},{7,5},{8,10},{9,11},{10,... | collective-permute-start | bytes 3145736 | tf_op jit(solution)/shard_map/across_1_0/ppermute | solution.py:315
  95.2 13.1 %collective-permute-start.17 = (bf16[4,256,512]{2,1,0:T(8,128)(2,1)S(1)}, bf16[4,256,512]{2,1,0:T(8,128)(2,1)S(1)}, u32[]{:S(2)}, u32[]{:S(2)}) collective-permute-start(bf16[4,256,512]{2,1,0:T(8,128)(2,1)S(1)} %collective-permute-done.16.refs_8_), channel_id=1, source_target_pairs={{0,2},{1,3},{2,0},{3,1},{4,6},{5,7},{6,4},{7,5},{8,10},{9,11},{10,... | collective-permute-start | bytes 3145736 | tf_op jit(solution)/shard_map/across_1_0/ppermute | solution.py:315
  96.1 12.2 %collective-permute-start.15 = (bf16[4,256,512]{2,1,0:T(8,128)(2,1)S(1)}, bf16[4,256,512]{2,1,0:T(8,128)(2,1)S(1)}, u32[]{:S(2)}, u32[]{:S(2)}) collective-permute-start(bf16[4,256,512]{2,1,0:T(8,128)(2,1)S(1)} %collective-permute-done.14.refs_6_), channel_id=1, source_target_pairs={{0,2},{1,3},{2,0},{3,1},{4,6},{5,7},{6,4},{7,5},{8,10},{9,11},{10,... | collective-permute-start | bytes 3145736 | tf_op jit(solution)/shard_map/across_1_0/ppermute | solution.py:315
  112.9 0.7 copy-start.3
  113.5 6.9 %collective-permute-start.20 = (bf16[256,256]{1,0:T(8,128)(2,1)S(1)}, bf16[256,256]{1,0:T(8,128)(2,1)S(1)}, u32[]{:S(2)}, u32[]{:S(2)}) collective-permute-start(bf16[256,256]{1,0:T(8,128)(2,1)S(1)} %get-tuple-element.47), channel_id=1, source_target_pairs={{0,7},{1,6},{2,5},{3,4},{4,3},{5,2},{6,1},{7,0},{8,15},{9,14},{10,... | collective-permute-start | bytes 393224 | tf_op jit(solution)/shard_map/across_3_1/ppermute | solution.py:315
  114.7 8.5 %collective-permute-start.21 = (bf16[256,256]{1,0:T(8,128)(2,1)S(1)}, bf16[256,256]{1,0:T(8,128)(2,1)S(1)}, u32[]{:S(2)}, u32[]{:S(2)}) collective-permute-start(bf16[256,256]{1,0:T(8,128)(2,1)S(1)} %get-tuple-element.48), channel_id=1, source_target_pairs={{0,5},{1,4},{2,7},{3,6},{4,1},{5,0},{6,3},{7,2},{8,13},{9,12},{10,... | collective-permute-start | bytes 393224 | tf_op jit(solution)/shard_map/across_2_1/ppermute | solution.py:315
  116.6 8.9 %collective-permute-start.22 = (bf16[256,256]{1,0:T(8,128)(2,1)S(1)}, bf16[256,256]{1,0:T(8,128)(2,1)S(1)}, u32[]{:S(2)}, u32[]{:S(2)}) collective-permute-start(bf16[256,256]{1,0:T(8,128)(2,1)S(1)} %get-tuple-element.49), channel_id=1, source_target_pairs={{0,6},{1,7},{2,4},{3,5},{4,2},{5,3},{6,0},{7,1},{8,14},{9,15},{10,... | collective-permute-start | bytes 393224 | tf_op jit(solution)/shard_map/across_3_0/ppermute | solution.py:315
  116.7 11.7 %collective-permute-start.23 = (bf16[256,256]{1,0:T(8,128)(2,1)S(1)}, bf16[256,256]{1,0:T(8,128)(2,1)S(1)}, u32[]{:S(2)}, u32[]{:S(2)}) collective-permute-start(bf16[256,256]{1,0:T(8,128)(2,1)S(1)} %get-tuple-element.50), channel_id=1, source_target_pairs={{0,4},{1,5},{2,6},{3,7},{4,0},{5,1},{6,2},{7,3},{8,12},{9,13},{10,... | collective-permute-start | bytes 393224 | tf_op jit(solution)/shard_map/across_2_0/ppermute | solution.py:315
  117.9 10.5 %collective-permute-start.24 = (bf16[256,256]{1,0:T(8,128)(2,1)S(1)}, bf16[256,256]{1,0:T(8,128)(2,1)S(1)}, u32[]{:S(2)}, u32[]{:S(2)}) collective-permute-start(bf16[256,256]{1,0:T(8,128)(2,1)S(1)} %get-tuple-element.51), channel_id=1, source_target_pairs={{0,3},{1,2},{2,1},{3,0},{4,7},{5,6},{6,5},{7,4},{8,11},{9,10},{10,... | collective-permute-start | bytes 393224 | tf_op jit(solution)/shard_map/across_1_1/ppermute | solution.py:315
  120.4 8.5 %copy-start.8 = (bf16[256,256]{1,0:T(8,128)(2,1)}, bf16[256,256]{1,0:T(8,128)(2,1)S(1)}, u32[]{:S(2)}) copy-start(bf16[256,256]{1,0:T(8,128)(2,1)S(1)} %collective-permute-done.20.refs_0_) | copy-start | bytes 393220
  120.4 8.5 %collective-permute-start.25 = (bf16[256,256]{1,0:T(8,128)(2,1)S(1)}, bf16[256,256]{1,0:T(8,128)(2,1)S(1)}, u32[]{:S(2)}, u32[]{:S(2)}) collective-permute-start(bf16[256,256]{1,0:T(8,128)(2,1)S(1)} %get-tuple-element.52), channel_id=1, source_target_pairs={{0,1},{1,0},{2,3},{3,2},{4,5},{5,4},{6,7},{7,6},{8,9},{9,8},{10,11... | collective-permute-start | bytes 393224 | tf_op jit(solution)/shard_map/across_0_1/ppermute | solution.py:315
  123.3 5.7 %copy-start.9 = (bf16[256,256]{1,0:T(8,128)(2,1)}, bf16[256,256]{1,0:T(8,128)(2,1)S(1)}, u32[]{:S(2)}) copy-start(bf16[256,256]{1,0:T(8,128)(2,1)S(1)} %collective-permute-done.21.refs_1_) | copy-start | bytes 393220
  123.3 5.7 %collective-permute-start.26 = (bf16[256,256]{1,0:T(8,128)(2,1)S(1)}, bf16[256,256]{1,0:T(8,128)(2,1)S(1)}, u32[]{:S(2)}, u32[]{:S(2)}) collective-permute-start(bf16[256,256]{1,0:T(8,128)(2,1)S(1)} %get-tuple-element.53), channel_id=1, source_target_pairs={{0,2},{1,3},{2,0},{3,1},{4,6},{5,7},{6,4},{7,5},{8,10},{9,11},{10,... | collective-permute-start | bytes 393224 | tf_op jit(solution)/shard_map/across_1_0/ppermute | solution.py:315
  125.5 3.5 %copy-start.10 = (bf16[256,256]{1,0:T(8,128)(2,1)}, bf16[256,256]{1,0:T(8,128)(2,1)S(1)}, u32[]{:S(2)}) copy-start(bf16[256,256]{1,0:T(8,128)(2,1)S(1)} %collective-permute-done.22.refs_2_) | copy-start | bytes 393220
  128.4 0.7 copy-start.11
  128.4 0.7 copy-start.12
  128.9 0.7 copy-start.13
  128.9 0.7 copy-start.14

commit v6 on v5

--- a/solution.py
+++ b/solution.py
@@ -349,6 +349,7 @@
         out_shape=[bf16(2, n, 2 * HEAD)] * (group // 2),
         in_specs=[VMEM] * 4,
         out_specs=[VMEM] * (group // 2),
+        compiler_params=params(60),
         name="split_kv",
     )(keys, values, across(keys, 1, 0), across(values, 1, 0))
     links = [[kv[0]] + [across(kv[o], 2 * o, 0) for o in range(1, group // 2)]]
@@ -360,6 +361,7 @@
         out_shape=[bf16(2, n, width)] * (group // 2),
         in_specs=[VMEM] * 2,
         out_specs=[VMEM] * (group // 2),
+        compiler_params=params(60),
         name="split_q",
     )(queries, far_queries)
     q = [q[0]] + [across(q[o], 2 * o, 0) for o in range(1, group // 2)]

time: 133 us -> 132 us (level)
    ppermute x3, waiting for transfers between devices: 42.3 us -> 44.4 us  [between(): return lax.ppermute(array, AXES, pairs(lambda z, g, y: (z ^ i, g, y)))]
    unnamed x30 -> x32, local copies, waits for them, and re-layouts: 4.38 us -> 4.42 us
  transfers between devices with their start and end apart: 27 -> 27, of which waited for: 10 -> 10; matrix products, arithmetic and copies ran while one was open for 1% -> 1% of each run, Pallas kernels for 17% -> 16%
where the time goes in v6:
time: 132 us
  waiting for transfers between devices  69.7 us (53%)
  starting transfers between devices  28.5 us (22%)
  Pallas kernels  28.2 us (21%)
  local copies, waits for them, and re-layouts  4.43 us (3%)
    ppermute x3, waiting for transfers between devices, between(): return lax.ppermute(array, AXES, pairs(lambda z, g, y: (z ^ i, g, y)))  44.4 us
    ppermute x20, waiting for transfers between devices, across(): return lax.ppermute(array, AXES, pairs(lambda z, g, y: (z, g ^ j, y ^ m)))  19.4 us
    ppermute x20, starting transfers between devices, across(): return lax.ppermute(array, AXES, pairs(lambda z, g, y: (z, g ^ j, y ^ m)))  18.5 us
    pallas_call x3, Pallas kernels, attention(): pl.pallas_call(functools.partial(attention_kernel, group, heads, back, pa...  14 us
    ppermute x4, waiting for transfers between devices, up(): return lax.ppermute(array, AXES, pairs(lambda z, g, y: (z + 1, g ^ j, y)))  5.84 us
    ppermute x4, starting transfers between devices, up(): return lax.ppermute(array, AXES, pairs(lambda z, g, y: (z + 1, g ^ j, y)))  5.13 us
    ppermute x3, starting transfers between devices, between(): return lax.ppermute(array, AXES, pairs(lambda z, g, y: (z ^ i, g, y)))  4.8 us
    pallas_call x1, Pallas kernels, shards(): pl.pallas_call(functools.partial(project_kernel, group, attn, planes), ou...  4.49 us
  transfers between devices with their start and end apart: 27, of which 10 were waited for; matrix products, arithmetic and copies ran while one was open for 1% of the time, Pallas kernels for 16%

profile of v6, /device:TPU:25, one launch (start us, length us, event | category | flops | bytes accessed | tf_op | source)
XLA Modules:
  0.0 132.1 jit_solution(15570998087276920775)
XLA Ops:
  0.0 0.7 collective-permute-start
  0.7 0.0 collective-permute-start.3
  0.7 2.4 %split_w.1 = (bf16[2048,128]{1,0:T(8,128)(2,1)}, bf16[2048,128]{1,0:T(8,128)(2,1)}) custom-call(bf16[2048,256]{1,0:T(8,128)(2,1)} %w_ref.1), custom_call_target="tpu_custom_call" | custom-call | tf_op jit(solution)/shard_map/split_w/pallas_call | solution.py:331
  3.1 0.5 collective-permute-start.2
  3.6 1.2 collective-permute-start.1
  4.8 0.0 collective-permute-done.3.refs_3_
  4.8 0.1 collective-permute-done.2.refs_2_
  4.9 0.6 copy-done.7
  5.5 0.7 copy-done.8
  6.2 2.1 %split_kv.1 = (bf16[2,256,256]{2,1,0:T(8,128)(2,1)}, bf16[2,256,256]{2,1,0:T(8,128)(2,1)}) custom-call(bf16[256,512]{1,0:T(8,128)(2,1)} %refs_0_, bf16[256,512]{1,0:T(8,128)(2,1)} %refs_1_.1, bf16[256,512]{1,0:T(8,128)(2,1)} %copy-done.8, bf16[256,512]{1,0:T(8,128)(2,1)} %copy-done.7), custom_call_target="tpu_custom_call" | custom-call | tf_op jit(solution)/shard_map/split_kv/pallas_call | solution.py:347
  8.3 1.3 collective-permute-start.9
  9.6 0.0 copy-start.2
  9.6 1.3 collective-permute-start.12
  10.9 1.3 collective-permute-start.4
  12.2 5.8 %collective-permute-done.9.refs_3_ = bf16[2,256,256]{2,1,0:T(8,128)(2,1)S(1)} collective-permute-done((bf16[2,256,256]{2,1,0:T(8,128)(2,1)}, bf16[2,256,256]{2,1,0:T(8,128)(2,1)S(1)}, u32[]{:S(2)}, u32[]{:S(2)}) %collective-permute-start.9) | collective-permute-done | bytes 262176 | tf_op jit(solution)/shard_map/up_0/ppermute | solution.py:319
  18.0 1.3 collective-permute-start.10
  19.3 0.0 collective-permute-done.refs_1_
  19.4 0.8 copy-done.6
  20.2 1.0 copy-done.4
  21.1 2.6 %split_q.1 = (bf16[2,256,512]{2,1,0:T(8,128)(2,1)}, bf16[2,256,512]{2,1,0:T(8,128)(2,1)}) custom-call(bf16[256,2048]{1,0:T(8,128)(2,1)} %refs_0_.1, bf16[256,2048]{1,0:T(8,128)(2,1)} %copy-done.4), custom_call_target="tpu_custom_call" | custom-call | tf_op jit(solution)/shard_map/split_q/pallas_call | solution.py:359
  23.7 1.2 collective-permute-start.8
  24.9 1.1 pad_maximum_fusion.refs_0_
  26.1 0.0 collective-permute-done.4.refs_4_
  26.1 1.3 collective-permute-start.11
  27.4 3.9 %collective-permute-start.6 = (bf16[4096,128]{1,0:T(8,128)(2,1)S(1)}, bf16[4096,128]{1,0:T(8,128)(2,1)S(1)}, u32[]{:S(2)}, u32[]{:S(2)}) collective-permute-start(bf16[4096,128]{1,0:T(8,128)(2,1)S(1)} %pad_maximum_fusion.refs_0_), channel_id=1, source_target_pairs={{0,16},{1,17},{2,18},{3,19},{4,20},{5,21},{6,22},{7,23},{8,24},{9,... | collective-permute-start | bytes 3145736 | tf_op jit(solution)/shard_map/between_2/ppermute | solution.py:323
  31.3 0.9 collective-permute-start.5
  32.2 6.1 %attention.3 = (f32[2,1024,128]{2,1,0:T(8,128)S(1)}, f32[2,1024,256]{2,1,0:T(8,128)S(1)}) custom-call(s32[4096]{0:T(1024)S(1)} %copy-done.2, s32[16,256]{1,0:T(8,128)S(1)} %reshape.2.segrow_ref, bf16[2,256,512]{2,1,0:T(8,128)(2,1)S(1)} %copy-done, bf16[2,256,256]{2,1,0:T(8,128)(2,1)S(1)} %copy-done.1, ...), custom_call_target="tpu_custom_call" | custom-call | tf_op jit(solution)/shard_map/attention/pallas_call | solution.py:218
  38.3 0.0 collective-permute-done.8.refs_0_.refs_1_
  38.3 5.0 %attention.4 = (f32[2,1024,128]{2,1,0:T(8,128)S(1)}, f32[2,1024,256]{2,1,0:T(8,128)S(1)}) custom-call(s32[4096]{0:T(1024)S(1)} %copy-done.2, s32[16,256]{1,0:T(8,128)S(1)} %reshape.2.segrow_ref, bf16[2,256,512]{2,1,0:T(8,128)(2,1)S(1)} %collective-permute-done.8.refs_0_.refs_1_, bf16[2,256,256]{2,1,0:T(8,128)(2,1)S(1)} %copy-done.1, ...), custom_call_target="tpu_custom_call" | custom-call | tf_op jit(solution)/shard_map/attention/pallas_call | solution.py:218
  43.4 0.0 collective-permute-done.11.refs_3_
  43.4 2.9 %attention.5.refs_4_ = bf16[4,256,512]{2,1,0:T(8,128)(2,1)S(1)} custom-call(s32[4096]{0:T(1024)S(1)} %copy-done.2, s32[16,256]{1,0:T(8,128)S(1)} %reshape.2.segrow_ref, bf16[2,256,512]{2,1,0:T(8,128)(2,1)S(1)} %copy-done, bf16[2,256,512]{2,1,0:T(8,128)(2,1)S(1)} %collective-permute-done.8.refs_0_.refs_1_, ...), custom_call_target="tpu_custom_call" | custom-call | tf_op jit(solution)/shard_map/attention/pallas_call | solution.py:218
  46.3 0.6 collective-permute-start.18
  46.9 0.9 collective-permute-start.16
  47.8 1.2 collective-permute-start.14
  49.0 31.1 %collective-permute-done.6.refs_2_ = bf16[4096,128]{1,0:T(8,128)(2,1)S(1)} collective-permute-done((bf16[4096,128]{1,0:T(8,128)(2,1)S(1)}, bf16[4096,128]{1,0:T(8,128)(2,1)S(1)}, u32[]{:S(2)}, u32[]{:S(2)}) %collective-permute-start.6) | collective-permute-done | bytes 1048608 | tf_op jit(solution)/shard_map/between_2/ppermute | solution.py:323
  80.2 3.3 %collective-permute-start.13 = (bf16[4,256,512]{2,1,0:T(8,128)(2,1)S(1)}, bf16[4,256,512]{2,1,0:T(8,128)(2,1)S(1)}, u32[]{:S(2)}, u32[]{:S(2)}) collective-permute-start(bf16[4,256,512]{2,1,0:T(8,128)(2,1)S(1)} %attention.5.refs_4_), channel_id=1, source_target_pairs={{0,2},{1,3},{2,0},{3,1},{4,6},{5,7},{6,4},{7,5},{8,10},{9,11},{10,... | collective-permute-start | bytes 3145736 | tf_op jit(solution)/shard_map/across_1_0/ppermute | solution.py:315
  83.4 0.0 collective-permute-done.5.refs_1_
  83.4 0.1 collective-permute-start.19
  83.5 10.5 %collective-permute-done.16.refs_8_ = bf16[4,256,512]{2,1,0:T(8,128)(2,1)S(1)} collective-permute-done((bf16[4,256,512]{2,1,0:T(8,128)(2,1)S(1)}, bf16[4,256,512]{2,1,0:T(8,128)(2,1)S(1)}, u32[]{:S(2)}, u32[]{:S(2)}) %collective-permute-start.16) | collective-permute-done | bytes 1048608 | tf_op jit(solution)/shard_map/across_0_1/ppermute | solution.py:315
  94.0 0.9 collective-permute-start.17
  95.0 0.0 collective-permute-done.14.refs_6_
  95.0 0.0 collective-permute-start.15
  95.0 0.0 collective-permute-done.13.refs_5_
  95.0 13.3 %collective-permute-done.7.refs_3_ = bf16[4096,128]{1,0:T(8,128)(2,1)S(1)} collective-permute-done((bf16[4096,128]{1,0:T(8,128)(2,1)S(1)}, bf16[4096,128]{1,0:T(8,128)(2,1)S(1)}, u32[]{:S(2)}, u32[]{:S(2)}) %collective-permute-start.7) | collective-permute-done | bytes 1048608 | tf_op jit(solution)/shard_map/between_1/ppermute | solution.py:323
  108.2 0.0 collective-permute-done.19.refs_11_
  108.2 4.5 %project.1 = (bf16[256,256]{1,0:T(8,128)(2,1)S(1)}, bf16[256,256]{1,0:T(8,128)(2,1)S(1)}, bf16[256,256]{1,0:T(8,128)(2,1)S(1)}, bf16[256,256]{1,0:T(8,128)(2,1)S...) custom-call(bf16[4096,128]{1,0:T(8,128)(2,1)S(1)} %pad_maximum_fusio, ...), custom_call_target="tpu_custom_call" | custom-call | tf_op jit(solution)/shard_map/project/pallas_call | solution.py:396
  112.7 0.6 copy-done.3
  113.4 1.2 collective-permute-start.20
  114.6 1.8 %collective-permute-start.21 = (bf16[256,256]{1,0:T(8,128)(2,1)S(1)}, bf16[256,256]{1,0:T(8,128)(2,1)S(1)}, u32[]{:S(2)}, u32[]{:S(2)}) collective-permute-start(bf16[256,256]{1,0:T(8,128)(2,1)S(1)} %get-tuple-element.48), channel_id=1, source_target_pairs={{0,5},{1,4},{2,7},{3,6},{4,1},{5,0},{6,3},{7,2},{8,13},{9,12},{10,... | collective-permute-start | bytes 393224 | tf_op jit(solution)/shard_map/across_2_1/ppermute | solution.py:315
  116.4 0.1 collective-permute-start.22
  116.6 1.2 collective-permute-start.23
  117.8 1.2 collective-permute-start.24
  119.0 1.3 collective-permute-done.20.refs_0_
  120.3 0.6 collective-permute-start.25
  120.9 2.3 %collective-permute-done.21.refs_1_ = bf16[256,256]{1,0:T(8,128)(2,1)S(1)} collective-permute-done((bf16[256,256]{1,0:T(8,128)(2,1)S(1)}, bf16[256,256]{1,0:T(8,128)(2,1)S(1)}, u32[]{:S(2)}, u32[]{:S(2)}) %collective-permute-start.21) | collective-permute-done | bytes 131104 | tf_op jit(solution)/shard_map/across_2_1/ppermute | solution.py:315
  123.1 0.5 collective-permute-start.26
  123.6 1.7 %collective-permute-done.22.refs_2_ = bf16[256,256]{1,0:T(8,128)(2,1)S(1)} collective-permute-done((bf16[256,256]{1,0:T(8,128)(2,1)S(1)}, bf16[256,256]{1,0:T(8,128)(2,1)S(1)}, u32[]{:S(2)}, u32[]{:S(2)}) %collective-permute-start.22) | collective-permute-done | bytes 131104 | tf_op jit(solution)/shard_map/across_3_0/ppermute | solution.py:315
  125.3 2.9 %collective-permute-done.23.refs_3_ = bf16[256,256]{1,0:T(8,128)(2,1)S(1)} collective-permute-done((bf16[256,256]{1,0:T(8,128)(2,1)S(1)}, bf16[256,256]{1,0:T(8,128)(2,1)S(1)}, u32[]{:S(2)}, u32[]{:S(2)}) %collective-permute-start.23) | collective-permute-done | bytes 131104 | tf_op jit(solution)/shard_map/across_2_0/ppermute | solution.py:315
  128.3 0.6 collective-permute-done.25.refs_5_
  128.8 0.1 copy-done.12
  128.9 0.1 copy-done.13
  129.0 0.5 copy-done.14
  129.5 0.0 copy-done.15
  129.5 2.6 %place.1 = bf16[256,2048]{1,0:T(8,128)(2,1)} custom-call(bf16[256,256]{1,0:T(8,128)(2,1)} %copy-done.9, bf16[256,256]{1,0:T(8,128)(2,1)} %copy-done.10, bf16[256,256]{1,0:T(8,128)(2,1)} %copy-done.11, bf16[256,256]{1,0:T(8,128)(2,1)} %copy-done.12, bf16[256,256]{1,0:T(8,128)(2,1)} %copy-done.13, bf16[256,256]{1,0:T(8,128)(2,1)} %copy-done.14, ...), custom_call_target="tpu_custom_call" | custom-call | tf_op jit(solution)/shard_map/place/pallas_call | solution.py:411
  (32 shorter events, 0.1 us)
Async XLA Ops:
  0.0 19.3 %collective-permute-start = (bf16[256,2048]{1,0:T(8,128)(2,1)}, bf16[256,2048]{1,0:T(8,128)(2,1)S(1)}, u32[]{:S(2)}, u32[]{:S(2)}) collective-permute-start(bf16[256,2048]{1,0:T(8,128)(2,1)} %refs_0_.1), channel_id=1, source_target_pairs={{0,2},{1,3},{2,0},{3,1},{4,6},{5,7},{6,4},{7,5},{8,10},{9,11},{10,... | collective-permute-start | bytes 3145736 | tf_op jit(solution)/shard_map/across_1_0/ppermute | solution.py:315
  0.7 4.1 %collective-permute-start.3 = (bf16[256,512]{1,0:T(8,128)(2,1)}, bf16[256,512]{1,0:T(8,128)(2,1)S(1)}, u32[]{:S(2)}, u32[]{:S(2)}) collective-permute-start(bf16[256,512]{1,0:T(8,128)(2,1)} %refs_1_.1), channel_id=1, source_target_pairs={{0,2},{1,3},{2,0},{3,1},{4,6},{5,7},{6,4},{7,5},{8,10},{9,11},{10,... | collective-permute-start | bytes 786440 | tf_op jit(solution)/shard_map/across_1_0/ppermute | solution.py:315
  3.1 21.9 %copy-start.5 = (bf16[2048,128]{1,0:T(8,128)(2,1)S(1)}, bf16[2048,128]{1,0:T(8,128)(2,1)}, u32[]{:S(2)}) copy-start(bf16[2048,128]{1,0:T(8,128)(2,1)} %get-tuple-element.32) | copy-start | bytes 1572868
  3.1 1.9 %collective-permute-start.2 = (bf16[256,512]{1,0:T(8,128)(2,1)}, bf16[256,512]{1,0:T(8,128)(2,1)S(1)}, u32[]{:S(2)}, u32[]{:S(2)}) collective-permute-start(bf16[256,512]{1,0:T(8,128)(2,1)} %refs_0_), channel_id=1, source_target_pairs={{0,2},{1,3},{2,0},{3,1},{4,6},{5,7},{6,4},{7,5},{8,10},{9,11},{10,... | collective-permute-start | bytes 786440 | tf_op jit(solution)/shard_map/across_1_0/ppermute | solution.py:315
  3.6 15.8 %collective-permute-start.1 = (bf16[2048,128]{1,0:T(8,128)(2,1)}, bf16[2048,128]{1,0:T(8,128)(2,1)S(1)}, u32[]{:S(2)}, u32[]{:S(2)}) collective-permute-start(bf16[2048,128]{1,0:T(8,128)(2,1)} %get-tuple-element.31), channel_id=1, source_target_pairs={{0,1},{1,0},{2,3},{3,2},{4,5},{5,4},{6,7},{7,6},{8,9},{9,8},{10,11... | collective-permute-start | bytes 1572872 | tf_op jit(solution)/shard_map/across_0_1/ppermute | solution.py:315
  4.8 0.7 copy-start.7
  5.5 0.7 copy-start.8
  8.3 9.7 %collective-permute-start.9 = (bf16[2,256,256]{2,1,0:T(8,128)(2,1)}, bf16[2,256,256]{2,1,0:T(8,128)(2,1)S(1)}, u32[]{:S(2)}, u32[]{:S(2)}) collective-permute-start(bf16[2,256,256]{2,1,0:T(8,128)(2,1)} %get-tuple-element.41.refs_1_), channel_id=1, source_target_pairs={{0,8},{1,9},{2,10},{3,11},{4,12},{5,13},{6,14},{7,15},{8,16},{9,17... | collective-permute-start | bytes 786440 | tf_op jit(solution)/shard_map/up_0/ppermute | solution.py:319
  9.6 17.8 %copy-start.2 = (s32[4096]{0:T(1024)S(1)}, s32[4096]{0:T(1024)}, u32[]{:S(2)}) copy-start(s32[4096]{0:T(1024)} %seg_ref.5) | copy-start | bytes 49156
  9.6 22.6 %copy-start.1 = (bf16[2,256,256]{2,1,0:T(8,128)(2,1)S(1)}, bf16[2,256,256]{2,1,0:T(8,128)(2,1)}, u32[]{:S(2)}) copy-start(bf16[2,256,256]{2,1,0:T(8,128)(2,1)} %get-tuple-element.41.refs_1_) | copy-start | bytes 786436
  9.6 21.7 %collective-permute-start.12 = (bf16[2,256,256]{2,1,0:T(8,128)(2,1)}, bf16[2,256,256]{2,1,0:T(8,128)(2,1)S(1)}, u32[]{:S(2)}, u32[]{:S(2)}) collective-permute-start(bf16[2,256,256]{2,1,0:T(8,128)(2,1)} %get-tuple-element.35), channel_id=1, source_target_pairs={{0,4},{1,5},{2,6},{3,7},{4,0},{5,1},{6,2},{7,3},{8,12},{9,13},{10,... | collective-permute-start | bytes 786440 | tf_op jit(solution)/shard_map/across_2_0/ppermute | solution.py:315
  10.9 15.2 %collective-permute-start.4 = (bf16[2,256,256]{2,1,0:T(8,128)(2,1)}, bf16[2,256,256]{2,1,0:T(8,128)(2,1)S(1)}, u32[]{:S(2)}, u32[]{:S(2)}) collective-permute-start(bf16[2,256,256]{2,1,0:T(8,128)(2,1)} %get-tuple-element.35), channel_id=1, source_target_pairs={{0,12},{1,13},{2,14},{3,15},{4,8},{5,9},{6,10},{7,11},{8,20},{9,21... | collective-permute-start | bytes 786440 | tf_op jit(solution)/shard_map/up_2/ppermute | solution.py:319
  18.0 25.3 %collective-permute-start.10 = (bf16[2,256,256]{2,1,0:T(8,128)(2,1)S(1)}, bf16[2,256,256]{2,1,0:T(8,128)(2,1)S(1)}, u32[]{:S(2)}, u32[]{:S(2)}) collective-permute-start(bf16[2,256,256]{2,1,0:T(8,128)(2,1)S(1)} %collective-permute-done.9.refs_3_), channel_id=1, source_target_pairs={{0,8},{1,9},{2,10},{3,11},{4,12},{5,13},{6,14},{7,15},{8,16},{9,17... | collective-permute-start | bytes 786440 | tf_op jit(solution)/shard_map/up_0/ppermute | solution.py:319
  19.3 0.8 copy-start.6
  20.2 1.0 copy-start.4
  23.7 8.5 %copy-start = (bf16[2,256,512]{2,1,0:T(8,128)(2,1)S(1)}, bf16[2,256,512]{2,1,0:T(8,128)(2,1)}, u32[]{:S(2)}) copy-start(bf16[2,256,512]{2,1,0:T(8,128)(2,1)} %get-tuple-element.39.refs_0_) | copy-start | bytes 1572868
  23.7 14.6 %collective-permute-start.8 = (bf16[2,256,512]{2,1,0:T(8,128)(2,1)}, bf16[2,256,512]{2,1,0:T(8,128)(2,1)S(1)}, u32[]{:S(2)}, u32[]{:S(2)}) collective-permute-start(bf16[2,256,512]{2,1,0:T(8,128)(2,1)} %get-tuple-element.40), channel_id=1, source_target_pairs={{0,4},{1,5},{2,6},{3,7},{4,0},{5,1},{6,2},{7,3},{8,12},{9,13},{10,... | collective-permute-start | bytes 1572872 | tf_op jit(solution)/shard_map/across_2_0/ppermute | solution.py:315
  26.1 17.3 %collective-permute-start.11 = (bf16[2,256,256]{2,1,0:T(8,128)(2,1)S(1)}, bf16[2,256,256]{2,1,0:T(8,128)(2,1)}, u32[]{:S(2)}, u32[]{:S(2)}) collective-permute-start(bf16[2,256,256]{2,1,0:T(8,128)(2,1)S(1)} %collective-permute-done.4.refs_4_), channel_id=1, source_target_pairs={{0,8},{1,9},{2,10},{3,11},{4,12},{5,13},{6,14},{7,15},{8,16},{9,17... | collective-permute-start | bytes 786440 | tf_op jit(solution)/shard_map/up_0/ppermute | solution.py:319
  27.4 52.8 %collective-permute-start.6 = (bf16[4096,128]{1,0:T(8,128)(2,1)S(1)}, bf16[4096,128]{1,0:T(8,128)(2,1)S(1)}, u32[]{:S(2)}, u32[]{:S(2)}) collective-permute-start(bf16[4096,128]{1,0:T(8,128)(2,1)S(1)} %pad_maximum_fusion.refs_0_), channel_id=1, source_target_pairs={{0,16},{1,17},{2,18},{3,19},{4,20},{5,21},{6,22},{7,23},{8,24},{9,... | collective-permute-start | bytes 3145736 | tf_op jit(solution)/shard_map/between_2/ppermute | solution.py:323
  31.3 52.1 %collective-permute-start.5 = (bf16[4096,128]{1,0:T(8,128)(2,1)S(1)}, bf16[4096,128]{1,0:T(8,128)(2,1)S(1)}, u32[]{:S(2)}, u32[]{:S(2)}) collective-permute-start(bf16[4096,128]{1,0:T(8,128)(2,1)S(1)} %pad_maximum_fusion.refs_0_), channel_id=1, source_target_pairs={{0,8},{1,9},{2,10},{3,11},{4,12},{5,13},{6,14},{7,15},{8,0},{9,1},... | collective-permute-start | bytes 3145736 | tf_op jit(solution)/shard_map/between_1/ppermute | solution.py:323
  46.3 37.1 %collective-permute-start.18 = (bf16[4,256,512]{2,1,0:T(8,128)(2,1)S(1)}, bf16[4,256,512]{2,1,0:T(8,128)(2,1)S(1)}, u32[]{:S(2)}, u32[]{:S(2)}) collective-permute-start(bf16[4,256,512]{2,1,0:T(8,128)(2,1)S(1)} %attention.5.refs_4_), channel_id=1, source_target_pairs={{0,5},{1,4},{2,7},{3,6},{4,1},{5,0},{6,3},{7,2},{8,13},{9,12},{10,... | collective-permute-start | bytes 3145736 | tf_op jit(solution)/shard_map/across_2_1/ppermute | solution.py:315
  46.9 47.1 %collective-permute-start.16 = (bf16[4,256,512]{2,1,0:T(8,128)(2,1)S(1)}, bf16[4,256,512]{2,1,0:T(8,128)(2,1)S(1)}, u32[]{:S(2)}, u32[]{:S(2)}) collective-permute-start(bf16[4,256,512]{2,1,0:T(8,128)(2,1)S(1)} %attention.5.refs_4_), channel_id=1, source_target_pairs={{0,1},{1,0},{2,3},{3,2},{4,5},{5,4},{6,7},{7,6},{8,9},{9,8},{10,11... | collective-permute-start | bytes 3145736 | tf_op jit(solution)/shard_map/across_0_1/ppermute | solution.py:315
  47.8 47.2 %collective-permute-start.14 = (bf16[4,256,512]{2,1,0:T(8,128)(2,1)S(1)}, bf16[4,256,512]{2,1,0:T(8,128)(2,1)S(1)}, u32[]{:S(2)}, u32[]{:S(2)}) collective-permute-start(bf16[4,256,512]{2,1,0:T(8,128)(2,1)S(1)} %attention.5.refs_4_), channel_id=1, source_target_pairs={{0,4},{1,5},{2,6},{3,7},{4,0},{5,1},{6,2},{7,3},{8,12},{9,13},{10,... | collective-permute-start | bytes 3145736 | tf_op jit(solution)/shard_map/across_2_0/ppermute | solution.py:315
  80.2 14.8 %collective-permute-start.13 = (bf16[4,256,512]{2,1,0:T(8,128)(2,1)S(1)}, bf16[4,256,512]{2,1,0:T(8,128)(2,1)S(1)}, u32[]{:S(2)}, u32[]{:S(2)}) collective-permute-start(bf16[4,256,512]{2,1,0:T(8,128)(2,1)S(1)} %attention.5.refs_4_), channel_id=1, source_target_pairs={{0,2},{1,3},{2,0},{3,1},{4,6},{5,7},{6,4},{7,5},{8,10},{9,11},{10,... | collective-permute-start | bytes 3145736 | tf_op jit(solution)/shard_map/across_1_0/ppermute | solution.py:315
  83.4 24.8 %collective-permute-start.7 = (bf16[4096,128]{1,0:T(8,128)(2,1)S(1)}, bf16[4096,128]{1,0:T(8,128)(2,1)S(1)}, u32[]{:S(2)}, u32[]{:S(2)}) collective-permute-start(bf16[4096,128]{1,0:T(8,128)(2,1)S(1)} %collective-permute-done.6.refs_2_), channel_id=1, source_target_pairs={{0,8},{1,9},{2,10},{3,11},{4,12},{5,13},{6,14},{7,15},{8,0},{9,1},... | collective-permute-start | bytes 3145736 | tf_op jit(solution)/shard_map/between_1/ppermute | solution.py:323
  83.4 24.8 %collective-permute-start.19 = (bf16[4,256,512]{2,1,0:T(8,128)(2,1)S(1)}, bf16[4,256,512]{2,1,0:T(8,128)(2,1)S(1)}, u32[]{:S(2)}, u32[]{:S(2)}) collective-permute-start(bf16[4,256,512]{2,1,0:T(8,128)(2,1)S(1)} %collective-permute-done.18.refs_10_), channel_id=1, source_target_pairs={{0,2},{1,3},{2,0},{3,1},{4,6},{5,7},{6,4},{7,5},{8,10},{9,11},{10,... | collective-permute-start | bytes 3145736 | tf_op jit(solution)/shard_map/across_1_0/ppermute | solution.py:315
  94.0 14.2 %collective-permute-start.17 = (bf16[4,256,512]{2,1,0:T(8,128)(2,1)S(1)}, bf16[4,256,512]{2,1,0:T(8,128)(2,1)S(1)}, u32[]{:S(2)}, u32[]{:S(2)}) collective-permute-start(bf16[4,256,512]{2,1,0:T(8,128)(2,1)S(1)} %collective-permute-done.16.refs_8_), channel_id=1, source_target_pairs={{0,2},{1,3},{2,0},{3,1},{4,6},{5,7},{6,4},{7,5},{8,10},{9,11},{10,... | collective-permute-start | bytes 3145736 | tf_op jit(solution)/shard_map/across_1_0/ppermute | solution.py:315
  95.0 13.3 %collective-permute-start.15 = (bf16[4,256,512]{2,1,0:T(8,128)(2,1)S(1)}, bf16[4,256,512]{2,1,0:T(8,128)(2,1)S(1)}, u32[]{:S(2)}, u32[]{:S(2)}) collective-permute-start(bf16[4,256,512]{2,1,0:T(8,128)(2,1)S(1)} %collective-permute-done.14.refs_6_), channel_id=1, source_target_pairs={{0,2},{1,3},{2,0},{3,1},{4,6},{5,7},{6,4},{7,5},{8,10},{9,11},{10,... | collective-permute-start | bytes 3145736 | tf_op jit(solution)/shard_map/across_1_0/ppermute | solution.py:315
  112.7 0.7 copy-start.3
  113.4 6.9 %collective-permute-start.20 = (bf16[256,256]{1,0:T(8,128)(2,1)S(1)}, bf16[256,256]{1,0:T(8,128)(2,1)S(1)}, u32[]{:S(2)}, u32[]{:S(2)}) collective-permute-start(bf16[256,256]{1,0:T(8,128)(2,1)S(1)} %get-tuple-element.47), channel_id=1, source_target_pairs={{0,7},{1,6},{2,5},{3,4},{4,3},{5,2},{6,1},{7,0},{8,15},{9,14},{10,... | collective-permute-start | bytes 393224 | tf_op jit(solution)/shard_map/across_3_1/ppermute | solution.py:315
  114.6 8.5 %collective-permute-start.21 = (bf16[256,256]{1,0:T(8,128)(2,1)S(1)}, bf16[256,256]{1,0:T(8,128)(2,1)S(1)}, u32[]{:S(2)}, u32[]{:S(2)}) collective-permute-start(bf16[256,256]{1,0:T(8,128)(2,1)S(1)} %get-tuple-element.48), channel_id=1, source_target_pairs={{0,5},{1,4},{2,7},{3,6},{4,1},{5,0},{6,3},{7,2},{8,13},{9,12},{10,... | collective-permute-start | bytes 393224 | tf_op jit(solution)/shard_map/across_2_1/ppermute | solution.py:315
  116.4 8.9 %collective-permute-start.22 = (bf16[256,256]{1,0:T(8,128)(2,1)S(1)}, bf16[256,256]{1,0:T(8,128)(2,1)S(1)}, u32[]{:S(2)}, u32[]{:S(2)}) collective-permute-start(bf16[256,256]{1,0:T(8,128)(2,1)S(1)} %get-tuple-element.49), channel_id=1, source_target_pairs={{0,6},{1,7},{2,4},{3,5},{4,2},{5,3},{6,0},{7,1},{8,14},{9,15},{10,... | collective-permute-start | bytes 393224 | tf_op jit(solution)/shard_map/across_3_0/ppermute | solution.py:315
  116.6 11.7 %collective-permute-start.23 = (bf16[256,256]{1,0:T(8,128)(2,1)S(1)}, bf16[256,256]{1,0:T(8,128)(2,1)S(1)}, u32[]{:S(2)}, u32[]{:S(2)}) collective-permute-start(bf16[256,256]{1,0:T(8,128)(2,1)S(1)} %get-tuple-element.50), channel_id=1, source_target_pairs={{0,4},{1,5},{2,6},{3,7},{4,0},{5,1},{6,2},{7,3},{8,12},{9,13},{10,... | collective-permute-start | bytes 393224 | tf_op jit(solution)/shard_map/across_2_0/ppermute | solution.py:315
  117.8 10.5 %collective-permute-start.24 = (bf16[256,256]{1,0:T(8,128)(2,1)S(1)}, bf16[256,256]{1,0:T(8,128)(2,1)S(1)}, u32[]{:S(2)}, u32[]{:S(2)}) collective-permute-start(bf16[256,256]{1,0:T(8,128)(2,1)S(1)} %get-tuple-element.51), channel_id=1, source_target_pairs={{0,3},{1,2},{2,1},{3,0},{4,7},{5,6},{6,5},{7,4},{8,11},{9,10},{10,... | collective-permute-start | bytes 393224 | tf_op jit(solution)/shard_map/across_1_1/ppermute | solution.py:315
  120.3 8.5 %copy-start.9 = (bf16[256,256]{1,0:T(8,128)(2,1)}, bf16[256,256]{1,0:T(8,128)(2,1)S(1)}, u32[]{:S(2)}) copy-start(bf16[256,256]{1,0:T(8,128)(2,1)S(1)} %collective-permute-done.20.refs_0_) | copy-start | bytes 393220
  120.3 8.5 %collective-permute-start.25 = (bf16[256,256]{1,0:T(8,128)(2,1)S(1)}, bf16[256,256]{1,0:T(8,128)(2,1)S(1)}, u32[]{:S(2)}, u32[]{:S(2)}) collective-permute-start(bf16[256,256]{1,0:T(8,128)(2,1)S(1)} %get-tuple-element.52), channel_id=1, source_target_pairs={{0,1},{1,0},{2,3},{3,2},{4,5},{5,4},{6,7},{7,6},{8,9},{9,8},{10,11... | collective-permute-start | bytes 393224 | tf_op jit(solution)/shard_map/across_0_1/ppermute | solution.py:315
  123.1 5.7 %copy-start.10 = (bf16[256,256]{1,0:T(8,128)(2,1)}, bf16[256,256]{1,0:T(8,128)(2,1)S(1)}, u32[]{:S(2)}) copy-start(bf16[256,256]{1,0:T(8,128)(2,1)S(1)} %collective-permute-done.21.refs_1_) | copy-start | bytes 393220
  123.1 5.7 %collective-permute-start.26 = (bf16[256,256]{1,0:T(8,128)(2,1)S(1)}, bf16[256,256]{1,0:T(8,128)(2,1)S(1)}, u32[]{:S(2)}, u32[]{:S(2)}) collective-permute-start(bf16[256,256]{1,0:T(8,128)(2,1)S(1)} %get-tuple-element.53), channel_id=1, source_target_pairs={{0,2},{1,3},{2,0},{3,1},{4,6},{5,7},{6,4},{7,5},{8,10},{9,11},{10,... | collective-permute-start | bytes 393224 | tf_op jit(solution)/shard_map/across_1_0/ppermute | solution.py:315
  125.3 3.5 %copy-start.11 = (bf16[256,256]{1,0:T(8,128)(2,1)}, bf16[256,256]{1,0:T(8,128)(2,1)S(1)}, u32[]{:S(2)}) copy-start(bf16[256,256]{1,0:T(8,128)(2,1)S(1)} %collective-permute-done.22.refs_2_) | copy-start | bytes 393220
  128.2 0.7 copy-start.12
  128.3 0.7 copy-start.13
  128.8 0.7 copy-start.14
  128.8 0.7 copy-start.15
